TPU v7x, 256 devices: a whole 4x4x8 slice. The times are simulated.
256 devices in a mesh: row: 128 (over x, y, z), col: 2 (over core).
Axes of the slice: x: 4, y: 4, z: 8, core: 2. Of those that a mesh axis runs over, the one named last changes fastest.
Arguments:
- inv_diag: float32 [128, 1088, 1088], P('row', None, 'col'), may hold values from -0.1875 to 0.1875
- low_left: float32 [128, 1088, 96], P('row', 'col'), may hold values from -0.1875 to 0.1875
- low_right: float32 [128, 1088, 96], P('row', 'col'), may hold values from -0.625 to 0.625
- deriv_diag: bfloat16 [3, 128, 1088, 1088], P(None, 'row', None, 'col'), may hold values from -0.1875 to 0.1875
- deriv_left: float32 [3, 128, 1088, 96], P(None, 'row', 'col'), may hold values from -0.1875 to 0.1875
- deriv_right: float32 [3, 128, 1088, 96], P(None, 'row', 'col'), may hold values from -0.625 to 0.625
- ranks: int32 [4, 128], P(None, 'row'), may hold values from 88 to 96
- whitened: float32 [139264], P(('row', 'col')), may hold values from -6 to 6
- probes: int32 [8, 139264], P(None, ('row', 'col')), may hold values from -1 to 1, as said below
Outputs:
- solved: float32 [9, 139264], P(None, ('row', 'col'))
- whitened_deriv: float32 [3, 8, 139264], P(None, None, ('row', 'col'))
- fisher: float32 [3, 3], replicated
- score: float32 [3], replicated
Inputs may be any that keep to these rules, and one draw needn't show every extreme that they name: `probes`: every entry is -1 or +1. `ranks`: column 0 belongs to no tile.
All inputs are finite; a program needn't handle non-finite values.
Results may differ from a plain program's by a relative error of at most 0.0019.
Values sent between devices are 32-bit elements; how exact they have to be, the bound alone decides.
No kernel may reach another device: no remote copies, remote signals or barrier semaphores. Data moves between devices by JAX's collectives and lax.ppermute only.
A program may use at most 64 MiB of HBM per device.

v0:
```python
import functools

import jax
import jax.numpy as jnp
from jax import lax
from jax.sharding import Mesh
from jax.sharding import PartitionSpec as P

ROW = ("row_0", "row_1", "row_2")
ROW_COL = ("row_0", "row_1", "row_2", "col")


highest = lax.Precision.HIGHEST


def from_behind(block, axis, distance):
    devices = range(lax.axis_size(axis))
    route = [(i - distance, i) for i in devices if i - distance in devices]
    return lax.ppermute(block, axis, route)


def rows_first(arrays, axis, dims):
    turned = [jnp.moveaxis(a, dim, 0) for a, dim in zip(arrays, dims)]
    both = jnp.concatenate([t.reshape(len(t), -1) for t in turned], axis=1)
    result, at, done = (lax.all_gather(both, axis, axis=0, tiled=True), 0, [])
    for t, dim in zip(turned, dims):
        piece = result[:, at : at + t[0].size].reshape(-1, *t.shape[1:])
        done.append(jnp.moveaxis(piece, 0, dim))
        at += t[0].size
    return tuple(done)


def from_everyone(x, axis):
    count = lax.axis_size(axis)
    return lax.all_to_all(jnp.broadcast_to(x[None], (count, *x.shape)), axis, 0, 0, tiled=True)


def taken_together(x, axis):
    everything = from_everyone(x, axis)
    return jnp.sum(everything, axis=0)


def in_one(arrays, axis):
    flat, at, done = (jnp.concatenate([a.reshape(-1) for a in arrays]), 0, [])
    so_far = taken_together(flat, axis)
    for a in arrays:
        done.append(so_far[at : at + a.size].reshape(a.shape))
        at += a.size
    return tuple(done)


def filled_with(x, identity):
    return jax.tree.map(
        lambda part, zero: jnp.zeros_like(part) + jnp.asarray(zero, part.dtype), x, identity
    )


def collected_together(x, axis):
    leaves = jax.tree.leaves(x)
    order = sorted(range(len(leaves)), key=lambda k: -leaves[k].size)
    width = (1, *leaves[order[0]].shape)[-1]
    lines = [
        jnp.pad(leaves[k].reshape(-1), (0, -leaves[k].size % width)).reshape(-1, width)
        for k in order
    ]
    both, at, found = (lax.all_gather(jnp.concatenate(lines), axis), 0, {})
    for k, line in zip(order, lines):
        piece = both[:, at : at + len(line)].reshape(len(both), -1)
        found[k] = piece[:, : leaves[k].size].reshape(-1, *leaves[k].shape)
        at += len(line)
    numbers = iter(range(len(leaves)))
    return jax.tree.map(lambda _: found[next(numbers)], x)


def carried_in(x, axes, combine, identity):
    before = start = filled_with(x, identity)
    so_far = x
    for axis in reversed(axes):
        count, mine = (lax.axis_size(axis), lax.axis_index(axis))
        pieces = collected_together(so_far, axis)
        inside, so_far = (start, start)
        for k in reversed(range(count)):
            passed = k > mine
            so_far = combine(so_far, jax.tree.map(lambda part: part[k], pieces))
            inside = jax.tree.map(lambda new, old: jnp.where(passed, new, old), so_far, inside)
        before = combine(inside, before)
    return before


def in_blocks(x, dim, count):
    before, after = (x.shape[:dim], x.shape[dim + 1 :])
    return jnp.moveaxis(x.reshape(*before, count, -1, *after), dim, 0)


def summed_on_arrival(x, axis, dim):
    count = lax.axis_size(axis)
    pieces = lax.all_to_all(in_blocks(x, dim, count), axis, 0, 0, tiled=True)
    return jnp.sum(pieces, axis=0)


def collected_alike(x, axis):
    leaves, found = (jax.tree.leaves(x), {})
    for first, a in enumerate(leaves):
        if first not in found:
            alike = [k for k, b in enumerate(leaves) if b.dtype == a.dtype]
            got = (
                collected_together([leaves[k] for k in alike], axis)
                if len(alike) > 1
                else [lax.all_gather(a, axis)]
            )
            for k, b in zip(alike, got):
                found[k] = b
    numbers = iter(range(len(leaves)))
    return jax.tree.map(lambda _: found[next(numbers)], x)


def entering(x, axes, combine, identity):
    before = start = filled_with(x, identity)
    so_far = x
    for axis in reversed(axes):
        count, mine = (lax.axis_size(axis), lax.axis_index(axis))
        pieces = collected_alike(so_far, axis)
        inside, so_far = (start, start)
        for k in range(count):
            passed = k < mine
            so_far = combine(so_far, jax.tree.map(lambda part: part[k], pieces))
            inside = jax.tree.map(lambda new, old: jnp.where(passed, new, old), so_far, inside)
        before = combine(inside, before)
    return before


def one_axis_at_a_time(x, axes):
    return functools.reduce(lax.psum, axes, x)


def compose_affine(earlier, later):
    offset = later[0] + jnp.dot(earlier[0], later[1], precision=highest)
    linear = jnp.dot(earlier[1], later[1], precision=highest)
    return (offset, linear)


def body(
    inv_diag, low_left, low_right, deriv_diag, deriv_left, deriv_right, ranks, whitened, probes
):
    inverse = inv_diag[0]
    size, half = inverse.shape
    own_left = low_left[0]
    rmax = own_left.shape[1]
    count = probes.shape[0]
    params = deriv_left.shape[0]
    columns = jnp.arange(rmax, dtype=jnp.int32)
    masks = (columns[None, :] < ranks[:, 0][:, None]).astype(jnp.float32)
    own_right = low_right[0] * masks[0][None, :]
    d_left = deriv_left[:, 0]
    d_right = deriv_right[:, 0] * masks[1:][:, None, :]
    source = jnp.concatenate([whitened[None, :], probes.astype(jnp.float32)], axis=0)
    identity_rank = jnp.eye(rmax, dtype=jnp.float32)
    next_left, next_right = from_behind((own_left, own_right), ROW, -1)
    source_full, right_full = rows_first((source, next_right), "col", (1, 0))
    wide = jnp.dot(inverse.T, right_full, precision=highest)
    base = jnp.dot(source_full, inverse, precision=highest)
    coupling, lift = in_one(
        (jnp.dot(own_left.T, wide, precision=highest), jnp.dot(base, own_left, precision=highest)),
        "col",
    )
    prefix = carried_in(
        (lift, -coupling.T), ROW, compose_affine, (jnp.zeros_like(lift), identity_rank)
    )
    coeff = prefix[0]
    solution = base - jnp.dot(coeff, wide.T, precision=highest)
    rounded = solution.astype(jnp.bfloat16)
    dense_part = jnp.einsum(
        "ph,kbh->kpb", rounded, deriv_diag[:, 0], preferred_element_type=jnp.float32
    )
    dense = summed_on_arrival(dense_part, "col", 2)
    prior = from_behind(solution, ROW, 1)
    lower_part = jnp.einsum("ph,khr->kpr", prior, d_right, precision=highest)
    upper_part = jnp.einsum("ph,khr->kpr", solution, d_left, precision=highest)
    lower_coeff, upper_coeff = in_one((lower_part, upper_part), "col")
    lower = jnp.einsum("kpr,khr->kph", lower_coeff, d_left, precision=highest)
    upper_send = jnp.einsum("kpr,khr->kph", upper_coeff, d_right, precision=highest)
    upper = from_behind(upper_send, ROW, -1)
    applied = dense + lower + upper
    drive = applied[:, 1:].reshape(params * count, half)
    shared = taken_together(jnp.dot(drive, wide, precision=highest), "col")
    prefix = entering(
        (shared, -coupling), ROW, compose_affine, (jnp.zeros_like(shared), identity_rank)
    )
    rest = drive - jnp.dot(prefix[0], own_left.T, precision=highest)
    outcome = summed_on_arrival(jnp.dot(rest, inverse.T, precision=highest), "col", 1)
    result = outcome.reshape(params, count, half)
    trace_part = jnp.einsum("kph,ph->k", result, source[1:], precision=highest)
    fisher_part = jnp.einsum("kph,lph->kl", result, result, precision=highest)
    data_part = jnp.einsum("kh,h->k", applied[:, 0], solution[0], precision=highest)
    trace, fisher_sum, data = (
        one_axis_at_a_time(trace_part, ROW_COL),
        one_axis_at_a_time(fisher_part, ROW_COL),
        one_axis_at_a_time(data_part, ROW_COL),
    )
    total = lax.axis_size(ROW) * lax.axis_size("col") * half
    fisher = fisher_sum / (2.0 * count * total)
    score = (data - trace / count) / (2.0 * total)
    return (solution, result, fisher, score)


def solution(mesh):
    finer = Mesh(
        mesh.devices.reshape(4, 4, 8, mesh.shape["col"]), ("row_0", "row_1", "row_2", "col")
    )
    placed = (
        P(ROW, None, "col"),
        P(ROW, "col", None),
        P(ROW, "col", None),
        P(None, ROW, None, "col"),
        P(None, ROW, "col", None),
        P(None, ROW, "col", None),
        P(None, ROW),
        P(ROW_COL),
        P(None, ROW_COL),
    )
    return jax.shard_map(
        body,
        mesh=finer,
        in_specs=placed,
        out_specs=(P(None, ROW_COL), P(None, None, ROW_COL), P(), P()),
        check_vma=False,
    )
```

profile of v0, /device:TPU:1, one launch (start us, length us, event | category | flops | bytes accessed | tf_op | source)
XLA Modules:
  0.0 283.7 jit_solution(11324847728179047510)
XLA Ops:
  7.5 3.6 %copy.316 = f32[1,1088,544]{2,1,0:T(8,128)} copy(f32[1,1088,544]{1,2,0:T(8,128)} %param.9) | data formatting | bytes 4734976 | tf_op jit(solution)/shard_map/dot_general | solution.py:190
  13.6 5.0 %all_gather.39 = f32[1088,105]{1,0:T(8,128)S(1)} all-gather(f32[544,105]{1,0:T(8,128)S(1)} %pad_maximum_fusion), channel_id=1, replica_groups=mesh['row_0'=4,'row_1'=4,'row_2'=8,'col'=2] {'col'}, dimensions={0}, use_global_device_ids=true | all-gather | bytes 685440 | tf_op jit(solution)/shard_map/all_gather | solution.py:25
  18.6 2.9 %fusion.4 = f32[9,544]{1,0:T(8,128)S(1)} fusion(f32[1,1088,544]{1,2,0:T(8,128)S(1)} %copy-done.1, f32[1088,105]{1,0:T(8,128)S(1)} %all_gather.39), kind=kOutput, calls=%fused_computation.4 | convolution fusion | flops 63922176 | bytes 2844032 | tf_op jit(solution)/shard_map/dot_general | solution.py:161
  21.4 3.3 %fusion.2 = f32[96,544]{1,0:T(8,128)S(1)} fusion(f32[1,1088,544]{1,2,0:T(8,128)S(1)} %copy-done.1, f32[1088,105]{1,0:T(8,128)S(1)} %all_gather.39), kind=kOutput, calls=%fused_computation.2 | convolution fusion | flops 681836544 | bytes 3033344 | tf_op jit(solution)/shard_map/dot_general | solution.py:160
  26.7 3.8 %all_to_all.27 = f32[2,1,10080]{2,1,0:T(1,128)S(1)} all-to-all(f32[2,1,10080]{2,1,0:T(1,128)S(1)} %broadcast_in_dim.13), channel_id=1, replica_groups=mesh['row_0'=4,'row_1'=4,'row_2'=8,'col'=2] {'col'}, dimensions={0} | all-to-all | bytes 161280 | tf_op jit(solution)/shard_map/all_to_all | solution.py:35
  31.0 23.8 %all-gather.6 = f32[8,105,96]{1,2,0:T(8,128)S(1)} all-gather(f32[1,105,96]{1,2,0:T(8,128)S(1)} %maximum_bitcast_fusion.1), channel_id=2, replica_groups=mesh['row_0'=4,'row_1'=4,'row_2'=8,'col'=2] {'row_2'}, dimensions={0}, use_global_device_ids=true | all-gather | bytes 362880 | tf_op jit(solution)/shard_map/all_gather | solution.py:66
  59.4 11.5 %all-gather.7 = f32[4,105,96]{1,2,0:T(8,128)S(1)} all-gather(f32[1,105,96]{1,2,0:T(8,128)S(1)} %maximum_bitcast_fusion.2), channel_id=3, replica_groups=mesh['row_0'=4,'row_1'=4,'row_2'=8,'col'=2] {'row_1'}, dimensions={0}, use_global_device_ids=true | all-gather | bytes 201600 | tf_op jit(solution)/shard_map/all_gather | solution.py:66
  74.0 9.9 %all-gather.8 = f32[4,105,96]{1,2,0:T(8,128)S(1)} all-gather(f32[1,105,96]{1,2,0:T(8,128)S(1)} %maximum_bitcast_fusion.3), channel_id=4, replica_groups=mesh['row_0'=4,'row_1'=4,'row_2'=8,'col'=2] {'row_0'}, dimensions={0}, use_global_device_ids=true | all-gather | bytes 201600 | tf_op jit(solution)/shard_map/all_gather | solution.py:66
  85.6 3.2 %collective-permute-start.1 = (f32[9,544]{1,0:T(8,128)S(1)}, f32[9,544]{1,0:T(8,128)S(1)}, u32[]{:S(2)}, u32[]{:S(2)}) collective-permute-start(f32[9,544]{1,0:T(8,128)S(1)} %convolution_subtract_fusion.1), channel_id=1, source_target_pairs={{0,2},{2,4},{4,6},{6,8},{8,10},{10,12},{12,14},{14,16},{16,18},{18... | collective-permute-start | bytes 58760 | tf_op jit(solution)/shard_map/ppermute | solution.py:19
  91.0 16.1 %all_to_all.28 = f32[2,1,5184]{2,1,0:T(1,128)S(1)} all-to-all(f32[2,1,5184]{2,1,0:T(1,128)S(1)} %broadcast_in_dim.15), channel_id=1, replica_groups=mesh['row_0'=4,'row_1'=4,'row_2'=8,'col'=2] {'col'}, dimensions={0} | all-to-all | bytes 82944 | tf_op jit(solution)/shard_map/all_to_all | solution.py:35
  109.2 2.7 fusion.6
  112.2 3.9 %all_to_all.29 = f32[2,3,9,544]{3,1,2,0:T(4,128)S(1)} all-to-all(f32[2,3,9,544]{3,1,2,0:T(4,128)S(1)} %copy.285), channel_id=1, replica_groups=mesh['row_0'=4,'row_1'=4,'row_2'=8,'col'=2] {'col'}, dimensions={0} | all-to-all | bytes 235008 | tf_op jit(solution)/shard_map/all_to_all | solution.py:97
  117.3 3.7 %all_to_all.30 = f32[2,24,96]{2,1,0:T(8,128)S(1)} all-to-all(f32[2,24,96]{2,1,0:T(8,128)S(1)} %broadcast_in_dim.16), channel_id=1, replica_groups=mesh['row_0'=4,'row_1'=4,'row_2'=8,'col'=2] {'col'}, dimensions={0} | all-to-all | bytes 36864 | tf_op jit(solution)/shard_map/all_to_all | solution.py:35
  121.2 20.7 %all-gather.9 = f32[8,120,96]{1,2,0:T(8,128)S(1)} all-gather(f32[1,120,96]{1,2,0:T(8,128)S(1)} %copy.289), channel_id=5, replica_groups=mesh['row_0'=4,'row_1'=4,'row_2'=8,'col'=2] {'row_2'}, dimensions={0}, use_global_device_ids=true | all-gather | bytes 414720 | tf_op jit(solution)/shard_map/all_gather | solution.py:66
  162.9 1.6 convolution_add_fusion.11
  166.8 12.2 %all-gather.10 = f32[4,120,96]{1,2,0:T(8,128)S(1)} all-gather(f32[1,120,96]{1,2,0:T(8,128)S(1)} %maximum_bitcast_fusion.4), channel_id=6, replica_groups=mesh['row_0'=4,'row_1'=4,'row_2'=8,'col'=2] {'row_1'}, dimensions={0}, use_global_device_ids=true | all-gather | bytes 230400 | tf_op jit(solution)/shard_map/all_gather | solution.py:66
  197.5 1.6 fusion.53
  201.6 10.2 %all-gather.11 = f32[4,120,96]{1,2,0:T(8,128)S(1)} all-gather(f32[1,120,96]{1,2,0:T(8,128)S(1)} %maximum_bitcast_fusion.5), channel_id=7, replica_groups=mesh['row_0'=4,'row_1'=4,'row_2'=8,'col'=2] {'row_0'}, dimensions={0}, use_global_device_ids=true | all-gather | bytes 230400 | tf_op jit(solution)/shard_map/all_gather | solution.py:66
  224.2 2.6 convolution_bitcast_fusion
  226.8 15.6 %all_to_all.31 = f32[2,24,544]{2,1,0:T(8,128)S(1)} all-to-all(f32[2,24,544]{2,1,0:T(8,128)S(1)} %convolution_bitcast_fusion), channel_id=1, replica_groups=mesh['row_0'=4,'row_1'=4,'row_2'=8,'col'=2] {'col'}, dimensions={0} | all-to-all | bytes 208896 | tf_op jit(solution)/shard_map/all_to_all | solution.py:97
  244.3 8.6 %all-reduce.2 = (f32[3,3]{1,0:T(4,128)S(1)}, f32[3]{0:T(128)S(1)}, f32[3]{0:T(128)S(1)}) all-reduce(f32[3,3]{1,0:T(4,128)S(1)} %convolution_bitcast_fusion.4, f32[3]{0:T(128)S(1)} %convolution_bitcast_fusion.5, f32[3]{0:T(128)S(1)} %convolution_bitcast_fusion.6), channel_id=1, replica_groups=mesh['row_0'=4,'row_1'=4,'row_2'=8,'col'=2] {'row_0'}, use_global_device_ids=true, to_apply=%region_5.6 | all-reduce | flops 15 | bytes 120 | tf_op jit(solution)/shard_map/psum | solution.py:133
  252.8 6.0 %all-reduce.1 = (f32[3,3]{1,0:T(4,128)S(1)}, f32[3]{0:T(128)S(1)}, f32[3]{0:T(128)S(1)}) all-reduce(f32[3,3]{1,0:T(4,128)S(1)} %get-tuple-element.10, f32[3]{0:T(128)S(1)} %get-tuple-element.11, f32[3]{0:T(128)S(1)} %get-tuple-element.12), channel_id=1, replica_groups=mesh['row_0'=4,'row_1'=4,'row_2'=8,'col'=2] {'row_1'}, use_global_device_ids=true, to_apply=%region_6.7 | all-reduce | flops 15 | bytes 120 | tf_op jit(solution)/shard_map/psum | solution.py:133
  258.8 14.0 %all-reduce = (f32[3,3]{1,0:T(4,128)S(1)}, f32[3]{0:T(128)S(1)}, f32[3]{0:T(128)S(1)}) all-reduce(f32[3,3]{1,0:T(4,128)S(1)} %get-tuple-element.7, f32[3]{0:T(128)S(1)} %get-tuple-element.8, f32[3]{0:T(128)S(1)} %get-tuple-element.9), channel_id=1, replica_groups=mesh['row_0'=4,'row_1'=4,'row_2'=8,'col'=2] {'row_2'}, use_global_device_ids=true, to_apply=%region_7.8 | all-reduce | flops 15 | bytes 120 | tf_op jit(solution)/shard_map/psum | solution.py:133
  272.8 9.8 %all-reduce.3 = (f32[3,3]{1,0:T(4,128)S(1)}, f32[3]{0:T(128)S(1)}, f32[3]{0:T(128)S(1)}) all-reduce(f32[3,3]{1,0:T(4,128)S(1)} %get-tuple-element.4, f32[3]{0:T(128)S(1)} %get-tuple-element.5, f32[3]{0:T(128)S(1)} %get-tuple-element.6), channel_id=1, replica_groups=mesh['row_0'=4,'row_1'=4,'row_2'=8,'col'=2] {'col'}, use_global_device_ids=true, to_apply=%region_8.9 | all-reduce | flops 15 | bytes 120 | tf_op jit(solution)/shard_map/psum | solution.py:133
  (230 shorter events, 86.0 us)
Async XLA Ops:
  0.6 88.2 %copy-start = (f32[3,1,544,96]{2,3,1,0:T(8,128)S(1)}, f32[3,1,544,96]{2,3,1,0:T(8,128)}, u32[]{:S(2)}) copy-start(f32[3,1,544,96]{2,3,1,0:T(8,128)} %param.13) | copy-start | bytes 1880068
  3.3 9.1 %collective-permute-start = (f32[544,96]{1,0:T(8,128)}, f32[544,96]{1,0:T(8,128)}, u32[]{:S(2)}, u32[]{:S(2)}) collective-permute-start(f32[544,96]{1,0:T(8,128)} %bitcast_multiply_fusion.3), channel_id=1, source_target_pairs={{2,0},{4,2},{6,4},{8,6},{10,8},{12,10},{14,12},{16,14},{18,16},{20... | collective-permute-start | bytes 626696 | tf_op jit(solution)/shard_map/ppermute | solution.py:19
  7.5 11.1 %copy-start.1 = (f32[1,1088,544]{1,2,0:T(8,128)S(1)}, f32[1,1088,544]{1,2,0:T(8,128)}, u32[]{:S(2)}) copy-start(f32[1,1088,544]{1,2,0:T(8,128)} %param.9) | copy-start | bytes 7102468
  18.6 6.1 %copy-start.6 = (f32[1,544,96]{1,2,0:T(8,128)S(1)}, f32[1,544,96]{1,2,0:T(8,128)}, u32[]{:S(2)}) copy-start(f32[1,544,96]{1,2,0:T(8,128)} %param.10) | copy-start | bytes 626692
  59.1 30.7 %copy-start.5 = (f32[3,1,544,96]{2,3,1,0:T(8,128)S(1)}, f32[3,1,544,96]{2,3,1,0:T(8,128)}, u32[]{:S(2)}) copy-start(f32[3,1,544,96]{2,3,1,0:T(8,128)} %param.14) | copy-start | bytes 1880068
  85.6 26.3 %copy-start.9 = (f32[9,544]{1,0:T(8,128)}, f32[9,544]{1,0:T(8,128)S(1)}, u32[]{:S(2)}) copy-start(f32[9,544]{1,0:T(8,128)S(1)} %convolution_subtract_fusion.1) | copy-start | bytes 58756
  85.6 4.2 %collective-permute-start.1 = (f32[9,544]{1,0:T(8,128)S(1)}, f32[9,544]{1,0:T(8,128)S(1)}, u32[]{:S(2)}, u32[]{:S(2)}) collective-permute-start(f32[9,544]{1,0:T(8,128)S(1)} %convolution_subtract_fusion.1), channel_id=1, source_target_pairs={{0,2},{2,4},{4,6},{6,8},{8,10},{10,12},{12,14},{14,16},{16,18},{18... | collective-permute-start | bytes 58760 | tf_op jit(solution)/shard_map/ppermute | solution.py:19
  107.9 8.2 %collective-permute-start.2 = (f32[3,9,544]{2,1,0:T(8,128)S(1)}, f32[3,9,544]{2,1,0:T(8,128)S(1)}, u32[]{:S(2)}, u32[]{:S(2)}) collective-permute-start(f32[3,9,544]{2,1,0:T(8,128)S(1)} %fusion.15), channel_id=1, source_target_pairs={{2,0},{4,2},{6,4},{8,6},{10,8},{12,10},{14,12},{16,14},{18,16},{20... | collective-permute-start | bytes 176264 | tf_op jit(solution)/shard_map/ppermute | solution.py:19
  116.7 0.6 copy-start.8
  141.9 11.6 %copy-start.3 = (f32[8,120,96]{1,2,0:T(8,128)}, f32[8,120,96]{1,2,0:T(8,128)S(1)}, u32[]{:S(2)}) copy-start(f32[8,120,96]{1,2,0:T(8,128)S(1)} %all-gather.9) | copy-start | bytes 1105924
  142.1 0.6 copy-start.10
  142.9 0.6 copy-start.12
  143.8 0.6 copy-start.13
  145.5 0.6 copy-start.15
  146.3 0.6 copy-start.16
  147.2 0.6 copy-start.17
  148.0 5.5 %copy-start.20 = (f32[96,96]{0,1:T(8,128)}, f32[96,96]{0,1:T(8,128)S(1)}, u32[]{:S(2)}) copy-start(f32[96,96]{0,1:T(8,128)S(1)} %fusion.77) | copy-start | bytes 110596
  153.7 70.5 %copy-start.2 = (f32[1,1088,544]{2,1,0:T(8,128)S(1)}, f32[1,1088,544]{2,1,0:T(8,128)}, u32[]{:S(2)}) copy-start(f32[1,1088,544]{2,1,0:T(8,128)} %copy.316) | copy-start | bytes 7102468
  179.0 3.7 %copy-start.4 = (f32[4,120,96]{1,2,0:T(8,128)}, f32[4,120,96]{1,2,0:T(8,128)S(1)}, u32[]{:S(2)}) copy-start(f32[4,120,96]{1,2,0:T(8,128)S(1)} %all-gather.10) | copy-start | bytes 552964
  179.2 2.4 copy-start.11
  181.8 0.6 copy-start.18
  211.7 0.7 copy-start.7
  221.9 21.0 %copy-start.28 = (f32[8,544,1]{1,0,2:T(8,128)S(1)}, f32[8,544,1]{1,0,2:T(8,128)}, u32[]{:S(2)}) copy-start(f32[8,544,1]{1,0,2:T(8,128)} %get-tuple-element.50) | copy-start | bytes 52228
  242.5 41.2 %copy-start.21 = (f32[24,544]{1,0:T(8,128)}, f32[24,544]{1,0:T(8,128)S(1)}, u32[]{:S(2)}) copy-start(f32[24,544]{1,0:T(8,128)S(1)} %reduce_sum.49) | copy-start | bytes 156676
  (8 other events, 4.8 us)
where the time goes:
time: 286 us; the launch traced here: 284 us
  blocking collectives  175 us (61%)
  matrix products  51.8 us (18%)
  local copies, waits for them, and re-layouts  40.8 us (14%)
  other arithmetic  7.57 us (3%)
  starting transfers between devices  5.79 us (2%)
    all_gather x6, blocking collectives, collected_together(): both, at, found = (lax.all_gather(jnp.concatenate(lines), axis), 0, {})  88.3 us
    psum x4, blocking collectives, one_axis_at_a_time(): return functools.reduce(lax.psum, axes, x)  38.3 us
    unnamed x92, local copies, waits for them, and re-layouts  27 us
    all_to_all x3, blocking collectives, from_everyone(): lax.all_to_all(jnp.broadcast_to(x[None], (count, *x.shape)), axis, 0, 0,...  23.7 us
    dot_general x38, matrix products, compose_affine(): offset = later[0] + jnp.dot(earlier[0], later[1], precision=highest)  23.5 us
    all_to_all x2, blocking collectives, summed_on_arrival(): pieces = lax.all_to_all(in_blocks(x, dim, count), axis, 0, 0, tiled=True)  19.5 us
    dot_general x28, matrix products, compose_affine(): linear = jnp.dot(earlier[1], later[1], precision=highest)  8.66 us
    ppermute x3, starting transfers between devices, from_behind(): return lax.ppermute(block, axis, route)  5.79 us
  transfers between devices with their start and end apart: 3, of which 1 were waited for; matrix products, arithmetic and copies ran while one was open for 4% of the time, Pallas kernels for 0%

commit v1 on v0

v1 whole, which is shorter than its diff:
```python
import jax
import jax.numpy as jnp
from jax import lax
from jax.sharding import Mesh
from jax.sharding import PartitionSpec as P

ROW = ("row_0", "row_1", "row_2")
PLANE = ("row_0", "row_1")
LINE = "row_2"
ROW_COL = ("row_0", "row_1", "row_2", "col")

high = lax.Precision.HIGH
highest = lax.Precision.HIGHEST


def dot(a, b, precision=highest):
    return lax.dot_general(a, b, (((1,), (0,)), ((), ())), precision=precision, preferred_element_type=jnp.float32)


def dot_nt(a, b, precision=highest):
    return lax.dot_general(a, b, (((1,), (1,)), ((), ())), precision=precision, preferred_element_type=jnp.float32)


def dot_tn(a, b, precision=highest):
    return lax.dot_general(a, b, (((0,), (0,)), ((), ())), precision=precision, preferred_element_type=jnp.float32)


def along_rows(block, distance):
    devices = range(lax.axis_size(ROW))
    route = [(i, i + distance) for i in devices if i + distance in devices]
    return lax.ppermute(block, ROW, route)


def swapped(block):
    return lax.ppermute(block, "col", [(0, 1), (1, 0)])


def part(x, index, axis):
    size = x.shape[axis] // 2
    return lax.dynamic_slice_in_dim(x, index * size, size, axis)


def joined(mine, other, side, axis):
    first = jnp.where(side == 0, mine, other)
    second = jnp.where(side == 0, other, mine)
    return jnp.concatenate([first, second], axis)


def everywhere(x, axis):
    count = lax.axis_size(axis)
    return lax.all_to_all(jnp.broadcast_to(x[None], (count, *x.shape)), axis, 0, 0, tiled=True)


def body(
    inv_diag, low_left, low_right, deriv_diag, deriv_left, deriv_right, ranks, whitened, probes
):
    inverse = inv_diag[0]
    size, half = inverse.shape
    rmax = low_left.shape[2]
    count = probes.shape[0]
    params = deriv_left.shape[0]
    side = lax.axis_index("col")
    place = lax.axis_index(LINE)
    group = lax.axis_index(PLANE)
    in_line = lax.axis_size(LINE)
    groups = lax.axis_size(PLANE)
    right_next = along_rows(low_right[0], -1)
    columns = jnp.arange(rmax, dtype=jnp.int32)
    masks = (columns[None, :] < ranks[:, 0][:, None]).astype(jnp.float32)
    own_left = low_left[0] * masks[0][None, :]
    d_left = deriv_left[:, 0] * masks[1:][:, None, :]
    d_right = deriv_right[:, 0]
    source = jnp.concatenate([whitened[None, :], probes.astype(jnp.float32)], axis=0)
    source_other = swapped(source)
    source_full = joined(source, source_other, side, 1)
    moved = dot(inverse, own_left)
    moved = part(moved, side, 0) + swapped(part(moved, 1 - side, 0))
    lines = -(-(count + 1) // 16) * 16
    blank = jnp.zeros((lines - count - 1, rmax), jnp.float32)
    own_map = jnp.concatenate([-dot_tn(right_next, moved), dot(source, moved), blank], axis=0)
    own_map = part(own_map, side, 0) + swapped(part(own_map, 1 - side, 0))
    right_full = joined(right_next, swapped(right_next), side, 0)
    base = dot(source_full, inverse)
    wide = dot_tn(right_full, inverse)

    got = everywhere(own_map, LINE)
    maps = joined(got, swapped(got), side, 1)
    turns = maps[:, :rmax]
    lifts = maps[:, rmax:]
    reach = [None] * in_line
    reach[-1] = maps[-1]
    zero_top = jnp.zeros((rmax, rmax), jnp.float32)
    for k in reversed(range(in_line - 1)):
        reach[k] = dot(reach[k + 1], turns[k]) + jnp.concatenate([zero_top, lifts[k]], axis=0)
    total_map = reach[0]
    got = everywhere(part(total_map, side, 0), PLANE)
    totals = joined(got, swapped(got), side, 1)
    state = jnp.zeros((lines, rmax), jnp.float32)
    ahead = state
    for g in reversed(range(1, groups)):
        state = totals[g, rmax:] + dot(state, totals[g, :rmax])
        ahead = jnp.where(group == g - 1, state, ahead)
    coeff = ahead
    for k in range(1, in_line):
        through = reach[k][rmax:] + dot(ahead, reach[k][:rmax])
        coeff = jnp.where(place == k - 1, through, coeff)
    coeff = coeff[: count + 1]
    solution = base - dot(coeff, wide)

    rounded = solution.astype(jnp.bfloat16)
    prior = along_rows(solution, 1)
    upper_part = jnp.einsum("ph,khr->kpr", solution, d_left, precision=high)
    upper_coeff = upper_part + swapped(upper_part)
    upper_send = jnp.einsum("kpr,khr->kph", upper_coeff, d_right, precision=high)
    upper = along_rows(upper_send, -1)
    dense_part = jnp.einsum(
        "ph,kbh->kpb", rounded, deriv_diag[:, 0], preferred_element_type=jnp.float32
    )
    dense = part(dense_part, side, 2) + swapped(part(dense_part, 1 - side, 2))
    lower_part = jnp.einsum("ph,khr->kpr", prior, d_right, precision=high)
    lower_coeff = lower_part + swapped(lower_part)
    lower = jnp.einsum("kpr,khr->kph", lower_coeff, d_left, precision=high)
    applied = dense + lower + upper
    drive = applied[:, 1:].reshape(params * count, half)
    shared = dot_nt(drive, wide, high)
    shared = shared + swapped(shared)
    plain = dot_nt(drive, inverse, high)
    plain = part(plain, side, 1) + swapped(part(plain, 1 - side, 1))

    offsets = everywhere(shared, LINE)
    state = jnp.zeros_like(shared)
    local = state
    spread = jnp.eye(rmax, dtype=jnp.float32)
    own_spread = spread
    for k in range(in_line):
        state = offsets[k] + dot_nt(state, turns[k], high)
        if k < in_line - 1:
            spread = dot_nt(spread, turns[k], high) if k else turns[0].T
            local = jnp.where(place == k + 1, state, local)
            own_spread = jnp.where(place == k + 1, spread, own_spread)
    outs = everywhere(state, PLANE)
    state = jnp.zeros_like(shared)
    behind = state
    for g in range(groups - 1):
        state = outs[g] + dot_nt(state, totals[g, :rmax], high)
        behind = jnp.where(group == g + 1, state, behind)
    entry = local + dot(behind, own_spread, high)
    flat_result = plain - dot_nt(entry, moved, high)
    result = flat_result.reshape(params, count, half)

    trace_part = jnp.einsum("kph,ph->k", result, source[1:], precision=high)
    fisher_part = jnp.einsum("kph,lph->kl", result, result, precision=high)
    data_part = jnp.einsum("kh,h->k", applied[:, 0], solution[0], precision=high)
    sums = jnp.concatenate(
        [fisher_part.reshape(-1), trace_part, data_part, jnp.zeros((128 - params * (params + 2),))]
    )
    sums = sums + swapped(sums)
    sums = jnp.sum(everywhere(sums, ROW).reshape(-1, 128), axis=0)
    fisher_sum = sums[: params * params].reshape(params, params)
    trace = sums[params * params : params * (params + 1)]
    data = sums[params * (params + 1) : params * (params + 2)]
    total = lax.axis_size(ROW) * lax.axis_size("col") * half
    fisher = fisher_sum / (2.0 * count * total)
    score = (data - trace / count) / (2.0 * total)
    return (solution, result, fisher, score)


def solution(mesh):
    finer = Mesh(
        mesh.devices.reshape(4, 4, 8, mesh.shape["col"]), ("row_0", "row_1", "row_2", "col")
    )
    placed = (
        P(ROW, None, "col"),
        P(ROW, "col", None),
        P(ROW, "col", None),
        P(None, ROW, None, "col"),
        P(None, ROW, "col", None),
        P(None, ROW, "col", None),
        P(None, ROW),
        P(ROW_COL),
        P(None, ROW_COL),
    )
    return jax.shard_map(
        body,
        mesh=finer,
        in_specs=placed,
        out_specs=(P(None, ROW_COL), P(None, None, ROW_COL), P(), P()),
        check_vma=False,
    )
```

time: 286 us -> 178 us (0.62)
  blocking collectives: 175 us -> 16.1 us
  starting transfers between devices: 5.79 us -> 50.4 us
  waiting for transfers between devices: 1.39 us -> 28 us
  local copies, waits for them, and re-layouts: 40.8 us -> 20.7 us
    all_gather x7 -> x0, blocking collectives: 93.2 us -> none  [the longest x6 88.3 us: collected_together(): both, at, found = (lax.all_gather(jnp.concatenate(lines), axis), 0, {})]
    psum x4 -> x0, blocking collectives: 38.3 us -> none  [one_axis_at_a_time(): return functools.reduce(lax.psum, axes, x)]
    all_to_all x0 -> x4, starting transfers between devices: none -> 30.5 us  [everywhere(): lax.all_to_all(jnp.broadcast_to(x[None], (count, *x.shape)), axis, 0, 0,...]
    all_to_all x5 -> x1, blocking collectives: 43.2 us -> 16.1 us  [everywhere(): lax.all_to_all(jnp.broadcast_to(x[None], (count, *x.shape)), axis, 0, 0,...]
    unnamed x92 -> x158, local copies, waits for them, and re-layouts: 27 us -> 4.71 us
    all_to_all x0 -> x4, waiting for transfers between devices: none -> 21.4 us  [everywhere(): lax.all_to_all(jnp.broadcast_to(x[None], (count, *x.shape)), axis, 0, 0,...]
    ppermute x3 -> x15, starting transfers between devices: 5.79 us -> 19.8 us  [the longest x12 14.8 us: swapped(): return lax.ppermute(block, 'col', [(0, 1), (1, 0)])]
    dot_general x6 -> x0, local copies, waits for them, and re-layouts: 6.01 us -> none  [the longest x1 3.56 us: body(): jnp.dot(rest, inverse.T, precision=highest)]
  transfers between devices with their start and end apart: 3 -> 19, of which waited for: 1 -> 7; matrix products, arithmetic and copies ran while one was open for 4% -> 26% of each run, Pallas kernels for 0% -> 0%
where the time goes in v1:
time: 178 us; the launch traced here: 176 us
  matrix products  50.9 us (29%)
  starting transfers between devices  50.4 us (28%)
  waiting for transfers between devices  28 us (16%)
  local copies, waits for them, and re-layouts  20.7 us (12%)
  blocking collectives  16.1 us (9%)
  other arithmetic  7.65 us (4%)
  between operations  2.21 us (1%)
    all_to_all x4, starting transfers between devices, everywhere(): lax.all_to_all(jnp.broadcast_to(x[None], (count, *x.shape)), axis, 0, 0,...  30.5 us
    dot_general x32, matrix products, dot_nt(): lax.dot_general(a, b, (((1,), (1,)), ((), ())), precision=precision, pref...  30.2 us
    all_to_all x4, waiting for transfers between devices, everywhere(): lax.all_to_all(jnp.broadcast_to(x[None], (count, *x.shape)), axis, 0, 0,...  21.4 us
    all_to_all x1, blocking collectives, everywhere(): lax.all_to_all(jnp.broadcast_to(x[None], (count, *x.shape)), axis, 0, 0,...  16.1 us
    ppermute x12, starting transfers between devices, swapped(): return lax.ppermute(block, 'col', [(0, 1), (1, 0)])  14.8 us
    dot_general x34, matrix products, dot(): lax.dot_general(a, b, (((1,), (0,)), ((), ())), precision=precision, pref...  12.1 us
    ppermute x3, waiting for transfers between devices, along_rows(): return lax.ppermute(block, ROW, route)  5.26 us
    ppermute x3, starting transfers between devices, along_rows(): return lax.ppermute(block, ROW, route)  5.04 us
  transfers between devices with their start and end apart: 19, of which 7 were waited for; matrix products, arithmetic and copies ran while one was open for 26% of the time, Pallas kernels for 0%

profile of v1, /device:TPU:1, one launch (start us, length us, event | category | flops | bytes accessed | tf_op | source)
XLA Modules:
  0.0 176.0 jit_solution(10583363199473147803)
XLA Ops:
  0.7 1.4 collective-permute-start.2
  2.8 2.7 %fusion.6 = f32[96,1088]{1,0:T(8,128)S(1)} fusion(f32[1,1088,544]{1,2,0:T(8,128)S(1)} %copy-done, f32[1,544,96]{1,2,0:T(8,128)} %param.10, f32[96]{0:T(128)S(1)} %slice_bitcast_fusion.51), kind=kOutput, calls=%fused_computation.6 | convolution fusion | flops 681888768 | bytes 2994560 | tf_op jit(solution)/shard_map/dot_general | solution.py:17
  5.7 3.3 %collective-permute-start.1 = (f32[544,96]{0,1:T(8,128)S(1)}, f32[544,96]{0,1:T(8,128)}, u32[]{:S(2)}, u32[]{:S(2)}) collective-permute-start(f32[544,96]{0,1:T(8,128)S(1)} %dynamic-slice_bitcast_fusion), channel_id=1, source_target_pairs={{0,1},{1,0},{2,3},{3,2},{4,5},{5,4},{6,7},{7,6},{8,9},{9,8},{10,11... | collective-permute-start | bytes 626696 | tf_op jit(solution)/shard_map/ppermute | solution.py:35
  15.0 8.7 %all-to-all-start = ((f32[8,56,96]{2,1,0:T(8,128)}), f32[8,56,96]{2,1,0:T(8,128)}, u32[]{:S(2)}, u32[]{:S(2)}) async-start(f32[8,56,96]{2,1,0:T(8,128)} %broadcast_in_dim.20), calls=%async_computation | async-start | bytes 458752 | tf_op jit(solution)/shard_map/all_to_all | solution.py:51
  25.2 10.2 %all-to-all-done = f32[8,56,96]{2,1,0:T(8,128)} async-done(((f32[8,56,96]{2,1,0:T(8,128)}), f32[8,56,96]{2,1,0:T(8,128)}, u32[]{:S(2)}, u32[]{:S(2)}) %all-to-all-start) | async-done | bytes 172064 | tf_op jit(solution)/shard_map/all_to_all | solution.py:51
  37.2 4.5 %fusion.4 = f32[96,544]{1,0:T(8,128)} fusion(f32[1,1088,544]{1,2,0:T(8,128)S(1)} %copy-done, f32[544,96]{0,1:T(8,128)} %get-tuple-element.30, f32[544,96]{0,1:T(8,128)} %get-tuple-element.29), kind=kOutput, calls=%fused_computation.4 | convolution fusion | flops 681940992 | bytes 2994176 | tf_op jit(solution)/shard_map/dot_general | solution.py:25
  46.6 8.7 %all-to-all-start.1 = ((f32[16,56,96]{2,1,0:T(8,128)}), f32[16,56,96]{2,1,0:T(8,128)S(1)}, u32[]{:S(2)}, u32[]{:S(2)}) async-start(f32[16,56,96]{2,1,0:T(8,128)} %broadcast_in_dim.21), calls=%async_computation.1 | async-start | bytes 917504 | tf_op jit(solution)/shard_map/all_to_all | solution.py:51
  57.6 1.5 slice.498
  60.6 4.3 %all-to-all-done.1 = f32[16,56,96]{2,1,0:T(8,128)S(1)} async-done(((f32[16,56,96]{2,1,0:T(8,128)}), f32[16,56,96]{2,1,0:T(8,128)S(1)}, u32[]{:S(2)}, u32[]{:S(2)}) %all-to-all-start.1) | async-done | bytes 344096 | tf_op jit(solution)/shard_map/all_to_all | solution.py:51
  64.9 2.2 %collective-permute-start.5 = (f32[16,56,96]{2,1,0:T(8,128)S(1)}, f32[16,56,96]{2,1,0:T(8,128)}, u32[]{:S(2)}, u32[]{:S(2)}) collective-permute-start(f32[16,56,96]{2,1,0:T(8,128)S(1)} %all-to-all-done.1), channel_id=1, source_target_pairs={{0,1},{1,0},{2,3},{3,2},{4,5},{5,4},{6,7},{7,6},{8,9},{9,8},{10,11... | collective-permute-start | bytes 1032200 | tf_op jit(solution)/shard_map/ppermute | solution.py:35
  70.6 2.2 %copy.102 = f32[16,56,96]{1,2,0:T(8,128)} copy(f32[16,56,96]{2,1,0:T(8,128)} %collective-permute-done.5) | data formatting | bytes 688128 | tf_op jit(solution)/shard_map/ppermute | solution.py:35
  72.8 1.5 broadcast_select_fusion
  80.0 2.2 %fusion.12 = f32[9,544]{1,0:T(8,128)S(1)} fusion(f32[9,544]{1,0:T(8,128)S(1)} %fusion.75, f32[1,1088,544]{1,2,0:T(8,128)S(1)} %copy-done, f32[9,544]{1,0:T(8,128)S(1)} %copy-done.62, f32[9,544]{1,0:T(8,128)S(1)} %copy-done.61), kind=kOutput, calls=%fused_computation.16 | convolution fusion | flops 63936864 | bytes 2445824 | tf_op jit(solution)/shard_map/dot_general | solution.py:17
  82.2 2.3 %collective-permute-start.8 = (f32[9,544]{1,0:T(8,128)S(1)}, f32[9,544]{1,0:T(8,128)S(1)}, u32[]{:S(2)}, u32[]{:S(2)}) collective-permute-start(f32[9,544]{1,0:T(8,128)S(1)} %fusion.12), channel_id=1, source_target_pairs={{0,2},{2,4},{4,6},{6,8},{8,10},{10,12},{12,14},{14,16},{16,18},{18... | collective-permute-start | bytes 58760 | tf_op jit(solution)/shard_map/ppermute | solution.py:31
  89.5 5.3 %collective-permute-done.11 = f32[3,9,544]{2,1,0:T(8,128)S(1)} collective-permute-done((f32[3,9,544]{2,1,0:T(8,128)S(1)}, f32[3,9,544]{2,1,0:T(8,128)S(1)}, u32[]{:S(2)}, u32[]{:S(2)}) %collective-permute-start.11) | collective-permute-done | bytes 58784 | tf_op jit(solution)/shard_map/ppermute | solution.py:31
  97.5 5.8 %all-to-all-start.2 = ((f32[8,24,96]{2,1,0:T(8,128)}), f32[8,24,96]{2,1,0:T(8,128)}, u32[]{:S(2)}, u32[]{:S(2)}) async-start(f32[8,24,96]{2,1,0:T(8,128)} %broadcast_in_dim.23), calls=%async_computation.2 | async-start | bytes 196608 | tf_op jit(solution)/shard_map/all_to_all | solution.py:51
  103.3 2.3 %fusion.2 = f32[24,1088]{1,0:T(8,128)} fusion(f32[1,1088,544]{1,2,0:T(8,128)S(1)} %copy-done, f32[3,9,544]{2,1,0:T(8,128)} %copy-done.24), kind=kOutput, calls=%fused_computation.2 | convolution fusion | flops 85229568 | bytes 2533376 | tf_op jit(solution)/shard_map/dot_general | solution.py:21
  105.6 5.2 %all-to-all-done.2 = f32[8,24,96]{2,1,0:T(8,128)} async-done(((f32[8,24,96]{2,1,0:T(8,128)}), f32[8,24,96]{2,1,0:T(8,128)}, u32[]{:S(2)}, u32[]{:S(2)}) %all-to-all-start.2) | async-done | bytes 73760 | tf_op jit(solution)/shard_map/all_to_all | solution.py:51
  122.8 7.3 %all-to-all-start.3 = ((f32[16,24,96]{2,1,0:T(8,128)}), f32[16,24,96]{2,1,0:T(8,128)}, u32[]{:S(2)}, u32[]{:S(2)}) async-start(f32[16,24,96]{2,1,0:T(8,128)} %broadcast_in_dim.24), calls=%async_computation.3 | async-start | bytes 393216 | tf_op jit(solution)/shard_map/all_to_all | solution.py:51
  130.1 1.6 constant_dynamic-slice_fusion
  132.5 2.2 %collective-permute-start.12 = (f32[24,544]{1,0:T(8,128)}, f32[24,544]{1,0:T(8,128)}, u32[]{:S(2)}, u32[]{:S(2)}) collective-permute-start(f32[24,544]{1,0:T(8,128)} %constant_dynamic-slice_fusion), channel_id=1, source_target_pairs={{0,1},{1,0},{2,3},{3,2},{4,5},{5,4},{6,7},{7,6},{8,9},{9,8},{10,11... | collective-permute-start | bytes 156680 | tf_op jit(solution)/shard_map/ppermute | solution.py:35
  135.6 1.7 all-to-all-done.3
  154.4 3.3 %collective-permute-start.14 = (f32[128]{0:T(128)S(1)}, f32[128]{0:T(128)S(1)}, u32[]{:S(2)}, u32[]{:S(2)}) collective-permute-start(f32[128]{0:T(128)S(1)} %pad_maximum_fusion.4), channel_id=1, source_target_pairs={{0,1},{1,0},{2,3},{3,2},{4,5},{5,4},{6,7},{7,6},{8,9},{9,8},{10,11... | collective-permute-start | bytes 1544 | tf_op jit(solution)/shard_map/ppermute | solution.py:35
  158.6 16.1 %all_to_all.26 = f32[128,1,128]{2,1,0:T(1,128)S(1)} all-to-all(f32[128,1,128]{2,1,0:T(1,128)S(1)} %broadcast_in_dim.26), channel_id=1, replica_groups=mesh['row_0'=4,'row_1'=4,'row_2'=8,'col'=2] {'row_0','row_1','row_2'}, dimensions={0} | all-to-all | bytes 131072 | tf_op jit(solution)/shard_map/all_to_all | solution.py:51
  (298 shorter events, 67.4 us)
Async XLA Ops:
  0.7 11.0 %collective-permute-start.2 = (f32[544,96]{0,1:T(8,128)}, f32[544,96]{0,1:T(8,128)S(1)}, u32[]{:S(2)}, u32[]{:S(2)}) collective-permute-start(f32[544,96]{0,1:T(8,128)} %bitcast.495), channel_id=1, source_target_pairs={{2,0},{4,2},{6,4},{8,6},{10,8},{12,10},{14,12},{16,14},{18,16},{20... | collective-permute-start | bytes 626696 | tf_op jit(solution)/shard_map/ppermute | solution.py:31
  5.7 4.6 %collective-permute-start.1 = (f32[544,96]{0,1:T(8,128)S(1)}, f32[544,96]{0,1:T(8,128)}, u32[]{:S(2)}, u32[]{:S(2)}) collective-permute-start(f32[544,96]{0,1:T(8,128)S(1)} %dynamic-slice_bitcast_fusion), channel_id=1, source_target_pairs={{0,1},{1,0},{2,3},{3,2},{4,5},{5,4},{6,7},{7,6},{8,9},{9,8},{10,11... | collective-permute-start | bytes 626696 | tf_op jit(solution)/shard_map/ppermute | solution.py:35
  12.3 1.9 %collective-permute-start.3 = (f32[56,96]{0,1:T(8,128)S(1)}, f32[56,96]{0,1:T(8,128)S(1)}, u32[]{:S(2)}, u32[]{:S(2)}) collective-permute-start(f32[56,96]{0,1:T(8,128)S(1)} %constant_dynamic-slice_fusion.1), channel_id=1, source_target_pairs={{0,1},{1,0},{2,3},{3,2},{4,5},{5,4},{6,7},{7,6},{8,9},{9,8},{10,11... | collective-permute-start | bytes 64520 | tf_op jit(solution)/shard_map/ppermute | solution.py:35
  13.0 10.8 %collective-permute-start = (f32[9,544]{1,0:T(8,128)S(1)}, f32[9,544]{1,0:T(8,128)S(1)}, u32[]{:S(2)}, u32[]{:S(2)}) collective-permute-start(f32[9,544]{1,0:T(8,128)S(1)} %pad_maximum_fusion.2), channel_id=1, source_target_pairs={{0,1},{1,0},{2,3},{3,2},{4,5},{5,4},{6,7},{7,6},{8,9},{9,8},{10,11... | collective-permute-start | bytes 58760 | tf_op jit(solution)/shard_map/ppermute | solution.py:35
  13.7 10.7 %collective-permute-start.6 = (f32[544,96]{0,1:T(8,128)S(1)}, f32[544,96]{0,1:T(8,128)S(1)}, u32[]{:S(2)}, u32[]{:S(2)}) collective-permute-start(f32[544,96]{0,1:T(8,128)S(1)} %collective-permute-done.2), channel_id=1, source_target_pairs={{0,1},{1,0},{2,3},{3,2},{4,5},{5,4},{6,7},{7,6},{8,9},{9,8},{10,11... | collective-permute-start | bytes 626696 | tf_op jit(solution)/shard_map/ppermute | solution.py:35
  15.0 20.4 %all-to-all-start = ((f32[8,56,96]{2,1,0:T(8,128)}), f32[8,56,96]{2,1,0:T(8,128)}, u32[]{:S(2)}, u32[]{:S(2)}) async-start(f32[8,56,96]{2,1,0:T(8,128)} %broadcast_in_dim.20), calls=%async_computation | async-start | bytes 458752 | tf_op jit(solution)/shard_map/all_to_all | solution.py:51
  36.5 5.1 %collective-permute-start.4 = (f32[8,56,96]{1,2,0:T(8,128)S(1)}, f32[8,56,96]{1,2,0:T(8,128)S(1)}, u32[]{:S(2)}, u32[]{:S(2)}) collective-permute-start(f32[8,56,96]{1,2,0:T(8,128)S(1)} %copy.97), channel_id=1, source_target_pairs={{0,1},{1,0},{2,3},{3,2},{4,5},{5,4},{6,7},{7,6},{8,9},{9,8},{10,11... | collective-permute-start | bytes 516104 | tf_op jit(solution)/shard_map/ppermute | solution.py:35
  43.3 27.2 %copy-start.14 = (f32[96,96]{0,1:T(8,128)}, f32[96,96]{0,1:T(8,128)S(1)}, u32[]{:S(2)}) copy-start(f32[96,96]{0,1:T(8,128)S(1)} %get-tuple-element.21) | copy-start | bytes 110596
  43.3 27.2 %copy-start.15 = (f32[96,96]{0,1:T(8,128)}, f32[96,96]{0,1:T(8,128)S(1)}, u32[]{:S(2)}) copy-start(f32[96,96]{0,1:T(8,128)S(1)} %get-tuple-element.22) | copy-start | bytes 110596
  43.3 27.2 %copy-start.16 = (f32[96,96]{0,1:T(8,128)}, f32[96,96]{0,1:T(8,128)S(1)}, u32[]{:S(2)}) copy-start(f32[96,96]{0,1:T(8,128)S(1)} %get-tuple-element.23) | copy-start | bytes 110596
  43.3 27.2 %copy-start.17 = (f32[96,96]{0,1:T(8,128)}, f32[96,96]{0,1:T(8,128)S(1)}, u32[]{:S(2)}) copy-start(f32[96,96]{0,1:T(8,128)S(1)} %get-tuple-element.24) | copy-start | bytes 110596
  43.6 27.0 %copy-start.12 = (f32[112,96]{0,1:T(8,128)}, f32[112,96]{0,1:T(8,128)S(1)}, u32[]{:S(2)}) copy-start(f32[112,96]{0,1:T(8,128)S(1)} %fusion.56) | copy-start | bytes 129028
  46.6 18.3 %all-to-all-start.1 = ((f32[16,56,96]{2,1,0:T(8,128)}), f32[16,56,96]{2,1,0:T(8,128)S(1)}, u32[]{:S(2)}, u32[]{:S(2)}) async-start(f32[16,56,96]{2,1,0:T(8,128)} %broadcast_in_dim.21), calls=%async_computation.1 | async-start | bytes 917504 | tf_op jit(solution)/shard_map/all_to_all | solution.py:51
  64.9 5.7 %collective-permute-start.5 = (f32[16,56,96]{2,1,0:T(8,128)S(1)}, f32[16,56,96]{2,1,0:T(8,128)}, u32[]{:S(2)}, u32[]{:S(2)}) collective-permute-start(f32[16,56,96]{2,1,0:T(8,128)S(1)} %all-to-all-done.1), channel_id=1, source_target_pairs={{0,1},{1,0},{2,3},{3,2},{4,5},{5,4},{6,7},{7,6},{8,9},{9,8},{10,11... | collective-permute-start | bytes 1032200 | tf_op jit(solution)/shard_map/ppermute | solution.py:35
  82.2 4.4 %collective-permute-start.8 = (f32[9,544]{1,0:T(8,128)S(1)}, f32[9,544]{1,0:T(8,128)S(1)}, u32[]{:S(2)}, u32[]{:S(2)}) collective-permute-start(f32[9,544]{1,0:T(8,128)S(1)} %fusion.12), channel_id=1, source_target_pairs={{0,2},{2,4},{4,6},{6,8},{8,10},{10,12},{12,14},{14,16},{16,18},{18... | collective-permute-start | bytes 58760 | tf_op jit(solution)/shard_map/ppermute | solution.py:31
  85.1 2.4 %collective-permute-start.10 = (f32[3,9,96]{2,1,0:T(8,128)S(1)}, f32[3,9,96]{2,1,0:T(8,128)S(1)}, u32[]{:S(2)}, u32[]{:S(2)}) collective-permute-start(f32[3,9,96]{2,1,0:T(8,128)S(1)} %convolution_bitcast_fusion), channel_id=1, source_target_pairs={{0,1},{1,0},{2,3},{3,2},{4,5},{5,4},{6,7},{7,6},{8,9},{9,8},{10,11... | collective-permute-start | bytes 31112 | tf_op jit(solution)/shard_map/ppermute | solution.py:35
  86.3 3.2 %collective-permute-start.7 = (f32[3,9,544]{2,1,0:T(8,128)S(1)}, f32[3,9,544]{2,1,0:T(8,128)S(1)}, u32[]{:S(2)}, u32[]{:S(2)}) collective-permute-start(f32[3,9,544]{2,1,0:T(8,128)S(1)} %dynamic-slice_bitcast_fusion.1), channel_id=1, source_target_pairs={{0,1},{1,0},{2,3},{3,2},{4,5},{5,4},{6,7},{7,6},{8,9},{9,8},{10,11... | collective-permute-start | bytes 176264 | tf_op jit(solution)/shard_map/ppermute | solution.py:35
  87.1 2.0 %collective-permute-start.9 = (f32[3,9,96]{2,1,0:T(8,128)S(1)}, f32[3,9,96]{2,1,0:T(8,128)S(1)}, u32[]{:S(2)}, u32[]{:S(2)}) collective-permute-start(f32[3,9,96]{2,1,0:T(8,128)S(1)} %convolution_bitcast_fusion.1), channel_id=1, source_target_pairs={{0,1},{1,0},{2,3},{3,2},{4,5},{5,4},{6,7},{7,6},{8,9},{9,8},{10,11... | collective-permute-start | bytes 31112 | tf_op jit(solution)/shard_map/ppermute | solution.py:35
  87.8 6.9 %collective-permute-start.11 = (f32[3,9,544]{2,1,0:T(8,128)S(1)}, f32[3,9,544]{2,1,0:T(8,128)S(1)}, u32[]{:S(2)}, u32[]{:S(2)}) collective-permute-start(f32[3,9,544]{2,1,0:T(8,128)S(1)} %fusion.16), channel_id=1, source_target_pairs={{2,0},{4,2},{6,4},{8,6},{10,8},{12,10},{14,12},{16,14},{18,16},{20... | collective-permute-start | bytes 176264 | tf_op jit(solution)/shard_map/ppermute | solution.py:31
  95.1 1.8 %collective-permute-start.13 = (f32[24,96]{1,0:T(8,128)S(1)}, f32[24,96]{1,0:T(8,128)S(1)}, u32[]{:S(2)}, u32[]{:S(2)}) collective-permute-start(f32[24,96]{1,0:T(8,128)S(1)} %fusion.35), channel_id=1, source_target_pairs={{0,1},{1,0},{2,3},{3,2},{4,5},{5,4},{6,7},{7,6},{8,9},{9,8},{10,11... | collective-permute-start | bytes 27656 | tf_op jit(solution)/shard_map/ppermute | solution.py:35
  97.5 13.3 %all-to-all-start.2 = ((f32[8,24,96]{2,1,0:T(8,128)}), f32[8,24,96]{2,1,0:T(8,128)}, u32[]{:S(2)}, u32[]{:S(2)}) async-start(f32[8,24,96]{2,1,0:T(8,128)} %broadcast_in_dim.23), calls=%async_computation.2 | async-start | bytes 196608 | tf_op jit(solution)/shard_map/all_to_all | solution.py:51
  122.8 14.5 %all-to-all-start.3 = ((f32[16,24,96]{2,1,0:T(8,128)}), f32[16,24,96]{2,1,0:T(8,128)}, u32[]{:S(2)}, u32[]{:S(2)}) async-start(f32[16,24,96]{2,1,0:T(8,128)} %broadcast_in_dim.24), calls=%async_computation.3 | async-start | bytes 393216 | tf_op jit(solution)/shard_map/all_to_all | solution.py:51
  132.5 20.1 %collective-permute-start.12 = (f32[24,544]{1,0:T(8,128)}, f32[24,544]{1,0:T(8,128)}, u32[]{:S(2)}, u32[]{:S(2)}) collective-permute-start(f32[24,544]{1,0:T(8,128)} %constant_dynamic-slice_fusion), channel_id=1, source_target_pairs={{0,1},{1,0},{2,3},{3,2},{4,5},{5,4},{6,7},{7,6},{8,9},{9,8},{10,11... | collective-permute-start | bytes 156680 | tf_op jit(solution)/shard_map/ppermute | solution.py:35
  154.4 4.1 %collective-permute-start.14 = (f32[128]{0:T(128)S(1)}, f32[128]{0:T(128)S(1)}, u32[]{:S(2)}, u32[]{:S(2)}) collective-permute-start(f32[128]{0:T(128)S(1)} %pad_maximum_fusion.4), channel_id=1, source_target_pairs={{0,1},{1,0},{2,3},{3,2},{4,5},{5,4},{6,7},{7,6},{8,9},{9,8},{10,11... | collective-permute-start | bytes 1544 | tf_op jit(solution)/shard_map/ppermute | solution.py:35
  (74 other events, 475.7 us)

commit v2 on v1

--- a/solution.py
+++ b/solution.py
@@ -1,6 +1,10 @@
+import functools
+
 import jax
 import jax.numpy as jnp
 from jax import lax
+from jax.experimental import pallas as pl
+from jax.experimental.pallas import tpu as pltpu
 from jax.sharding import Mesh
 from jax.sharding import PartitionSpec as P
 
@@ -49,6 +53,114 @@
 def everywhere(x, axis):
     count = lax.axis_size(axis)
     return lax.all_to_all(jnp.broadcast_to(x[None], (count, *x.shape)), axis, 0, 0, tiled=True)
+
+
+LANES = 128
+SMEM = pl.BlockSpec(memory_space=pltpu.SMEM)
+VMEM = pl.BlockSpec(memory_space=pltpu.VMEM)
+
+
+def on_core(kernel, outs, scalars, arrays, flops):
+    moved = sum(a.size * a.dtype.itemsize for a in arrays) + sum(4 * o.size for o in outs)
+    return pl.pallas_call(
+        kernel,
+        out_shape=outs,
+        in_specs=[SMEM] + [VMEM] * len(arrays),
+        out_specs=[VMEM] * len(outs),
+        compiler_params=pltpu.CompilerParams(vmem_limit_bytes=40 * 1024 * 1024),
+        cost_estimate=pl.CostEstimate(flops=flops, bytes_accessed=moved, transcendentals=0),
+    )(scalars, *arrays)
+
+
+def floats(*shape):
+    return jax.ShapeDtypeStruct(shape, jnp.float32)
+
+
+def whole_map(side, mine, other, k):
+    first = jnp.where(side == 0, mine[k], other[k])
+    second = jnp.where(side == 0, other[k], mine[k])
+    return jnp.concatenate([first, second], axis=0)
+
+
+def line_back(rmax, where, mine, other, reach, prefix, send):
+    side, place = where[0], where[1]
+    count, half_rows = mine.shape[0], mine.shape[1]
+    rows = 2 * half_rows
+    maps = [whole_map(side, mine, other, k) for k in range(count)]
+    run = maps[-1]
+    reach[count - 1] = run
+    row = lax.broadcasted_iota(jnp.int32, (rmax, LANES), 0)
+    lane = lax.broadcasted_iota(jnp.int32, (rmax, LANES), 1)
+    early = (row == lane).astype(jnp.float32)
+    chosen = early
+    for k in range(count - 1):
+        run = dot(run[:, :rows], maps[count - 2 - k])
+        reach[count - 2 - k] = run
+        early = maps[0][:rmax] if k == 0 else dot(maps[k][:rmax, :rmax], early)
+        chosen = jnp.where(place == k + 1, early, chosen)
+    prefix[...] = chosen
+    out = jnp.where(side == 0, run[:half_rows], run[half_rows:])
+    for g in range(send.shape[0]):
+        send[g] = out
+
+
+def plane_back(rmax, where, mine, other, reach, base, wide, solution):
+    side, place, group = where[0], where[1], where[2]
+    groups, half_rows = mine.shape[0], mine.shape[1]
+    count = reach.shape[0]
+    rows = 2 * half_rows
+    row = lax.broadcasted_iota(jnp.int32, (rows - rmax, LANES), 0)
+    lane = lax.broadcasted_iota(jnp.int32, (rows - rmax, LANES), 1)
+    state = ((row + rmax == lane) & (row < base.shape[0])).astype(jnp.float32)
+    ahead = state
+    for g in reversed(range(1, groups)):
+        state = dot(state[:, :rows], whole_map(side, mine, other, g))
+        ahead = jnp.where(group == g - 1, state, ahead)
+    through = dot(ahead[:, :rows], reach[jnp.minimum(place + 1, count - 1)])
+    coeff = jnp.where(place == count - 1, ahead, through)
+    change = dot(coeff[:, :rmax], wide[...])
+    solution[...] = base[...] - change[: base.shape[0]]
+
+
+def line_forward(rmax, where, mine, other, offsets, local, send):
+    side, place = where[0], where[1]
+    state = jnp.zeros(local.shape, jnp.float32)
+    chosen = state
+    for k in range(mine.shape[0]):
+        chosen = jnp.where(place == k, state, chosen)
+        turn = whole_map(side, mine, other, k)[:rmax, :rmax]
+        state = offsets[k] + dot_nt(state, turn)
+    local[...] = chosen
+    for g in range(send.shape[0]):
+        send[g] = state
+
+
+def plane_forward(
+    rmax, where, mine, other, outs, prefix, local, plain, moved, source, result, sums
+):
+    side, group = where[0], where[2]
+    params = plain.shape[0] // (source.shape[0] - 1)
+    state = jnp.zeros(local.shape, jnp.float32)
+    behind = state
+    for g in range(mine.shape[0] - 1):
+        turn = whole_map(side, mine, other, g)[:rmax, :rmax]
+        state = outs[g] + dot_nt(state, turn)
+        behind = jnp.where(group == g + 1, state, behind)
+    entry = local[...] + dot_nt(behind, prefix[:, :rmax])
+    final = plain[...] - dot_nt(entry, moved[:, :rmax])
+    result[...] = final
+    each = final.shape[0] // params
+    parts = [final[k * each : (k + 1) * each] for k in range(params)]
+    signs = source[1:]
+    lane = lax.broadcasted_iota(jnp.int32, sums.shape, 1)
+    total = jnp.zeros(sums.shape, jnp.float32)
+    for k in range(params):
+        for j in range(k, params):
+            both = jnp.sum(parts[k] * parts[j], keepdims=True)
+            total = jnp.where((lane == k * params + j) | (lane == j * params + k), both, total)
+        both = jnp.sum(parts[k] * signs, keepdims=True)
+        total = jnp.where(lane == params * params + k, both, total)
+    sums[...] = total
 
 
 def body(
@@ -67,7 +179,8 @@
     right_next = along_rows(low_right[0], -1)
     columns = jnp.arange(rmax, dtype=jnp.int32)
     masks = (columns[None, :] < ranks[:, 0][:, None]).astype(jnp.float32)
-    own_left = low_left[0] * masks[0][None, :]
+    own_left = jnp.pad(low_left[0] * masks[0][None, :], ((0, 0), (0, LANES - rmax)))
+    where = jnp.stack([side, place, group]).astype(jnp.int32)
     d_left = deriv_left[:, 0] * masks[1:][:, None, :]
     d_right = deriv_right[:, 0]
     source = jnp.concatenate([whitened[None, :], probes.astype(jnp.float32)], axis=0)
@@ -76,36 +189,33 @@
     moved = dot(inverse, own_left)
     moved = part(moved, side, 0) + swapped(part(moved, 1 - side, 0))
     lines = -(-(count + 1) // 16) * 16
-    blank = jnp.zeros((lines - count - 1, rmax), jnp.float32)
+    blank = jnp.zeros((lines - count - 1, LANES), jnp.float32)
+    keep = jnp.pad(jnp.eye(count + 1, dtype=jnp.float32), ((rmax, lines - count - 1), (rmax, LANES - rmax - count - 1)))
     own_map = jnp.concatenate([-dot_tn(right_next, moved), dot(source, moved), blank], axis=0)
-    own_map = part(own_map, side, 0) + swapped(part(own_map, 1 - side, 0))
+    own_map = part(own_map, side, 0) + swapped(part(own_map, 1 - side, 0)) + part(keep, side, 0)
     right_full = joined(right_next, swapped(right_next), side, 0)
     base = dot(source_full, inverse)
     wide = dot_tn(right_full, inverse)
 
-    got = everywhere(own_map, LINE)
-    maps = joined(got, swapped(got), side, 1)
-    turns = maps[:, :rmax]
-    lifts = maps[:, rmax:]
-    reach = [None] * in_line
-    reach[-1] = maps[-1]
-    zero_top = jnp.zeros((rmax, rmax), jnp.float32)
-    for k in reversed(range(in_line - 1)):
-        reach[k] = dot(reach[k + 1], turns[k]) + jnp.concatenate([zero_top, lifts[k]], axis=0)
-    total_map = reach[0]
-    got = everywhere(part(total_map, side, 0), PLANE)
-    totals = joined(got, swapped(got), side, 1)
-    state = jnp.zeros((lines, rmax), jnp.float32)
-    ahead = state
-    for g in reversed(range(1, groups)):
-        state = totals[g, rmax:] + dot(state, totals[g, :rmax])
-        ahead = jnp.where(group == g - 1, state, ahead)
-    coeff = ahead
-    for k in range(1, in_line):
-        through = reach[k][rmax:] + dot(ahead, reach[k][:rmax])
-        coeff = jnp.where(place == k - 1, through, coeff)
-    coeff = coeff[: count + 1]
-    solution = base - dot(coeff, wide)
+    rows = rmax + lines
+    maps = everywhere(own_map, LINE)
+    maps_other = swapped(maps)
+    reach, prefix, send = on_core(
+        functools.partial(line_back, rmax),
+        [floats(in_line, rows, LANES), floats(rmax, LANES), floats(groups, rows // 2, LANES)],
+        where,
+        [maps, maps_other],
+        4 * in_line * rows * rmax * rmax,
+    )
+    totals = lax.all_to_all(send, PLANE, 0, 0, tiled=True)
+    totals_other = swapped(totals)
+    (solution,) = on_core(
+        functools.partial(plane_back, rmax),
+        [floats(count + 1, half)],
+        where,
+        [totals, totals_other, reach, base, wide],
+        2 * lines * rmax * (groups * LANES + half),
+    )
 
     rounded = solution.astype(jnp.bfloat16)
     prior = along_rows(solution, 1)
@@ -127,33 +237,26 @@
     plain = dot_nt(drive, inverse, high)
     plain = part(plain, side, 1) + swapped(part(plain, 1 - side, 1))
 
+    data_part = jnp.einsum("kh,h->k", applied[:, 0], solution[0], precision=highest)
     offsets = everywhere(shared, LINE)
-    state = jnp.zeros_like(shared)
-    local = state
-    spread = jnp.eye(rmax, dtype=jnp.float32)
-    own_spread = spread
-    for k in range(in_line):
-        state = offsets[k] + dot_nt(state, turns[k], high)
-        if k < in_line - 1:
-            spread = dot_nt(spread, turns[k], high) if k else turns[0].T
-            local = jnp.where(place == k + 1, state, local)
-            own_spread = jnp.where(place == k + 1, spread, own_spread)
-    outs = everywhere(state, PLANE)
-    state = jnp.zeros_like(shared)
-    behind = state
-    for g in range(groups - 1):
-        state = outs[g] + dot_nt(state, totals[g, :rmax], high)
-        behind = jnp.where(group == g + 1, state, behind)
-    entry = local + dot(behind, own_spread, high)
-    flat_result = plain - dot_nt(entry, moved, high)
+    local, send = on_core(
+        functools.partial(line_forward, rmax),
+        [floats(params * count, rmax), floats(groups, params * count, rmax)],
+        where,
+        [maps, maps_other, offsets],
+        2 * in_line * params * count * rmax * rmax,
+    )
+    outs = lax.all_to_all(send, PLANE, 0, 0, tiled=True)
+    flat_result, sums = on_core(
+        functools.partial(plane_forward, rmax),
+        [floats(params * count, half), floats(1, LANES)],
+        where,
+        [totals, totals_other, outs, prefix, local, plain, moved, source],
+        2 * params * count * rmax * (groups * rmax + half),
+    )
     result = flat_result.reshape(params, count, half)
-
-    trace_part = jnp.einsum("kph,ph->k", result, source[1:], precision=high)
-    fisher_part = jnp.einsum("kph,lph->kl", result, result, precision=high)
-    data_part = jnp.einsum("kh,h->k", applied[:, 0], solution[0], precision=high)
-    sums = jnp.concatenate(
-        [fisher_part.reshape(-1), trace_part, data_part, jnp.zeros((128 - params * (params + 2),))]
-    )
+    data_at = params * (params + 1)
+    sums = sums.reshape(-1) + jnp.pad(data_part, (data_at, LANES - data_at - params))
     sums = sums + swapped(sums)
     sums = jnp.sum(everywhere(sums, ROW).reshape(-1, 128), axis=0)
     fisher_sum = sums[: params * params].reshape(params, params)

time: 178 us -> 156 us (0.88)
  matrix products: 50.9 us -> 17 us
  blocking collectives: 16.1 us -> 33.3 us
  Pallas kernels: 0 us -> 13.1 us
  local copies, waits for them, and re-layouts: 20.7 us -> 11 us
  starting transfers between devices: 50.4 us -> 41.7 us
  waiting for transfers between devices: 28 us -> 30.8 us
    dot_general x32 -> x2, matrix products: 30.2 us -> 1.65 us  [dot_nt(): lax.dot_general(a, b, (((1,), (1,)), ((), ())), precision=precision, pref...]
    all_to_all x4 -> x1, starting transfers between devices: 30.5 us -> 5.78 us  [everywhere(): lax.all_to_all(jnp.broadcast_to(x[None], (count, *x.shape)), axis, 0, 0,...]
    all_to_all x1 -> x2, blocking collectives: 16.1 us -> 33.3 us  [everywhere(): lax.all_to_all(jnp.broadcast_to(x[None], (count, *x.shape)), axis, 0, 0,...]
    all_to_all x4 -> x1, waiting for transfers between devices: 21.4 us -> 4.45 us  [everywhere(): lax.all_to_all(jnp.broadcast_to(x[None], (count, *x.shape)), axis, 0, 0,...]
    all_to_all x0 -> x2, starting transfers between devices: none -> 16.1 us  [the longest x1 8.69 us: body(): totals = lax.all_to_all(send, PLANE, 0, 0, tiled=True)]
    pallas_call x0 -> x4, Pallas kernels: none -> 13.1 us  [on_core(): pl.pallas_call(kernel, out_shape=outs, in_specs=[SMEM] + [VMEM] * len(arr...]
    all_to_all x0 -> x2, waiting for transfers between devices: none -> 12.3 us  [the longest x1 6.15 us: body(): outs = lax.all_to_all(send, PLANE, 0, 0, tiled=True)]
    ppermute x3, waiting for transfers between devices: 5.26 us -> 12 us  [along_rows(): return lax.ppermute(block, ROW, route)]
  transfers between devices with their start and end apart: 19 -> 18, of which waited for: 7 -> 8; matrix products, arithmetic and copies ran while one was open for 26% -> 12% of each run, Pallas kernels for 0% -> 3%
where the time goes in v2:
time: 156 us; the launch traced here: 155 us
  starting transfers between devices  41.7 us (27%)
  blocking collectives  33.3 us (21%)
  waiting for transfers between devices  30.8 us (20%)
  matrix products  17 us (11%)
  Pallas kernels  13.1 us (8%)
  local copies, waits for them, and re-layouts  11 us (7%)
  other arithmetic  6.82 us (4%)
    all_to_all x2, blocking collectives, everywhere(): lax.all_to_all(jnp.broadcast_to(x[None], (count, *x.shape)), axis, 0, 0,...  33.3 us
    ppermute x12, starting transfers between devices, swapped(): return lax.ppermute(block, 'col', [(0, 1), (1, 0)])  14.8 us
    pallas_call x4, Pallas kernels, on_core(): pl.pallas_call(kernel, out_shape=outs, in_specs=[SMEM] + [VMEM] * len(arr...  13.1 us
    ppermute x3, waiting for transfers between devices, along_rows(): return lax.ppermute(block, ROW, route)  12 us
    all_to_all x1, starting transfers between devices, body(): totals = lax.all_to_all(send, PLANE, 0, 0, tiled=True)  8.69 us
    all_to_all x1, starting transfers between devices, body(): outs = lax.all_to_all(send, PLANE, 0, 0, tiled=True)  7.37 us
    dot_general x3, matrix products, dot(): lax.dot_general(a, b, (((1,), (0,)), ((), ())), precision=precision, pref...  7.17 us
    unnamed x48, local copies, waits for them, and re-layouts  6.43 us
  transfers between devices with their start and end apart: 18, of which 8 were waited for; matrix products, arithmetic and copies ran while one was open for 12% of the time, Pallas kernels for 3%

profile of v2, /device:TPU:1, one launch (start us, length us, event | category | flops | bytes accessed | tf_op | source)
XLA Modules:
  0.0 154.8 jit_solution(138956355019632425)
XLA Ops:
  2.6 4.7 %fusion.8 = f32[128,1088]{0,1:T(8,128)S(1)} fusion(f32[1,1088,544]{1,2,0:T(8,128)S(1)} %copy-done, f32[544,96]{0,1:T(8,128)S(1)} %bitcast_multiply_fusion.3), kind=kOutput, calls=%fused_computation.8 | convolution fusion | flops 909115392 | bytes 3133440 | tf_op jit(solution)/shard_map/dot_general | solution.py:21
  7.4 3.3 %collective-permute-start = (f32[544,128]{1,0:T(8,128)S(1)}, f32[544,128]{1,0:T(8,128)}, u32[]{:S(2)}, u32[]{:S(2)}) collective-permute-start(f32[544,128]{1,0:T(8,128)S(1)} %dynamic-slice_bitcast_fusion), channel_id=1, source_target_pairs={{0,1},{1,0},{2,3},{3,2},{4,5},{5,4},{6,7},{7,6},{8,9},{9,8},{10,11... | collective-permute-start | bytes 835592 | tf_op jit(solution)/shard_map/ppermute | solution.py:39
  13.4 7.1 %collective-permute-done.1 = f32[544,96]{0,1:T(8,128)} collective-permute-done((f32[544,96]{0,1:T(8,128)}, f32[544,96]{0,1:T(8,128)}, u32[]{:S(2)}, u32[]{:S(2)}) %collective-permute-start.1) | collective-permute-done | bytes 208928 | tf_op jit(solution)/shard_map/ppermute | solution.py:35
  23.8 17.2 %all_to_all.26.mine = f32[8,56,128]{2,1,0:T(8,128)S(1)} all-to-all(f32[8,56,128]{2,1,0:T(8,128)S(1)} %broadcast_in_dim.12), channel_id=1, replica_groups=mesh['row_0'=4,'row_1'=4,'row_2'=8,'col'=2] {'row_2'}, dimensions={0} | all-to-all | bytes 458752 | tf_op jit(solution)/shard_map/all_to_all | solution.py:55
  41.0 1.9 %collective-permute-start.3 = (f32[8,56,128]{2,1,0:T(8,128)S(1)}, f32[8,56,128]{2,1,0:T(8,128)S(1)}, u32[]{:S(2)}, u32[]{:S(2)}) collective-permute-start(f32[8,56,128]{2,1,0:T(8,128)S(1)} %all_to_all.26.mine), channel_id=1, source_target_pairs={{0,1},{1,0},{2,3},{3,2},{4,5},{5,4},{6,7},{7,6},{8,9},{9,8},{10,11... | collective-permute-start | bytes 688136 | tf_op jit(solution)/shard_map/ppermute | solution.py:39
  44.0 2.0 %shard_map.120 = (f32[8,112,128]{2,1,0:T(8,128)S(1)}, f32[96,128]{1,0:T(8,128)S(1)}, f32[16,56,128]{2,1,0:T(8,128)S(1)}) custom-call(s32[3]{0:T(128)S(1)} %pad_add_fusion.where, f32[8,56,128]{2,1,0:T(8,128)S(1)} %all_to_all.26.mine, f32[8,56,128]{2,1,0:T(8,128)S(1)} %collective-permute-done.3.other), custom_call_target="tpu_custom_call" | custom-call | flops 33030144 | bytes 1425408 | tf_op jit(solution)/shard_map/pallas_call | solution.py:65
  48.2 8.7 %all-to-all-start.1 = ((f32[16,56,128]{2,1,0:T(8,128)}), f32[16,56,128]{2,1,0:T(8,128)S(1)}, u32[]{:S(2)}, u32[]{:S(2)}) async-start(f32[16,56,128]{2,1,0:T(8,128)} %copy-done.5), calls=%async_computation.1 | async-start | bytes 917504 | tf_op jit(solution)/shard_map/all_to_all | solution.py:210
  58.4 2.2 %fusion.6.base = f32[9,544]{1,0:T(8,128)S(1)} fusion(f32[1,1088,544]{1,2,0:T(8,128)S(1)} %copy-done, f32[9,544]{1,0:T(8,128)S(1)} %get-tuple-element.21, f32[9,544]{1,0:T(8,128)S(1)} %get-tuple-element.20), kind=kOutput, calls=%fused_computation.6 | convolution fusion | flops 63931968 | bytes 2426240 | tf_op jit(solution)/shard_map/dot_general | solution.py:21
  60.6 6.1 %all-to-all-done.1.mine = f32[16,56,128]{2,1,0:T(8,128)S(1)} async-done(((f32[16,56,128]{2,1,0:T(8,128)}), f32[16,56,128]{2,1,0:T(8,128)S(1)}, u32[]{:S(2)}, u32[]{:S(2)}) %all-to-all-start.1) | async-done | bytes 458784 | tf_op jit(solution)/shard_map/all_to_all | solution.py:210
  66.7 1.9 %collective-permute-start.4 = (f32[16,56,128]{2,1,0:T(8,128)S(1)}, f32[16,56,128]{2,1,0:T(8,128)S(1)}, u32[]{:S(2)}, u32[]{:S(2)}) collective-permute-start(f32[16,56,128]{2,1,0:T(8,128)S(1)} %all-to-all-done.1.mine), channel_id=1, source_target_pairs={{0,1},{1,0},{2,3},{3,2},{4,5},{5,4},{6,7},{7,6},{8,9},{9,8},{10,11... | collective-permute-start | bytes 1376264 | tf_op jit(solution)/shard_map/ppermute | solution.py:39
  69.8 2.8 %fusion.4.wide = f32[96,544]{1,0:T(8,128)S(1)} fusion(f32[1,1088,544]{1,2,0:T(8,128)S(1)} %copy-done, f32[544,96]{0,1:T(8,128)S(1)} %get-tuple-element.19, f32[544,96]{0,1:T(8,128)S(1)} %get-tuple-element.18), kind=kOutput, calls=%fused_computation.4 | convolution fusion | flops 681940992 | bytes 2994176 | tf_op jit(solution)/shard_map/dot_general | solution.py:29
  72.6 4.5 %shard_map.121 = f32[9,544]{1,0:T(8,128)} custom-call(s32[3]{0:T(128)S(1)} %copy-done.14, f32[16,56,128]{2,1,0:T(8,128)S(1)} %all-to-all-done.1.mine, f32[16,56,128]{2,1,0:T(8,128)S(1)} %collective-permute-done.4.other, f32[8,112,128]{2,1,0:T(8,128)S(1)} %copy-done.7, f32[9,544]{1,0:T(8,128)S(1)} %fusion.6.base, f32[96,544]{1,0:T(8,128)S(1)} %fusion.4.wide), custom_call_target="tpu_custom_call" | custom-call | flops 7962624 | bytes 1624320 | tf_op jit(solution)/shard_map/pallas_call | solution.py:65
  77.1 2.3 %collective-permute-start.8 = (f32[9,544]{1,0:T(8,128)}, f32[9,544]{1,0:T(8,128)S(1)}, u32[]{:S(2)}, u32[]{:S(2)}) collective-permute-start(f32[9,544]{1,0:T(8,128)} %shard_map.121), channel_id=1, source_target_pairs={{0,2},{2,4},{4,6},{6,8},{8,10},{10,12},{12,14},{14,16},{16,18},{18... | collective-permute-start | bytes 58760 | tf_op jit(solution)/shard_map/ppermute | solution.py:35
  86.1 5.0 %collective-permute-done.11 = f32[3,9,544]{2,1,0:T(8,128)S(1)} collective-permute-done((f32[3,9,544]{2,1,0:T(8,128)S(1)}, f32[3,9,544]{2,1,0:T(8,128)S(1)}, u32[]{:S(2)}, u32[]{:S(2)}) %collective-permute-start.11) | collective-permute-done | bytes 58784 | tf_op jit(solution)/shard_map/ppermute | solution.py:35
  92.5 1.5 fusion.2
  94.6 5.8 %all-to-all-start.2 = ((f32[8,24,96]{2,1,0:T(8,128)}), f32[8,24,96]{2,1,0:T(8,128)}, u32[]{:S(2)}, u32[]{:S(2)}) async-start(f32[8,24,96]{2,1,0:T(8,128)} %broadcast_in_dim.13), calls=%async_computation.2 | async-start | bytes 196608 | tf_op jit(solution)/shard_map/all_to_all | solution.py:55
  100.4 1.6 %constant_dynamic-slice_fusion = f32[24,544]{1,0:T(8,128)} fusion(f32[24,1088]{1,0:T(8,128)} %fusion.2, s32[]{:T(128)S(6)} %select_n.42), kind=kLoop, calls=%fused_computation.58 | loop fusion | bytes 104452 | tf_op jit(solution)/shard_map/dynamic_slice | solution.py:44
  103.5 4.4 %all-to-all-done.2.offsets = f32[8,24,96]{2,1,0:T(8,128)} async-done(((f32[8,24,96]{2,1,0:T(8,128)}), f32[8,24,96]{2,1,0:T(8,128)}, u32[]{:S(2)}, u32[]{:S(2)}) %all-to-all-start.2) | async-done | bytes 73760 | tf_op jit(solution)/shard_map/all_to_all | solution.py:55
  108.9 2.3 %shard_map.122 = (f32[24,96]{1,0:T(8,128)S(1)}, f32[16,24,96]{2,1,0:T(8,128)S(1)}) custom-call(s32[3]{0:T(128)S(1)} %copy-done.15, f32[8,56,128]{2,1,0:T(8,128)S(1)} %all_to_all.26.mine, f32[8,56,128]{2,1,0:T(8,128)S(1)} %copy-done.4, f32[8,24,96]{2,1,0:T(8,128)} %all-to-all-done.2.offsets), custom_call_target="tpu_custom_call" | custom-call | flops 3538944 | bytes 689152 | tf_op jit(solution)/shard_map/pallas_call | solution.py:65
  111.8 7.4 %all-to-all-start.3 = ((f32[16,24,96]{2,1,0:T(8,128)}), f32[16,24,96]{2,1,0:T(8,128)S(1)}, u32[]{:S(2)}, u32[]{:S(2)}) async-start(f32[16,24,96]{2,1,0:T(8,128)} %copy-done.8), calls=%async_computation.3 | async-start | bytes 393216 | tf_op jit(solution)/shard_map/all_to_all | solution.py:249
  120.2 6.2 %all-to-all-done.3.outs = f32[16,24,96]{2,1,0:T(8,128)S(1)} async-done(((f32[16,24,96]{2,1,0:T(8,128)}), f32[16,24,96]{2,1,0:T(8,128)S(1)}, u32[]{:S(2)}, u32[]{:S(2)}) %all-to-all-start.3) | async-done | bytes 147488 | tf_op jit(solution)/shard_map/all_to_all | solution.py:249
  128.9 4.3 %shard_map.123 = (f32[24,544]{1,0:T(8,128)}, f32[1,128]{1,0:T(1,128)S(1)}) custom-call(s32[3]{0:T(128)S(1)} %copy-done.15, f32[16,56,128]{2,1,0:T(8,128)S(1)} %all-to-all-done.1.mine, f32[16,56,128]{2,1,0:T(8,128)S(1)} %copy-done.2, f32[16,24,96]{2,1,0:T(8,128)S(1)} %all-to-all-done.3.outs, f32[96,128]{1,0:T(8,128)S(1)} %copy-done.12, ...), custom_call_target="tpu_custom_call" | custom-call | flops 9584640 | bytes 1526400 | tf_op jit(solution)/shard_map/pallas_call | solution.py:65
  133.3 3.2 %collective-permute-start.14 = (f32[128]{0:T(128)S(1)}, f32[128]{0:T(128)S(1)}, u32[]{:S(2)}, u32[]{:S(2)}) collective-permute-start(f32[128]{0:T(128)S(1)} %bitcast_add_fusion.2), channel_id=1, source_target_pairs={{0,1},{1,0},{2,3},{3,2},{4,5},{5,4},{6,7},{7,6},{8,9},{9,8},{10,11... | collective-permute-start | bytes 1544 | tf_op jit(solution)/shard_map/ppermute | solution.py:39
  137.4 16.1 %all_to_all.27 = f32[128,1,128]{2,1,0:T(1,128)S(1)} all-to-all(f32[128,1,128]{2,1,0:T(1,128)S(1)} %broadcast_in_dim.14), channel_id=1, replica_groups=mesh['row_0'=4,'row_1'=4,'row_2'=8,'col'=2] {'row_0','row_1','row_2'}, dimensions={0} | all-to-all | bytes 131072 | tf_op jit(solution)/shard_map/all_to_all | solution.py:55
  (112 shorter events, 31.3 us)
Async XLA Ops:
  0.6 11.3 %copy-start.23 = (f32[544]{0:T(1024)S(1)}, f32[544]{0:T(1024)}, u32[]{:S(2)}) copy-start(f32[544]{0:T(1024)} %param.16) | copy-start | bytes 6532
  0.7 11.4 %copy-start.21 = (s32[8,544]{1,0:T(8,128)S(1)}, s32[8,544]{1,0:T(8,128)}, u32[]{:S(2)}) copy-start(s32[8,544]{1,0:T(8,128)} %param.17) | copy-start | bytes 52228
  7.4 4.8 %collective-permute-start = (f32[544,128]{1,0:T(8,128)S(1)}, f32[544,128]{1,0:T(8,128)}, u32[]{:S(2)}, u32[]{:S(2)}) collective-permute-start(f32[544,128]{1,0:T(8,128)S(1)} %dynamic-slice_bitcast_fusion), channel_id=1, source_target_pairs={{0,1},{1,0},{2,3},{3,2},{4,5},{5,4},{6,7},{7,6},{8,9},{9,8},{10,11... | collective-permute-start | bytes 835592 | tf_op jit(solution)/shard_map/ppermute | solution.py:39
  10.7 9.8 %collective-permute-start.1 = (f32[544,96]{0,1:T(8,128)}, f32[544,96]{0,1:T(8,128)}, u32[]{:S(2)}, u32[]{:S(2)}) collective-permute-start(f32[544,96]{0,1:T(8,128)} %bitcast.9), channel_id=1, source_target_pairs={{2,0},{4,2},{6,4},{8,6},{10,8},{12,10},{14,12},{16,14},{18,16},{20... | collective-permute-start | bytes 626696 | tf_op jit(solution)/shard_map/ppermute | solution.py:35
  21.9 1.7 %collective-permute-start.2 = (f32[56,128]{1,0:T(8,128)S(1)}, f32[56,128]{1,0:T(8,128)S(1)}, u32[]{:S(2)}, u32[]{:S(2)}) collective-permute-start(f32[56,128]{1,0:T(8,128)S(1)} %constant_dynamic-slice_fusion.1), channel_id=1, source_target_pairs={{0,1},{1,0},{2,3},{3,2},{4,5},{5,4},{6,7},{7,6},{8,9},{9,8},{10,11... | collective-permute-start | bytes 86024 | tf_op jit(solution)/shard_map/ppermute | solution.py:39
  41.0 3.1 %collective-permute-start.3 = (f32[8,56,128]{2,1,0:T(8,128)S(1)}, f32[8,56,128]{2,1,0:T(8,128)S(1)}, u32[]{:S(2)}, u32[]{:S(2)}) collective-permute-start(f32[8,56,128]{2,1,0:T(8,128)S(1)} %all_to_all.26.mine), channel_id=1, source_target_pairs={{0,1},{1,0},{2,3},{3,2},{4,5},{5,4},{6,7},{7,6},{8,9},{9,8},{10,11... | collective-permute-start | bytes 688136 | tf_op jit(solution)/shard_map/ppermute | solution.py:39
  42.9 26.8 %copy-start.9 = (f32[9,544]{1,0:T(8,128)}, f32[9,544]{1,0:T(8,128)S(1)}, u32[]{:S(2)}) copy-start(f32[9,544]{1,0:T(8,128)S(1)} %pad_maximum_fusion.source) | copy-start | bytes 58756
  43.0 13.9 %collective-permute-start.5 = (f32[9,544]{1,0:T(8,128)S(1)}, f32[9,544]{1,0:T(8,128)}, u32[]{:S(2)}, u32[]{:S(2)}) collective-permute-start(f32[9,544]{1,0:T(8,128)S(1)} %pad_maximum_fusion.source), channel_id=1, source_target_pairs={{0,1},{1,0},{2,3},{3,2},{4,5},{5,4},{6,7},{7,6},{8,9},{9,8},{10,11... | collective-permute-start | bytes 58760 | tf_op jit(solution)/shard_map/ppermute | solution.py:39
  48.2 18.5 %all-to-all-start.1 = ((f32[16,56,128]{2,1,0:T(8,128)}), f32[16,56,128]{2,1,0:T(8,128)S(1)}, u32[]{:S(2)}, u32[]{:S(2)}) async-start(f32[16,56,128]{2,1,0:T(8,128)} %copy-done.5), calls=%async_computation.1 | async-start | bytes 917504 | tf_op jit(solution)/shard_map/all_to_all | solution.py:210
  57.7 10.9 %collective-permute-start.6 = (f32[544,96]{0,1:T(8,128)}, f32[544,96]{0,1:T(8,128)}, u32[]{:S(2)}, u32[]{:S(2)}) collective-permute-start(f32[544,96]{0,1:T(8,128)} %collective-permute-done.1), channel_id=1, source_target_pairs={{0,1},{1,0},{2,3},{3,2},{4,5},{5,4},{6,7},{7,6},{8,9},{9,8},{10,11... | collective-permute-start | bytes 626696 | tf_op jit(solution)/shard_map/ppermute | solution.py:39
  66.7 5.8 %collective-permute-start.4 = (f32[16,56,128]{2,1,0:T(8,128)S(1)}, f32[16,56,128]{2,1,0:T(8,128)S(1)}, u32[]{:S(2)}, u32[]{:S(2)}) collective-permute-start(f32[16,56,128]{2,1,0:T(8,128)S(1)} %all-to-all-done.1.mine), channel_id=1, source_target_pairs={{0,1},{1,0},{2,3},{3,2},{4,5},{5,4},{6,7},{7,6},{8,9},{9,8},{10,11... | collective-permute-start | bytes 1376264 | tf_op jit(solution)/shard_map/ppermute | solution.py:39
  69.8 11.5 %copy-start.16 = (bf16[3,1,1088,544]{2,3,1,0:T(8,128)(2,1)S(1)}, bf16[3,1,1088,544]{2,3,1,0:T(8,128)(2,1)}, u32[]{:S(2)}) copy-start(bf16[3,1,1088,544]{2,3,1,0:T(8,128)(2,1)} %param.12) | copy-start | bytes 10653700
  77.1 5.9 %collective-permute-start.8 = (f32[9,544]{1,0:T(8,128)}, f32[9,544]{1,0:T(8,128)S(1)}, u32[]{:S(2)}, u32[]{:S(2)}) collective-permute-start(f32[9,544]{1,0:T(8,128)} %shard_map.121), channel_id=1, source_target_pairs={{0,2},{2,4},{4,6},{6,8},{8,10},{10,12},{12,14},{14,16},{16,18},{18... | collective-permute-start | bytes 58760 | tf_op jit(solution)/shard_map/ppermute | solution.py:35
  80.8 3.1 %collective-permute-start.10 = (f32[3,9,96]{2,1,0:T(8,128)S(1)}, f32[3,9,96]{2,1,0:T(8,128)S(1)}, u32[]{:S(2)}, u32[]{:S(2)}) collective-permute-start(f32[3,9,96]{2,1,0:T(8,128)S(1)} %convolution_bitcast_fusion), channel_id=1, source_target_pairs={{0,1},{1,0},{2,3},{3,2},{4,5},{5,4},{6,7},{7,6},{8,9},{9,8},{10,11... | collective-permute-start | bytes 31112 | tf_op jit(solution)/shard_map/ppermute | solution.py:39
  82.7 3.4 %collective-permute-start.7 = (f32[3,9,544]{2,1,0:T(8,128)S(1)}, f32[3,9,544]{2,1,0:T(8,128)S(1)}, u32[]{:S(2)}, u32[]{:S(2)}) collective-permute-start(f32[3,9,544]{2,1,0:T(8,128)S(1)} %dynamic-slice_bitcast_fusion.1), channel_id=1, source_target_pairs={{0,1},{1,0},{2,3},{3,2},{4,5},{5,4},{6,7},{7,6},{8,9},{9,8},{10,11... | collective-permute-start | bytes 176264 | tf_op jit(solution)/shard_map/ppermute | solution.py:39
  83.5 2.2 %collective-permute-start.9 = (f32[3,9,96]{2,1,0:T(8,128)S(1)}, f32[3,9,96]{2,1,0:T(8,128)S(1)}, u32[]{:S(2)}, u32[]{:S(2)}) collective-permute-start(f32[3,9,96]{2,1,0:T(8,128)S(1)} %convolution_bitcast_fusion.1), channel_id=1, source_target_pairs={{0,1},{1,0},{2,3},{3,2},{4,5},{5,4},{6,7},{7,6},{8,9},{9,8},{10,11... | collective-permute-start | bytes 31112 | tf_op jit(solution)/shard_map/ppermute | solution.py:39
  84.2 19.1 %copy-start.20 = (f32[9,544]{1,0:T(8,128)S(1)}, f32[9,544]{1,0:T(8,128)}, u32[]{:S(2)}) copy-start(f32[9,544]{1,0:T(8,128)} %shard_map.121) | copy-start | bytes 58756
  84.3 23.7 %copy-start.15 = (s32[3]{0:T(128)S(1)}, s32[3]{0:T(128)}, u32[]{:S(2)}) copy-start(s32[3]{0:T(128)} %copy-done.13) | copy-start | bytes 40
  84.3 6.8 %collective-permute-start.11 = (f32[3,9,544]{2,1,0:T(8,128)S(1)}, f32[3,9,544]{2,1,0:T(8,128)S(1)}, u32[]{:S(2)}, u32[]{:S(2)}) collective-permute-start(f32[3,9,544]{2,1,0:T(8,128)S(1)} %fusion.11), channel_id=1, source_target_pairs={{2,0},{4,2},{6,4},{8,6},{10,8},{12,10},{14,12},{16,14},{18,16},{20... | collective-permute-start | bytes 176264 | tf_op jit(solution)/shard_map/ppermute | solution.py:35
  91.4 2.5 %collective-permute-start.12 = (f32[24,96]{1,0:T(8,128)S(1)}, f32[24,96]{1,0:T(8,128)S(1)}, u32[]{:S(2)}, u32[]{:S(2)}) collective-permute-start(f32[24,96]{1,0:T(8,128)S(1)} %fusion.26), channel_id=1, source_target_pairs={{0,1},{1,0},{2,3},{3,2},{4,5},{5,4},{6,7},{7,6},{8,9},{9,8},{10,11... | collective-permute-start | bytes 27656 | tf_op jit(solution)/shard_map/ppermute | solution.py:39
  94.6 13.3 %all-to-all-start.2 = ((f32[8,24,96]{2,1,0:T(8,128)}), f32[8,24,96]{2,1,0:T(8,128)}, u32[]{:S(2)}, u32[]{:S(2)}) async-start(f32[8,24,96]{2,1,0:T(8,128)} %broadcast_in_dim.13), calls=%async_computation.2 | async-start | bytes 196608 | tf_op jit(solution)/shard_map/all_to_all | solution.py:55
  102.8 16.4 %collective-permute-start.13 = (f32[24,544]{1,0:T(8,128)}, f32[24,544]{1,0:T(8,128)}, u32[]{:S(2)}, u32[]{:S(2)}) collective-permute-start(f32[24,544]{1,0:T(8,128)} %constant_dynamic-slice_fusion), channel_id=1, source_target_pairs={{0,1},{1,0},{2,3},{3,2},{4,5},{5,4},{6,7},{7,6},{8,9},{9,8},{10,11... | collective-permute-start | bytes 156680 | tf_op jit(solution)/shard_map/ppermute | solution.py:39
  111.8 14.5 %all-to-all-start.3 = ((f32[16,24,96]{2,1,0:T(8,128)}), f32[16,24,96]{2,1,0:T(8,128)S(1)}, u32[]{:S(2)}, u32[]{:S(2)}) async-start(f32[16,24,96]{2,1,0:T(8,128)} %copy-done.8), calls=%async_computation.3 | async-start | bytes 393216 | tf_op jit(solution)/shard_map/all_to_all | solution.py:249
  133.3 4.1 %collective-permute-start.14 = (f32[128]{0:T(128)S(1)}, f32[128]{0:T(128)S(1)}, u32[]{:S(2)}, u32[]{:S(2)}) collective-permute-start(f32[128]{0:T(128)S(1)} %bitcast_add_fusion.2), channel_id=1, source_target_pairs={{0,1},{1,0},{2,3},{3,2},{4,5},{5,4},{6,7},{7,6},{8,9},{9,8},{10,11... | collective-permute-start | bytes 1544 | tf_op jit(solution)/shard_map/ppermute | solution.py:39
  (18 other events, 65.8 us)

commit v3 on v2

--- a/solution.py
+++ b/solution.py
@@ -60,16 +60,17 @@
 VMEM = pl.BlockSpec(memory_space=pltpu.VMEM)
 
 
-def on_core(kernel, outs, scalars, arrays, flops):
-    moved = sum(a.size * a.dtype.itemsize for a in arrays) + sum(4 * o.size for o in outs)
+def on_core(kernel, outs, scalars, arrays, flops, far=(), scratch=(), limit=40):
+    moved = sum(a.size * a.dtype.itemsize for a in [*arrays, *far]) + sum(4 * o.size for o in outs)
     return pl.pallas_call(
         kernel,
         out_shape=outs,
-        in_specs=[SMEM] + [VMEM] * len(arrays),
+        in_specs=[SMEM] + [VMEM] * len(arrays) + [pl.BlockSpec(memory_space=pl.ANY)] * len(far),
         out_specs=[VMEM] * len(outs),
-        compiler_params=pltpu.CompilerParams(vmem_limit_bytes=40 * 1024 * 1024),
+        scratch_shapes=list(scratch),
+        compiler_params=pltpu.CompilerParams(vmem_limit_bytes=limit * 1024 * 1024),
         cost_estimate=pl.CostEstimate(flops=flops, bytes_accessed=moved, transcendentals=0),
-    )(scalars, *arrays)
+    )(scalars, *arrays, *far)
 
 
 def floats(*shape):
@@ -104,22 +105,122 @@
         send[g] = out
 
 
-def plane_back(rmax, where, mine, other, reach, base, wide, solution):
+def in_pieces(x, count):
+    pieces = []
+    for _ in range(count):
+        piece = x.astype(jnp.bfloat16).astype(jnp.float32)
+        pieces.append(piece)
+        x = x - piece
+    return pieces
+
+
+def by_pieces(a, b, count, dims):
+    rows = a.shape[0]
+    stacked = jnp.concatenate(in_pieces(a, count), axis=0).astype(jnp.bfloat16)
+    total = None
+    for k, piece in enumerate(in_pieces(b, count)):
+        product = lax.dot_general(
+            stacked, piece.astype(jnp.bfloat16), (dims, ((), ())), preferred_element_type=jnp.float32
+        )
+        for j in reversed(range(count - k)):
+            term = product[j * rows : (j + 1) * rows]
+            total = term if total is None else total + term
+    return total
+
+
+def exact(a, b):
+    return by_pieces(a, b, 3, ((1,), (0,)))
+
+
+def close_nt(a, b):
+    return by_pieces(a, b, 2, ((1,), (1,)))
+
+
+def left_products(where, inverse, left, mine, other):
+    half = left.shape[1]
+    row = lax.broadcasted_iota(jnp.int32, left.shape, 0)
+    product = dot(jnp.where(row < where[3], left[...], 0.0), inverse[...])
+    first, second = product[:, :half], product[:, half:]
+    mine[...] = jnp.where(where[0] == 0, first, second)
+    other[...] = jnp.where(where[0] == 0, second, first)
+
+
+def coupled(where, right, right_other, source, source_other, moved, moved_other, mine, other):
+    rmax = right.shape[0]
+    half_rows = mine.shape[0]
+    vectors = source.shape[0]
+    top = -(dot_nt(right[...], moved[...]) + dot_nt(right_other[...], moved_other[...]))
+    low = dot_nt(source[...], moved[...]) + dot_nt(source_other[...], moved_other[...])
+    low = jnp.concatenate([low, jnp.zeros((2 * half_rows - rmax - vectors, rmax), jnp.float32)], axis=0)
+    full = jnp.concatenate([top, low], axis=0)
+    full = jnp.concatenate([full, jnp.zeros((2 * half_rows, LANES - rmax), jnp.float32)], axis=1)
+    row = lax.broadcasted_iota(jnp.int32, full.shape, 0)
+    lane = lax.broadcasted_iota(jnp.int32, full.shape, 1)
+    keep = (row == lane) & (row >= rmax) & (row < rmax + vectors)
+    full = full + jnp.where(keep, 0.5, 0.0)
+    first, second = full[:half_rows], full[half_rows:]
+    mine[...] = jnp.where(where[0] == 0, first, second)
+    other[...] = jnp.where(where[0] == 0, second, first)
+
+
+def tile_products(where, inverse, source, source_other, right, right_other, out):
+    half = source.shape[1]
+    blank = jnp.zeros((16 - source.shape[0], half), jnp.float32)
+    mine = jnp.concatenate([source[...], blank, right[...]], axis=0)
+    other = jnp.concatenate([source_other[...], blank, right_other[...]], axis=0)
+    first = jnp.where(where[0] == 0, mine, other)
+    second = jnp.where(where[0] == 0, other, mine)
+    out[...] = dot_nt(first, inverse[:, :half]) + dot_nt(second, inverse[:, half:])
+
+
+def plane_back(
+    rmax, where, mine, other, reach, both, wide_other, ahead_terms, here_terms, left, right, deriv,
+    solution, upper, dense, dense_other, terms, held, arrived,
+):
+    params = left.shape[0]
+    fetch = pltpu.make_async_copy(deriv, held, arrived)
+    fetch.start()
     side, place, group = where[0], where[1], where[2]
     groups, half_rows = mine.shape[0], mine.shape[1]
     count = reach.shape[0]
     rows = 2 * half_rows
-    row = lax.broadcasted_iota(jnp.int32, (rows - rmax, LANES), 0)
-    lane = lax.broadcasted_iota(jnp.int32, (rows - rmax, LANES), 1)
-    state = ((row + rmax == lane) & (row < base.shape[0])).astype(jnp.float32)
+    vectors = solution.shape[0]
+    lines = rows - rmax
+    row = lax.broadcasted_iota(jnp.int32, (lines, LANES), 0)
+    lane = lax.broadcasted_iota(jnp.int32, (lines, LANES), 1)
+    state = ((row + rmax == lane) & (row < vectors)).astype(jnp.float32)
     ahead = state
     for g in reversed(range(1, groups)):
-        state = dot(state[:, :rows], whole_map(side, mine, other, g))
+        state = exact(state[:, :rows], whole_map(side, mine, other, g))
         ahead = jnp.where(group == g - 1, state, ahead)
-    through = dot(ahead[:, :rows], reach[jnp.minimum(place + 1, count - 1)])
-    coeff = jnp.where(place == count - 1, ahead, through)
-    change = dot(coeff[:, :rmax], wide[...])
-    solution[...] = base[...] - change[: base.shape[0]]
+    through = exact(ahead[:, :rows], reach[jnp.minimum(place + 1, count - 1)])
+    coeff = jnp.where(place == count - 1, ahead, through)[:, :rmax]
+    own = exact(ahead[:, :rows], reach[place])[:, :rmax]
+    solved = (both[:lines] - dot(coeff, both[lines:]))[:vectors]
+    solution[...] = jnp.concatenate([solved[vectors - 1 :], solved[: vectors - 1]], axis=0)
+    column = lax.broadcasted_iota(jnp.int32, (lines, rmax), 1)
+    for k in range(left.shape[0]):
+        below = here_terms[k, :lines] - dot(coeff, here_terms[k, lines:])
+        below = jnp.where(column < where[4 + k], below, 0.0)
+        above = ahead_terms[k, :lines] - dot(own, ahead_terms[k, lines:])
+        above = jnp.where(column < where[4 + k], above, 0.0)
+        upper[k] = dot(below, right[k])[:vectors]
+        dense[k] = dot(above, left[k])[:vectors]
+        terms[params + k] = dot_nt(above, here_terms[k, lines:])[: vectors - 1]
+        terms[2 * params + k] = dot_nt(below, ahead_terms[k, lines:])[: vectors - 1]
+    fetch.wait()
+    half = both.shape[1]
+    rounded = jnp.concatenate([solved, jnp.zeros((lines - vectors, half), jnp.float32)], axis=0)
+    rounded = rounded.astype(jnp.bfloat16)
+    wide = both[lines:]
+    for k in range(left.shape[0]):
+        product = jnp.dot(rounded, held[k], preferred_element_type=jnp.float32)
+        first, second = product[:, :half], product[:, half:]
+        here = jnp.where(side == 0, first, second)
+        there = jnp.where(side == 0, second, first)
+        dense[k] += here[:vectors]
+        dense_other[k] = there[:vectors]
+        terms[k] = (dot_nt(here, wide) + dot_nt(there, wide_other[...]))[: vectors - 1]
 
 
 def line_forward(rmax, where, mine, other, offsets, local, send):
@@ -129,10 +230,14 @@
     for k in range(mine.shape[0]):
         chosen = jnp.where(place == k, state, chosen)
         turn = whole_map(side, mine, other, k)[:rmax, :rmax]
-        state = offsets[k] + dot_nt(state, turn)
+        offset = offsets[k, : local.shape[0]]
+        if k + 1 < mine.shape[0]:
+            offset += offsets[k + 1, local.shape[0] :]
+        state = offset + close_nt(state, turn)
     local[...] = chosen
     for g in range(send.shape[0]):
-        send[g] = state
+        send[g, : local.shape[0]] = state
+        send[g, local.shape[0] :] = offsets[0, local.shape[0] :]
 
 
 def plane_forward(
@@ -144,14 +249,15 @@
     behind = state
     for g in range(mine.shape[0] - 1):
         turn = whole_map(side, mine, other, g)[:rmax, :rmax]
-        state = outs[g] + dot_nt(state, turn)
+        offset = outs[g, : local.shape[0]] + outs[g + 1, local.shape[0] :]
+        state = offset + close_nt(state, turn)
         behind = jnp.where(group == g + 1, state, behind)
     entry = local[...] + dot_nt(behind, prefix[:, :rmax])
-    final = plain[...] - dot_nt(entry, moved[:, :rmax])
+    final = plain[...] - dot(entry, moved[...])
     result[...] = final
     each = final.shape[0] // params
     parts = [final[k * each : (k + 1) * each] for k in range(params)]
-    signs = source[1:]
+    signs = source[: source.shape[0] - 1]
     lane = lax.broadcasted_iota(jnp.int32, sums.shape, 1)
     total = jnp.zeros(sums.shape, jnp.float32)
     for k in range(params):
@@ -166,8 +272,8 @@
 def body(
     inv_diag, low_left, low_right, deriv_diag, deriv_left, deriv_right, ranks, whitened, probes
 ):
-    inverse = inv_diag[0]
-    size, half = inverse.shape
+    inverse = jnp.swapaxes(inv_diag[0], 0, 1)
+    half, size = inverse.shape
     rmax = low_left.shape[2]
     count = probes.shape[0]
     params = deriv_left.shape[0]
@@ -176,30 +282,47 @@
     group = lax.axis_index(PLANE)
     in_line = lax.axis_size(LINE)
     groups = lax.axis_size(PLANE)
-    right_next = along_rows(low_right[0], -1)
-    columns = jnp.arange(rmax, dtype=jnp.int32)
-    masks = (columns[None, :] < ranks[:, 0][:, None]).astype(jnp.float32)
-    own_left = jnp.pad(low_left[0] * masks[0][None, :], ((0, 0), (0, LANES - rmax)))
-    where = jnp.stack([side, place, group]).astype(jnp.int32)
-    d_left = deriv_left[:, 0] * masks[1:][:, None, :]
-    d_right = deriv_right[:, 0]
-    source = jnp.concatenate([whitened[None, :], probes.astype(jnp.float32)], axis=0)
+    d_left = jnp.swapaxes(deriv_left[:, 0], 1, 2)
+    d_right = jnp.swapaxes(deriv_right[:, 0], 1, 2)
+    d_diag = jnp.swapaxes(deriv_diag[:, 0], 1, 2)
+    left = jnp.swapaxes(low_left[0], 0, 1)
+    right = jnp.swapaxes(low_right[0], 0, 1)
+    where = jnp.concatenate([jnp.stack([side, place, group]).astype(jnp.int32), ranks[:, 0]])
+    source = jnp.concatenate([probes.astype(jnp.float32), whitened[None, :]], axis=0)
+    lines = -(-(count + 1) // 16) * 16
+    rows = rmax + lines
     source_other = swapped(source)
-    source_full = joined(source, source_other, side, 1)
-    moved = dot(inverse, own_left)
-    moved = part(moved, side, 0) + swapped(part(moved, 1 - side, 0))
-    lines = -(-(count + 1) // 16) * 16
-    blank = jnp.zeros((lines - count - 1, LANES), jnp.float32)
-    keep = jnp.pad(jnp.eye(count + 1, dtype=jnp.float32), ((rmax, lines - count - 1), (rmax, LANES - rmax - count - 1)))
-    own_map = jnp.concatenate([-dot_tn(right_next, moved), dot(source, moved), blank], axis=0)
-    own_map = part(own_map, side, 0) + swapped(part(own_map, 1 - side, 0)) + part(keep, side, 0)
-    right_full = joined(right_next, swapped(right_next), side, 0)
-    base = dot(source_full, inverse)
-    wide = dot_tn(right_full, inverse)
-
-    rows = rmax + lines
+    right_next = along_rows(right, -1)
+    moved, moved_other = on_core(
+        left_products, [floats(rmax, half)] * 2, where, [inverse, left], 2 * size * half * rmax
+    )
+    right_next, moved, moved_other = lax.optimization_barrier((right_next, moved, moved_other))
+    right_other = swapped(right_next)
+    map_mine, map_other = on_core(
+        coupled,
+        [floats(rows // 2, LANES)] * 2,
+        where,
+        [right_next, right_other, source, source_other, moved, moved_other],
+        2 * size * rows * rmax,
+    )
+    own_map = map_mine + swapped(map_other)
+    moved = moved + swapped(moved_other)
+    (both,) = on_core(
+        tile_products,
+        [floats(rmax + lines, half)],
+        where,
+        [inverse, source, source_other, right_next, right_other],
+        2 * (rmax + lines) * size * half,
+    )
     maps = everywhere(own_map, LINE)
+    maps, both = lax.optimization_barrier((maps, both))
     maps_other = swapped(maps)
+    both_before = along_rows(both, 1)
+    both_other = swapped(both[lines:])
+    here_terms = jnp.einsum("mh,krh->kmr", both, d_left, precision=highest)
+    here_terms = here_terms + swapped(here_terms)
+    ahead_terms = jnp.einsum("mh,krh->kmr", both_before, d_right, precision=highest)
+    ahead_terms = ahead_terms + swapped(ahead_terms)
     reach, prefix, send = on_core(
         functools.partial(line_back, rmax),
         [floats(in_line, rows, LANES), floats(rmax, LANES), floats(groups, rows // 2, LANES)],
@@ -208,40 +331,37 @@
         4 * in_line * rows * rmax * rmax,
     )
     totals = lax.all_to_all(send, PLANE, 0, 0, tiled=True)
+    totals, here_terms, ahead_terms, moved, both_other = lax.optimization_barrier(
+        (totals, here_terms, ahead_terms, moved, both_other)
+    )
     totals_other = swapped(totals)
-    (solution,) = on_core(
+    solution, upper_send, dense, dense_other, terms = on_core(
         functools.partial(plane_back, rmax),
-        [floats(count + 1, half)],
-        where,
-        [totals, totals_other, reach, base, wide],
-        2 * lines * rmax * (groups * LANES + half),
-    )
-
-    rounded = solution.astype(jnp.bfloat16)
-    prior = along_rows(solution, 1)
-    upper_part = jnp.einsum("ph,khr->kpr", solution, d_left, precision=high)
-    upper_coeff = upper_part + swapped(upper_part)
-    upper_send = jnp.einsum("kpr,khr->kph", upper_coeff, d_right, precision=high)
+        [floats(count + 1, half)]
+        + [floats(params, count + 1, half)] * 3
+        + [floats(3 * params, count, rmax)],
+        where,
+        [totals, totals_other, reach, both, both_other, ahead_terms, here_terms, d_left, d_right],
+        2 * lines * rmax * (groups * LANES + (2 * params + 1) * half),
+        [d_diag],
+        [pltpu.VMEM(d_diag.shape, d_diag.dtype), pltpu.SemaphoreType.DMA],
+        60,
+    )
     upper = along_rows(upper_send, -1)
-    dense_part = jnp.einsum(
-        "ph,kbh->kpb", rounded, deriv_diag[:, 0], preferred_element_type=jnp.float32
-    )
-    dense = part(dense_part, side, 2) + swapped(part(dense_part, 1 - side, 2))
-    lower_part = jnp.einsum("ph,khr->kpr", prior, d_right, precision=high)
-    lower_coeff = lower_part + swapped(lower_part)
-    lower = jnp.einsum("kpr,khr->kph", lower_coeff, d_left, precision=high)
-    applied = dense + lower + upper
-    drive = applied[:, 1:].reshape(params * count, half)
-    shared = dot_nt(drive, wide, high)
-    shared = shared + swapped(shared)
-    plain = dot_nt(drive, inverse, high)
+    partial = terms[:params]
+    shared = jnp.concatenate([partial + swapped(partial) + terms[params : 2 * params], terms[2 * params :]], axis=0)
+    shared = shared.reshape(2 * params * count, rmax)
+    offsets = everywhere(shared, LINE)
+    dense = dense + swapped(dense_other)
+    applied = dense + upper
+    drive = applied[:, :count].reshape(params * count, half)
+    plain = dot(drive, inverse, high)
     plain = part(plain, side, 1) + swapped(part(plain, 1 - side, 1))
 
-    data_part = jnp.einsum("kh,h->k", applied[:, 0], solution[0], precision=highest)
-    offsets = everywhere(shared, LINE)
+    data_part = jnp.einsum("kh,h->k", applied[:, count], solution[0], precision=highest)
     local, send = on_core(
         functools.partial(line_forward, rmax),
-        [floats(params * count, rmax), floats(groups, params * count, rmax)],
+        [floats(params * count, rmax), floats(groups, 2 * params * count, rmax)],
         where,
         [maps, maps_other, offsets],
         2 * in_line * params * count * rmax * rmax,

time: 156 us -> 144 us (0.923)
  blocking collectives: 33.3 us -> 16.3 us
  Pallas kernels: 13.1 us -> 25.3 us
  matrix products: 17 us -> 6.14 us
  starting transfers between devices: 41.7 us -> 49.2 us
  waiting for transfers between devices: 30.8 us -> 23.9 us
  local copies, waits for them, and re-layouts: 11 us -> 13.4 us
    all_to_all x2 -> x1, blocking collectives: 33.3 us -> 16.3 us  [everywhere(): lax.all_to_all(jnp.broadcast_to(x[None], (count, *x.shape)), axis, 0, 0,...]
    pallas_call x4 -> x7, Pallas kernels: 13.1 us -> 25.3 us  [on_core(): pl.pallas_call(kernel, out_shape=outs, in_specs=[SMEM] + [VMEM] * len(arr...]
    ppermute x3, waiting for transfers between devices: 12 us -> 1.12 us  [along_rows(): return lax.ppermute(block, ROW, route)]
    all_to_all x1 -> x2, starting transfers between devices: 5.78 us -> 13.9 us  [everywhere(): lax.all_to_all(jnp.broadcast_to(x[None], (count, *x.shape)), axis, 0, 0,...]
    all_to_all x1 -> x2, waiting for transfers between devices: 4.45 us -> 12.2 us  [everywhere(): lax.all_to_all(jnp.broadcast_to(x[None], (count, *x.shape)), axis, 0, 0,...]
    dot_general x3 -> x1, matrix products: 7.17 us -> 0.88 us  [dot(): lax.dot_general(a, b, (((1,), (0,)), ((), ())), precision=precision, pref...]
    all_to_all x1, waiting for transfers between devices: 6.11 us -> 0.01 us  [body(): totals = lax.all_to_all(send, PLANE, 0, 0, tiled=True)]
    dot_general x10 -> x3, matrix products: 9.84 us -> 5.26 us  [the longest x1 2.22 us: body(): jnp.einsum('mh,krh->kmr', both_before, d_right, precision=highest)]
  transfers between devices with their start and end apart: 18 -> 20, of which waited for: 8 -> 8; matrix products, arithmetic and copies ran while one was open for 12% -> 9% of each run, Pallas kernels for 3% -> 7%
where the time goes in v3:
time: 144 us; the launch traced here: 143 us
  starting transfers between devices  49.2 us (34%)
  Pallas kernels  25.3 us (18%)
  waiting for transfers between devices  23.9 us (17%)
  blocking collectives  16.3 us (11%)
  local copies, waits for them, and re-layouts  13.4 us (9%)
  other arithmetic  7.3 us (5%)
  matrix products  6.14 us (4%)
    pallas_call x7, Pallas kernels, on_core(): pl.pallas_call(kernel, out_shape=outs, in_specs=[SMEM] + [VMEM] * len(arr...  25.3 us
    all_to_all x1, blocking collectives, everywhere(): lax.all_to_all(jnp.broadcast_to(x[None], (count, *x.shape)), axis, 0, 0,...  16.3 us
    ppermute x13, starting transfers between devices, swapped(): return lax.ppermute(block, 'col', [(0, 1), (1, 0)])  13.9 us
    all_to_all x2, starting transfers between devices, everywhere(): lax.all_to_all(jnp.broadcast_to(x[None], (count, *x.shape)), axis, 0, 0,...  13.9 us
    all_to_all x2, waiting for transfers between devices, everywhere(): lax.all_to_all(jnp.broadcast_to(x[None], (count, *x.shape)), axis, 0, 0,...  12.2 us
    unnamed x50, local copies, waits for them, and re-layouts  10.5 us
    all_to_all x1, starting transfers between devices, body(): totals = lax.all_to_all(send, PLANE, 0, 0, tiled=True)  7.99 us
    all_to_all x1, starting transfers between devices, body(): outs = lax.all_to_all(send, PLANE, 0, 0, tiled=True)  7.72 us
  transfers between devices with their start and end apart: 20, of which 8 were waited for; matrix products, arithmetic and copies ran while one was open for 9% of the time, Pallas kernels for 7%

profile of v3, /device:TPU:1, one launch (start us, length us, event | category | flops | bytes accessed | tf_op | source)
XLA Modules:
  0.0 142.5 jit_solution(6488483389302873583)
XLA Ops:
  2.8 1.7 %copy-done = f32[1,1088,544]{1,2,0:T(8,128)S(1)} copy-done((f32[1,1088,544]{1,2,0:T(8,128)S(1)}, f32[1,1088,544]{1,2,0:T(8,128)}, u32[]{:S(2)}) %copy-start) | copy-done | bytes 2367512
  5.5 2.3 %shard_map.120 = (f32[96,544]{1,0:T(8,128)S(1)}, f32[96,544]{1,0:T(8,128)S(1)}) custom-call(s32[7]{0:T(128)S(1)} %pad_add_fusion.where, f32[544,1088]{1,0:T(8,128)S(1)} %bitcast.55, f32[96,544]{1,0:T(8,128)S(1)} %bitcast.57), custom_call_target="tpu_custom_call" | custom-call | flops 113639424 | bytes 2994176 | tf_op jit(solution)/shard_map/pallas_call | solution.py:65
  8.9 3.4 %collective-permute-start.1 = (f32[96,544]{1,0:T(8,128)S(1)}, f32[96,544]{1,0:T(8,128)S(1)}, u32[]{:S(2)}, u32[]{:S(2)}) collective-permute-start(f32[96,544]{1,0:T(8,128)S(1)} %collective-permute-done.right), channel_id=1, source_target_pairs={{0,1},{1,0},{2,3},{3,2},{4,5},{5,4},{6,7},{7,6},{8,9},{9,8},{10,11... | collective-permute-start | bytes 626696 | tf_op jit(solution)/shard_map/ppermute | solution.py:39
  13.7 1.6 %shard_map.121 = (f32[56,128]{1,0:T(8,128)S(1)}, f32[56,128]{1,0:T(8,128)S(1)}) custom-call(s32[7]{0:T(128)S(1)} %pad_add_fusion.where, f32[96,544]{1,0:T(8,128)S(1)} %collective-permute-done.right, f32[96,544]{1,0:T(8,128)S(1)} %collective-permute-done.1.right_other, f32[9,544]{1,0:T(8,128)S(1)} %pad_maximum_fusion.source, ...), custom_call_target="tpu_custom_call" | custom-call | flops 23396352 | bytes 932096 | tf_op jit(solution)/shard_map/pallas_call | solution.py:65
  17.9 8.7 %all-to-all-start = ((f32[8,56,128]{2,1,0:T(8,128)}), f32[8,56,128]{2,1,0:T(8,128)S(1)}, u32[]{:S(2)}, u32[]{:S(2)}) async-start(f32[8,56,128]{2,1,0:T(8,128)} %broadcast_in_dim.11), calls=%async_computation | async-start | bytes 458752 | tf_op jit(solution)/shard_map/all_to_all | solution.py:55
  27.6 3.5 %shard_map.122.both = f32[112,544]{1,0:T(8,128)S(1)} custom-call(s32[7]{0:T(128)S(1)} %pad_add_fusion.where, f32[544,1088]{1,0:T(8,128)S(1)} %bitcast.56, f32[9,544]{1,0:T(8,128)S(1)} %pad_maximum_fusion.source, f32[9,544]{1,0:T(8,128)S(1)} %collective-permute-done.2.source_other, f32[96,544]{1,0:T(8,128)S(1)} %collective-permute-done.right, ...), custom_call_target="tpu_custom_call" | custom-call | flops 132579328 | bytes 3068160 | tf_op jit(solution)/shard_map/pallas_call | solution.py:65
  31.2 6.1 %all-to-all-done.mine = f32[8,56,128]{2,1,0:T(8,128)S(1)} async-done(((f32[8,56,128]{2,1,0:T(8,128)}), f32[8,56,128]{2,1,0:T(8,128)S(1)}, u32[]{:S(2)}, u32[]{:S(2)}) %all-to-all-start) | async-done | bytes 229408 | tf_op jit(solution)/shard_map/all_to_all | solution.py:55
  37.3 1.5 %collective-permute-start.4 = (f32[8,56,128]{2,1,0:T(8,128)S(1)}, f32[8,56,128]{2,1,0:T(8,128)S(1)}, u32[]{:S(2)}, u32[]{:S(2)}) collective-permute-start(f32[8,56,128]{2,1,0:T(8,128)S(1)} %all-to-all-done.mine), channel_id=1, source_target_pairs={{0,1},{1,0},{2,3},{3,2},{4,5},{5,4},{6,7},{7,6},{8,9},{9,8},{10,11... | collective-permute-start | bytes 688136 | tf_op jit(solution)/shard_map/ppermute | solution.py:39
  38.8 2.9 %collective-permute-start.6 = (f32[112,544]{1,0:T(8,128)S(1)}, f32[112,544]{1,0:T(8,128)}, u32[]{:S(2)}, u32[]{:S(2)}) collective-permute-start(f32[112,544]{1,0:T(8,128)S(1)} %shard_map.122.both), channel_id=1, source_target_pairs={{0,2},{2,4},{4,6},{6,8},{8,10},{10,12},{12,14},{14,16},{16,18},{18... | collective-permute-start | bytes 731144 | tf_op jit(solution)/shard_map/ppermute | solution.py:35
  41.7 2.0 %shard_map.123 = (f32[8,112,128]{2,1,0:T(8,128)S(1)}, f32[96,128]{1,0:T(8,128)S(1)}, f32[16,56,128]{2,1,0:T(8,128)S(1)}) custom-call(s32[7]{0:T(128)S(1)} %pad_add_fusion.where, f32[8,56,128]{2,1,0:T(8,128)S(1)} %all-to-all-done.mine, f32[8,56,128]{2,1,0:T(8,128)S(1)} %collective-permute-done.4.other), custom_call_target="tpu_custom_call" | custom-call | flops 33030144 | bytes 1425408 | tf_op jit(solution)/shard_map/pallas_call | solution.py:65
  46.5 8.0 %all-to-all-start.1 = ((f32[16,56,128]{2,1,0:T(8,128)}), f32[16,56,128]{2,1,0:T(8,128)S(1)}, u32[]{:S(2)}, u32[]{:S(2)}) async-start(f32[16,56,128]{2,1,0:T(8,128)} %copy-done.14), calls=%async_computation.1 | async-start | bytes 917504 | tf_op jit(solution)/shard_map/all_to_all | solution.py:333
  54.5 2.2 %convolution_bitcast_fusion.1 = f32[3,112,96]{2,1,0:T(8,128)S(1)} fusion(f32[112,544]{1,0:T(8,128)S(1)} %shard_map.122.both, f32[3,1,544,96]{2,3,1,0:T(8,128)} %param.13), kind=kOutput, calls=%fused_computation.3 | convolution fusion | flops 210567168 | bytes 999424 | tf_op jit(solution)/shard_map/mh,krh->kmr/dot_general | solution.py:322
  58.2 2.2 %convolution_bitcast_fusion = f32[3,112,96]{2,1,0:T(8,128)S(1)} fusion(f32[112,544]{1,0:T(8,128)} %collective-permute-done.6, f32[3,1,544,96]{2,3,1,0:T(8,128)} %param.14), kind=kOutput, calls=%fused_computation.2 | convolution fusion | flops 210567168 | bytes 999424 | tf_op jit(solution)/shard_map/mh,krh->kmr/dot_general | solution.py:324
  60.7 1.7 %add.48.moved = f32[96,544]{1,0:T(8,128)} add(f32[96,544]{1,0:T(8,128)S(1)} %copy-done.9, f32[96,544]{1,0:T(8,128)} %collective-permute-done.8) | non-fusion elementwise | flops 52224 | bytes 626688 | tf_op jit(solution)/shard_map/add | solution.py:309
  63.8 2.5 %collective-permute-start.10 = (f32[16,56,128]{2,1,0:T(8,128)S(1)}, f32[16,56,128]{2,1,0:T(8,128)S(1)}, u32[]{:S(2)}, u32[]{:S(2)}) collective-permute-start(f32[16,56,128]{2,1,0:T(8,128)S(1)} %all-to-all-done.1.mine), channel_id=1, source_target_pairs={{0,1},{1,0},{2,3},{3,2},{4,5},{5,4},{6,7},{7,6},{8,9},{9,8},{10,11... | collective-permute-start | bytes 1376264 | tf_op jit(solution)/shard_map/ppermute | solution.py:39
  68.5 9.6 %shard_map.124 = (f32[9,544]{1,0:T(8,128)}, f32[3,9,544]{2,1,0:T(8,128)}, f32[3,9,544]{2,1,0:T(8,128)}, f32[3,9,544]{2,1,0:T(8,128)}, f32[9,8,96]{2,1,0:T(8,128)}) custom-call(s32[7]{0:T(128)} %copy-done.20, f32[16,56,128]{2,1,0:T(8,128)} %copy-done.3, f32[16,56,128]{2,1,0:T(8,128)} %copy-done.5, f32[8,112,128]{2,1,0:T(8,128)} %copy-done.15, ...), custom_call_target="tpu_custom_call" | custom-call | flops 17989632 | bytes 7115008 | tf_op jit(solution)/shard_map/pallas_call | solution.py:65
  82.1 5.2 %all-to-all-start.2 = ((f32[8,48,96]{2,1,0:T(8,128)}), f32[8,48,96]{2,1,0:T(8,128)}, u32[]{:S(2)}, u32[]{:S(2)}) async-start(f32[8,48,96]{2,1,0:T(8,128)} %broadcast_in_dim.25), calls=%async_computation.2 | async-start | bytes 393216 | tf_op jit(solution)/shard_map/all_to_all | solution.py:55
  90.8 6.0 %all-to-all-done.2.offsets = f32[8,48,96]{2,1,0:T(8,128)} async-done(((f32[8,48,96]{2,1,0:T(8,128)}), f32[8,48,96]{2,1,0:T(8,128)}, u32[]{:S(2)}, u32[]{:S(2)}) %all-to-all-start.2) | async-done | bytes 147488 | tf_op jit(solution)/shard_map/all_to_all | solution.py:55
  97.8 2.7 %shard_map.125 = (f32[24,96]{1,0:T(8,128)S(1)}, f32[16,48,96]{2,1,0:T(8,128)}) custom-call(s32[7]{0:T(128)S(1)} %copy-done.21, f32[8,56,128]{2,1,0:T(8,128)S(1)} %all-to-all-done.mine, f32[8,56,128]{2,1,0:T(8,128)S(1)} %copy-done.13, f32[8,48,96]{2,1,0:T(8,128)} %all-to-all-done.2.offsets), custom_call_target="tpu_custom_call" | custom-call | flops 3538944 | bytes 910336 | tf_op jit(solution)/shard_map/pallas_call | solution.py:65
  100.5 7.7 %all-to-all-start.3 = ((f32[16,48,96]{2,1,0:T(8,128)}), f32[16,48,96]{2,1,0:T(8,128)S(1)}, u32[]{:S(2)}, u32[]{:S(2)}) async-start(f32[16,48,96]{2,1,0:T(8,128)} %get-tuple-element.47), calls=%async_computation.3 | async-start | bytes 786432 | tf_op jit(solution)/shard_map/all_to_all | solution.py:369
  110.1 6.2 %all-to-all-done.3.outs = f32[16,48,96]{2,1,0:T(8,128)S(1)} async-done(((f32[16,48,96]{2,1,0:T(8,128)}), f32[16,48,96]{2,1,0:T(8,128)S(1)}, u32[]{:S(2)}, u32[]{:S(2)}) %all-to-all-start.3) | async-done | bytes 294944 | tf_op jit(solution)/shard_map/all_to_all | solution.py:369
  117.2 3.5 %shard_map.126 = (f32[24,544]{1,0:T(8,128)}, f32[1,128]{1,0:T(1,128)S(1)}) custom-call(s32[7]{0:T(128)S(1)} %copy-done.21, f32[16,56,128]{2,1,0:T(8,128)S(1)} %copy-done.4, f32[16,56,128]{2,1,0:T(8,128)S(1)} %copy-done.6, f32[16,48,96]{2,1,0:T(8,128)S(1)} %all-to-all-done.3.outs, f32[96,128]{1,0:T(8,128)S(1)} %copy-done.19, ...), custom_call_target="tpu_custom_call" | custom-call | flops 9584640 | bytes 1604224 | tf_op jit(solution)/shard_map/pallas_call | solution.py:65
  120.8 3.3 %collective-permute-start.15 = (f32[128]{0:T(128)S(1)}, f32[128]{0:T(128)S(1)}, u32[]{:S(2)}, u32[]{:S(2)}) collective-permute-start(f32[128]{0:T(128)S(1)} %bitcast_add_fusion), channel_id=1, source_target_pairs={{0,1},{1,0},{2,3},{3,2},{4,5},{5,4},{6,7},{7,6},{8,9},{9,8},{10,11... | collective-permute-start | bytes 1544 | tf_op jit(solution)/shard_map/ppermute | solution.py:39
  125.0 16.3 %all_to_all.26 = f32[128,1,128]{2,1,0:T(1,128)S(1)} all-to-all(f32[128,1,128]{2,1,0:T(1,128)S(1)} %broadcast_in_dim.26), channel_id=1, replica_groups=mesh['row_0'=4,'row_1'=4,'row_2'=8,'col'=2] {'row_0','row_1','row_2'}, dimensions={0} | all-to-all | bytes 131072 | tf_op jit(solution)/shard_map/all_to_all | solution.py:55
  (103 shorter events, 30.7 us)
Async XLA Ops:
  0.7 8.3 %collective-permute-start = (f32[96,544]{1,0:T(8,128)}, f32[96,544]{1,0:T(8,128)S(1)}, u32[]{:S(2)}, u32[]{:S(2)}) collective-permute-start(f32[96,544]{1,0:T(8,128)} %bitcast.63), channel_id=1, source_target_pairs={{2,0},{4,2},{6,4},{8,6},{10,8},{12,10},{14,12},{16,14},{18,16},{20... | collective-permute-start | bytes 626696 | tf_op jit(solution)/shard_map/ppermute | solution.py:35
  2.8 38.9 %copy-start.20 = (s32[7]{0:T(128)}, s32[7]{0:T(128)S(1)}, u32[]{:S(2)}) copy-start(s32[7]{0:T(128)S(1)} %pad_add_fusion.where) | copy-start | bytes 88
  8.9 4.7 %collective-permute-start.1 = (f32[96,544]{1,0:T(8,128)S(1)}, f32[96,544]{1,0:T(8,128)S(1)}, u32[]{:S(2)}, u32[]{:S(2)}) collective-permute-start(f32[96,544]{1,0:T(8,128)S(1)} %collective-permute-done.right), channel_id=1, source_target_pairs={{0,1},{1,0},{2,3},{3,2},{4,5},{5,4},{6,7},{7,6},{8,9},{9,8},{10,11... | collective-permute-start | bytes 626696 | tf_op jit(solution)/shard_map/ppermute | solution.py:39
  12.4 1.3 collective-permute-start.2
  16.0 1.2 collective-permute-start.3
  17.9 19.4 %all-to-all-start = ((f32[8,56,128]{2,1,0:T(8,128)}), f32[8,56,128]{2,1,0:T(8,128)S(1)}, u32[]{:S(2)}, u32[]{:S(2)}) async-start(f32[8,56,128]{2,1,0:T(8,128)} %broadcast_in_dim.11), calls=%async_computation | async-start | bytes 458752 | tf_op jit(solution)/shard_map/all_to_all | solution.py:55
  31.2 31.9 %copy-start.2 = (f32[112,544]{1,0:T(8,128)}, f32[112,544]{1,0:T(8,128)S(1)}, u32[]{:S(2)}) copy-start(f32[112,544]{1,0:T(8,128)S(1)} %shard_map.122.both) | copy-start | bytes 731140
  37.3 4.4 %collective-permute-start.4 = (f32[8,56,128]{2,1,0:T(8,128)S(1)}, f32[8,56,128]{2,1,0:T(8,128)S(1)}, u32[]{:S(2)}, u32[]{:S(2)}) collective-permute-start(f32[8,56,128]{2,1,0:T(8,128)S(1)} %all-to-all-done.mine), channel_id=1, source_target_pairs={{0,1},{1,0},{2,3},{3,2},{4,5},{5,4},{6,7},{7,6},{8,9},{9,8},{10,11... | collective-permute-start | bytes 688136 | tf_op jit(solution)/shard_map/ppermute | solution.py:39
  38.8 21.9 %collective-permute-start.8 = (f32[96,544]{1,0:T(8,128)}, f32[96,544]{1,0:T(8,128)}, u32[]{:S(2)}, u32[]{:S(2)}) collective-permute-start(f32[96,544]{1,0:T(8,128)} %copy-done.17), channel_id=1, source_target_pairs={{0,1},{1,0},{2,3},{3,2},{4,5},{5,4},{6,7},{7,6},{8,9},{9,8},{10,11... | collective-permute-start | bytes 626696 | tf_op jit(solution)/shard_map/ppermute | solution.py:39
  38.8 19.4 %collective-permute-start.6 = (f32[112,544]{1,0:T(8,128)S(1)}, f32[112,544]{1,0:T(8,128)}, u32[]{:S(2)}, u32[]{:S(2)}) collective-permute-start(f32[112,544]{1,0:T(8,128)S(1)} %shard_map.122.both), channel_id=1, source_target_pairs={{0,2},{2,4},{4,6},{6,8},{8,10},{10,12},{12,14},{14,16},{16,18},{18... | collective-permute-start | bytes 731144 | tf_op jit(solution)/shard_map/ppermute | solution.py:35
  46.5 17.3 %all-to-all-start.1 = ((f32[16,56,128]{2,1,0:T(8,128)}), f32[16,56,128]{2,1,0:T(8,128)S(1)}, u32[]{:S(2)}, u32[]{:S(2)}) async-start(f32[16,56,128]{2,1,0:T(8,128)} %copy-done.14), calls=%async_computation.1 | async-start | bytes 917504 | tf_op jit(solution)/shard_map/all_to_all | solution.py:333
  56.7 5.6 %collective-permute-start.5 = (f32[3,112,96]{2,1,0:T(8,128)S(1)}, f32[3,112,96]{2,1,0:T(8,128)S(1)}, u32[]{:S(2)}, u32[]{:S(2)}) collective-permute-start(f32[3,112,96]{2,1,0:T(8,128)S(1)} %convolution_bitcast_fusion.1), channel_id=1, source_target_pairs={{0,1},{1,0},{2,3},{3,2},{4,5},{5,4},{6,7},{7,6},{8,9},{9,8},{10,11... | collective-permute-start | bytes 387080 | tf_op jit(solution)/shard_map/ppermute | solution.py:39
  57.9 5.9 %collective-permute-start.9 = (f32[96,544]{1,0:T(8,128)S(1)}, f32[96,544]{1,0:T(8,128)}, u32[]{:S(2)}, u32[]{:S(2)}) collective-permute-start(f32[96,544]{1,0:T(8,128)S(1)} %slice.30), channel_id=1, source_target_pairs={{0,1},{1,0},{2,3},{3,2},{4,5},{5,4},{6,7},{7,6},{8,9},{9,8},{10,11... | collective-permute-start | bytes 626696 | tf_op jit(solution)/shard_map/ppermute | solution.py:39
  60.4 2.7 %collective-permute-start.7 = (f32[3,112,96]{2,1,0:T(8,128)S(1)}, f32[3,112,96]{2,1,0:T(8,128)S(1)}, u32[]{:S(2)}, u32[]{:S(2)}) collective-permute-start(f32[3,112,96]{2,1,0:T(8,128)S(1)} %convolution_bitcast_fusion), channel_id=1, source_target_pairs={{0,1},{1,0},{2,3},{3,2},{4,5},{5,4},{6,7},{7,6},{8,9},{9,8},{10,11... | collective-permute-start | bytes 387080 | tf_op jit(solution)/shard_map/ppermute | solution.py:39
  63.8 3.9 %collective-permute-start.10 = (f32[16,56,128]{2,1,0:T(8,128)S(1)}, f32[16,56,128]{2,1,0:T(8,128)S(1)}, u32[]{:S(2)}, u32[]{:S(2)}) collective-permute-start(f32[16,56,128]{2,1,0:T(8,128)S(1)} %all-to-all-done.1.mine), channel_id=1, source_target_pairs={{0,1},{1,0},{2,3},{3,2},{4,5},{5,4},{6,7},{7,6},{8,9},{9,8},{10,11... | collective-permute-start | bytes 1376264 | tf_op jit(solution)/shard_map/ppermute | solution.py:39
  78.9 1.8 %collective-permute-start.11 = (f32[3,8,96]{2,1,0:T(8,128)S(1)}, f32[3,8,96]{2,1,0:T(8,128)S(1)}, u32[]{:S(2)}, u32[]{:S(2)}) collective-permute-start(f32[3,8,96]{2,1,0:T(8,128)S(1)} %slice.31), channel_id=1, source_target_pairs={{0,1},{1,0},{2,3},{3,2},{4,5},{5,4},{6,7},{7,6},{8,9},{9,8},{10,11... | collective-permute-start | bytes 27656 | tf_op jit(solution)/shard_map/ppermute | solution.py:39
  79.2 8.1 %collective-permute-start.12 = (f32[3,9,544]{2,1,0:T(8,128)}, f32[3,9,544]{2,1,0:T(8,128)}, u32[]{:S(2)}, u32[]{:S(2)}) collective-permute-start(f32[3,9,544]{2,1,0:T(8,128)} %get-tuple-element.51), channel_id=1, source_target_pairs={{0,1},{1,0},{2,3},{3,2},{4,5},{5,4},{6,7},{7,6},{8,9},{9,8},{10,11... | collective-permute-start | bytes 176264 | tf_op jit(solution)/shard_map/ppermute | solution.py:39
  79.4 8.0 %collective-permute-start.13 = (f32[3,9,544]{2,1,0:T(8,128)}, f32[3,9,544]{2,1,0:T(8,128)}, u32[]{:S(2)}, u32[]{:S(2)}) collective-permute-start(f32[3,9,544]{2,1,0:T(8,128)} %get-tuple-element.52), channel_id=1, source_target_pairs={{2,0},{4,2},{6,4},{8,6},{10,8},{12,10},{14,12},{16,14},{18,16},{20... | collective-permute-start | bytes 176264 | tf_op jit(solution)/shard_map/ppermute | solution.py:35
  82.1 14.7 %all-to-all-start.2 = ((f32[8,48,96]{2,1,0:T(8,128)}), f32[8,48,96]{2,1,0:T(8,128)}, u32[]{:S(2)}, u32[]{:S(2)}) async-start(f32[8,48,96]{2,1,0:T(8,128)} %broadcast_in_dim.25), calls=%async_computation.2 | async-start | bytes 393216 | tf_op jit(solution)/shard_map/all_to_all | solution.py:55
  87.3 28.9 %copy-start.4 = (f32[16,56,128]{2,1,0:T(8,128)S(1)}, f32[16,56,128]{2,1,0:T(8,128)}, u32[]{:S(2)}) copy-start(f32[16,56,128]{2,1,0:T(8,128)} %copy-done.3) | copy-start | bytes 1376260
  87.3 28.9 %copy-start.7 = (f32[96,544]{1,0:T(8,128)S(1)}, f32[96,544]{1,0:T(8,128)}, u32[]{:S(2)}) copy-start(f32[96,544]{1,0:T(8,128)} %add.48.moved) | copy-start | bytes 626692
  90.1 19.0 %collective-permute-start.14 = (f32[24,544]{1,0:T(8,128)S(1)}, f32[24,544]{1,0:T(8,128)S(1)}, u32[]{:S(2)}, u32[]{:S(2)}) collective-permute-start(f32[24,544]{1,0:T(8,128)S(1)} %constant_dynamic-slice_fusion), channel_id=1, source_target_pairs={{0,1},{1,0},{2,3},{3,2},{4,5},{5,4},{6,7},{7,6},{8,9},{9,8},{10,11... | collective-permute-start | bytes 156680 | tf_op jit(solution)/shard_map/ppermute | solution.py:39
  100.5 15.7 %all-to-all-start.3 = ((f32[16,48,96]{2,1,0:T(8,128)}), f32[16,48,96]{2,1,0:T(8,128)S(1)}, u32[]{:S(2)}, u32[]{:S(2)}) async-start(f32[16,48,96]{2,1,0:T(8,128)} %get-tuple-element.47), calls=%async_computation.3 | async-start | bytes 786432 | tf_op jit(solution)/shard_map/all_to_all | solution.py:369
  120.8 4.1 %collective-permute-start.15 = (f32[128]{0:T(128)S(1)}, f32[128]{0:T(128)S(1)}, u32[]{:S(2)}, u32[]{:S(2)}) collective-permute-start(f32[128]{0:T(128)S(1)} %bitcast_add_fusion), channel_id=1, source_target_pairs={{0,1},{1,0},{2,3},{3,2},{4,5},{5,4},{6,7},{7,6},{8,9},{9,8},{10,11... | collective-permute-start | bytes 1544 | tf_op jit(solution)/shard_map/ppermute | solution.py:39
  (21 other events, 122.7 us)

commit v4 on v3

--- a/solution.py
+++ b/solution.py
@@ -130,6 +130,10 @@
 
 def exact(a, b):
     return by_pieces(a, b, 3, ((1,), (0,)))
+
+
+def close(a, b):
+    return by_pieces(a, b, 2, ((1,), (0,)))
 
 
 def close_nt(a, b):
@@ -200,14 +204,14 @@
     solution[...] = jnp.concatenate([solved[vectors - 1 :], solved[: vectors - 1]], axis=0)
     column = lax.broadcasted_iota(jnp.int32, (lines, rmax), 1)
     for k in range(left.shape[0]):
-        below = here_terms[k, :lines] - dot(coeff, here_terms[k, lines:])
+        below = here_terms[k, :lines] - close(coeff, here_terms[k, lines:])
         below = jnp.where(column < where[4 + k], below, 0.0)
-        above = ahead_terms[k, :lines] - dot(own, ahead_terms[k, lines:])
+        above = ahead_terms[k, :lines] - close(own, ahead_terms[k, lines:])
         above = jnp.where(column < where[4 + k], above, 0.0)
-        upper[k] = dot(below, right[k])[:vectors]
-        dense[k] = dot(above, left[k])[:vectors]
-        terms[params + k] = dot_nt(above, here_terms[k, lines:])[: vectors - 1]
-        terms[2 * params + k] = dot_nt(below, ahead_terms[k, lines:])[: vectors - 1]
+        upper[k] = close(below, right[k])[:vectors]
+        dense[k] = close(above, left[k])[:vectors]
+        terms[params + k] = close_nt(above, here_terms[k, lines:])[: vectors - 1]
+        terms[2 * params + k] = close_nt(below, ahead_terms[k, lines:])[: vectors - 1]
     fetch.wait()
     half = both.shape[1]
     rounded = jnp.concatenate([solved, jnp.zeros((lines - vectors, half), jnp.float32)], axis=0)
@@ -220,7 +224,7 @@
         there = jnp.where(side == 0, second, first)
         dense[k] += here[:vectors]
         dense_other[k] = there[:vectors]
-        terms[k] = (dot_nt(here, wide) + dot_nt(there, wide_other[...]))[: vectors - 1]
+        terms[k] = (close_nt(here, wide) + close_nt(there, wide_other[...]))[: vectors - 1]
 
 
 def line_forward(rmax, where, mine, other, offsets, local, send):
@@ -252,8 +256,8 @@
         offset = outs[g, : local.shape[0]] + outs[g + 1, local.shape[0] :]
         state = offset + close_nt(state, turn)
         behind = jnp.where(group == g + 1, state, behind)
-    entry = local[...] + dot_nt(behind, prefix[:, :rmax])
-    final = plain[...] - dot(entry, moved[...])
+    entry = local[...] + close_nt(behind, prefix[:, :rmax])
+    final = plain[...] - close(entry, moved[...])
     result[...] = final
     each = final.shape[0] // params
     parts = [final[k * each : (k + 1) * each] for k in range(params)]
@@ -315,13 +319,13 @@
         2 * (rmax + lines) * size * half,
     )
     maps = everywhere(own_map, LINE)
-    maps, both = lax.optimization_barrier((maps, both))
+    here_terms = jnp.einsum("mh,krh->kmr", both, d_left, precision=high)
+    maps, both, here_terms = lax.optimization_barrier((maps, both, here_terms))
     maps_other = swapped(maps)
     both_before = along_rows(both, 1)
     both_other = swapped(both[lines:])
-    here_terms = jnp.einsum("mh,krh->kmr", both, d_left, precision=highest)
     here_terms = here_terms + swapped(here_terms)
-    ahead_terms = jnp.einsum("mh,krh->kmr", both_before, d_right, precision=highest)
+    ahead_terms = jnp.einsum("mh,krh->kmr", both_before, d_right, precision=high)
     ahead_terms = ahead_terms + swapped(ahead_terms)
     reach, prefix, send = on_core(
         functools.partial(line_back, rmax),
@@ -329,6 +333,7 @@
         where,
         [maps, maps_other],
         4 * in_line * rows * rmax * rmax,
+        limit=60,
     )
     totals = lax.all_to_all(send, PLANE, 0, 0, tiled=True)
     totals, here_terms, ahead_terms, moved, both_other = lax.optimization_barrier(
@@ -348,8 +353,8 @@
         60,
     )
     upper = along_rows(upper_send, -1)
-    partial = terms[:params]
-    shared = jnp.concatenate([partial + swapped(partial) + terms[params : 2 * params], terms[2 * params :]], axis=0)
+    partial = terms[:params] + swapped(terms)[:params]
+    shared = jnp.concatenate([partial + terms[params : 2 * params], terms[2 * params :]], axis=0)
     shared = shared.reshape(2 * params * count, rmax)
     offsets = everywhere(shared, LINE)
     dense = dense + swapped(dense_other)

time: 144 us -> 139 us (0.965)
  local copies, waits for them, and re-layouts: 13.4 us -> 11.6 us
  starting transfers between devices: 49.2 us -> 47.5 us
  waiting for transfers between devices: 23.9 us -> 25.6 us
    all_to_all x1, waiting for transfers between devices: 0.01 us -> 4.08 us  [body(): totals = lax.all_to_all(send, PLANE, 0, 0, tiled=True)]
    all_to_all x2, waiting for transfers between devices: 12.2 us -> 9.76 us  [everywhere(): lax.all_to_all(jnp.broadcast_to(x[None], (count, *x.shape)), axis, 0, 0,...]
    unnamed x50 -> x52, local copies, waits for them, and re-layouts: 10.5 us -> 9.37 us
  transfers between devices with their start and end apart: 20 -> 20, of which waited for: 8 -> 9; matrix products, arithmetic and copies ran while one was open for 9% -> 8% of each run, Pallas kernels for 7% -> 9%
where the time goes in v4:
time: 139 us; the launch traced here: 138 us
  starting transfers between devices  47.5 us (34%)
  waiting for transfers between devices  25.6 us (18%)
  Pallas kernels  24.8 us (18%)
  blocking collectives  16.3 us (12%)
  local copies, waits for them, and re-layouts  11.6 us (8%)
  other arithmetic  6.59 us (5%)
  matrix products  4.74 us (3%)
    pallas_call x7, Pallas kernels, on_core(): pl.pallas_call(kernel, out_shape=outs, in_specs=[SMEM] + [VMEM] * len(arr...  24.8 us
    all_to_all x1, blocking collectives, everywhere(): lax.all_to_all(jnp.broadcast_to(x[None], (count, *x.shape)), axis, 0, 0,...  16.3 us
    all_to_all x2, starting transfers between devices, everywhere(): lax.all_to_all(jnp.broadcast_to(x[None], (count, *x.shape)), axis, 0, 0,...  13.9 us
    ppermute x13, starting transfers between devices, swapped(): return lax.ppermute(block, 'col', [(0, 1), (1, 0)])  13.5 us
    all_to_all x2, waiting for transfers between devices, everywhere(): lax.all_to_all(jnp.broadcast_to(x[None], (count, *x.shape)), axis, 0, 0,...  9.76 us
    unnamed x52, local copies, waits for them, and re-layouts  9.37 us
    all_to_all x1, starting transfers between devices, body(): totals = lax.all_to_all(send, PLANE, 0, 0, tiled=True)  7.98 us
    all_to_all x1, starting transfers between devices, body(): outs = lax.all_to_all(send, PLANE, 0, 0, tiled=True)  6.51 us
  transfers between devices with their start and end apart: 20, of which 9 were waited for; matrix products, arithmetic and copies ran while one was open for 8% of the time, Pallas kernels for 9%

profile of v4, /device:TPU:1, one launch (start us, length us, event | category | flops | bytes accessed | tf_op | source)
XLA Modules:
  0.0 138.1 jit_solution(3707730030498005027)
XLA Ops:
  2.8 1.7 %copy-done = f32[1,1088,544]{1,2,0:T(8,128)S(1)} copy-done((f32[1,1088,544]{1,2,0:T(8,128)S(1)}, f32[1,1088,544]{1,2,0:T(8,128)}, u32[]{:S(2)}) %copy-start) | copy-done | bytes 2367512
  5.5 2.3 %shard_map.120 = (f32[96,544]{1,0:T(8,128)S(1)}, f32[96,544]{1,0:T(8,128)S(1)}) custom-call(s32[7]{0:T(128)S(1)} %pad_add_fusion.where, f32[544,1088]{1,0:T(8,128)S(1)} %bitcast.55, f32[96,544]{1,0:T(8,128)S(1)} %bitcast.57), custom_call_target="tpu_custom_call" | custom-call | flops 113639424 | bytes 2994176 | tf_op jit(solution)/shard_map/pallas_call | solution.py:65
  8.9 3.4 %collective-permute-start.1 = (f32[96,544]{1,0:T(8,128)S(1)}, f32[96,544]{1,0:T(8,128)S(1)}, u32[]{:S(2)}, u32[]{:S(2)}) collective-permute-start(f32[96,544]{1,0:T(8,128)S(1)} %collective-permute-done.right), channel_id=1, source_target_pairs={{0,1},{1,0},{2,3},{3,2},{4,5},{5,4},{6,7},{7,6},{8,9},{9,8},{10,11... | collective-permute-start | bytes 626696 | tf_op jit(solution)/shard_map/ppermute | solution.py:39
  13.7 1.6 %shard_map.121 = (f32[56,128]{1,0:T(8,128)S(1)}, f32[56,128]{1,0:T(8,128)S(1)}) custom-call(s32[7]{0:T(128)S(1)} %pad_add_fusion.where, f32[96,544]{1,0:T(8,128)S(1)} %collective-permute-done.right, f32[96,544]{1,0:T(8,128)S(1)} %collective-permute-done.1.right_other, f32[9,544]{1,0:T(8,128)S(1)} %pad_maximum_fusion.source, ...), custom_call_target="tpu_custom_call" | custom-call | flops 23396352 | bytes 932096 | tf_op jit(solution)/shard_map/pallas_call | solution.py:65
  18.0 8.7 %all-to-all-start = ((f32[8,56,128]{2,1,0:T(8,128)}), f32[8,56,128]{2,1,0:T(8,128)S(1)}, u32[]{:S(2)}, u32[]{:S(2)}) async-start(f32[8,56,128]{2,1,0:T(8,128)} %broadcast_in_dim.11), calls=%async_computation | async-start | bytes 458752 | tf_op jit(solution)/shard_map/all_to_all | solution.py:55
  28.6 3.5 %shard_map.122.both = f32[112,544]{1,0:T(8,128)S(1)} custom-call(s32[7]{0:T(128)S(1)} %pad_add_fusion.where, f32[544,1088]{1,0:T(8,128)S(1)} %bitcast.56, f32[9,544]{1,0:T(8,128)S(1)} %pad_maximum_fusion.source, f32[9,544]{1,0:T(8,128)S(1)} %collective-permute-done.2.source_other, f32[96,544]{1,0:T(8,128)S(1)} %copy-done.11, f32[96,544]{1,0:T(8,128)S(1)} %copy-done.13), custom_call_target="tpu_custom_call" | custom-call | flops 132579328 | bytes 3068160 | tf_op jit(solution)/shard_map/pallas_call | solution.py:65
  33.4 3.9 %all-to-all-done.mine = f32[8,56,128]{2,1,0:T(8,128)S(1)} async-done(((f32[8,56,128]{2,1,0:T(8,128)}), f32[8,56,128]{2,1,0:T(8,128)S(1)}, u32[]{:S(2)}, u32[]{:S(2)}) %all-to-all-start) | async-done | bytes 229408 | tf_op jit(solution)/shard_map/all_to_all | solution.py:55
  37.3 1.5 %collective-permute-start.4 = (f32[8,56,128]{2,1,0:T(8,128)S(1)}, f32[8,56,128]{2,1,0:T(8,128)S(1)}, u32[]{:S(2)}, u32[]{:S(2)}) collective-permute-start(f32[8,56,128]{2,1,0:T(8,128)S(1)} %all-to-all-done.mine), channel_id=1, source_target_pairs={{0,1},{1,0},{2,3},{3,2},{4,5},{5,4},{6,7},{7,6},{8,9},{9,8},{10,11... | collective-permute-start | bytes 688136 | tf_op jit(solution)/shard_map/ppermute | solution.py:39
  38.8 2.9 %collective-permute-start.6 = (f32[112,544]{1,0:T(8,128)S(1)}, f32[112,544]{1,0:T(8,128)}, u32[]{:S(2)}, u32[]{:S(2)}) collective-permute-start(f32[112,544]{1,0:T(8,128)S(1)} %shard_map.122.both), channel_id=1, source_target_pairs={{0,2},{2,4},{4,6},{6,8},{8,10},{10,12},{12,14},{14,16},{16,18},{18... | collective-permute-start | bytes 731144 | tf_op jit(solution)/shard_map/ppermute | solution.py:35
  42.4 3.4 %shard_map.123 = (f32[8,112,128]{2,1,0:T(8,128)}, f32[96,128]{1,0:T(8,128)}, f32[16,56,128]{2,1,0:T(8,128)}) custom-call(s32[7]{0:T(128)} %copy-done.19, f32[8,56,128]{2,1,0:T(8,128)} %copy-done.5, f32[8,56,128]{2,1,0:T(8,128)} %copy-done.14), custom_call_target="tpu_custom_call" | custom-call | flops 33030144 | bytes 1425408 | tf_op jit(solution)/shard_map/pallas_call | solution.py:65
  45.8 8.0 %all-to-all-start.1 = ((f32[16,56,128]{2,1,0:T(8,128)}), f32[16,56,128]{2,1,0:T(8,128)S(1)}, u32[]{:S(2)}, u32[]{:S(2)}) async-start(f32[16,56,128]{2,1,0:T(8,128)} %get-tuple-element.39), calls=%async_computation.1 | async-start | bytes 917504 | tf_op jit(solution)/shard_map/all_to_all | solution.py:338
  55.1 1.8 %convolution_bitcast_fusion = f32[3,112,96]{2,1,0:T(8,128)S(1)} fusion(f32[112,544]{1,0:T(8,128)} %collective-permute-done.6, f32[3,1,544,96]{2,3,1,0:T(8,128)} %param.14), kind=kOutput, calls=%fused_computation.2 | convolution fusion | flops 105283584 | bytes 999424 | tf_op jit(solution)/shard_map/mh,krh->kmr/dot_general | solution.py:328
  59.6 4.1 %all-to-all-done.1.mine = f32[16,56,128]{2,1,0:T(8,128)S(1)} async-done(((f32[16,56,128]{2,1,0:T(8,128)}), f32[16,56,128]{2,1,0:T(8,128)S(1)}, u32[]{:S(2)}, u32[]{:S(2)}) %all-to-all-start.1) | async-done | bytes 458784 | tf_op jit(solution)/shard_map/all_to_all | solution.py:338
  63.7 1.9 %collective-permute-start.10 = (f32[16,56,128]{2,1,0:T(8,128)S(1)}, f32[16,56,128]{2,1,0:T(8,128)S(1)}, u32[]{:S(2)}, u32[]{:S(2)}) collective-permute-start(f32[16,56,128]{2,1,0:T(8,128)S(1)} %all-to-all-done.1.mine), channel_id=1, source_target_pairs={{0,1},{1,0},{2,3},{3,2},{4,5},{5,4},{6,7},{7,6},{8,9},{9,8},{10,11... | collective-permute-start | bytes 1376264 | tf_op jit(solution)/shard_map/ppermute | solution.py:39
  65.6 1.4 %collective-permute-done.10.other = f32[16,56,128]{2,1,0:T(8,128)S(1)} collective-permute-done((f32[16,56,128]{2,1,0:T(8,128)S(1)}, f32[16,56,128]{2,1,0:T(8,128)S(1)}, u32[]{:S(2)}, u32[]{:S(2)}) %collective-permute-start.10) | collective-permute-done | bytes 458784 | tf_op jit(solution)/shard_map/ppermute | solution.py:39
  67.8 7.8 %shard_map.124 = (f32[9,544]{1,0:T(8,128)}, f32[3,9,544]{2,1,0:T(8,128)}, f32[3,9,544]{2,1,0:T(8,128)}, f32[3,9,544]{2,1,0:T(8,128)}, f32[9,8,96]{2,1,0:T(8,128)}) custom-call(s32[7]{0:T(128)} %copy-done.19, f32[16,56,128]{2,1,0:T(8,128)} %copy-done.3, f32[16,56,128]{2,1,0:T(8,128)} %copy-done.7, f32[8,112,128]{2,1,0:T(8,128)} %get-tuple-element.43.reach, ...), custom_call_target="tpu_custom_call" | custom-call | flops 17989632 | bytes 7115008 | tf_op jit(solution)/shard_map/pallas_call | solution.py:65
  79.0 5.2 %all-to-all-start.2 = ((f32[8,48,96]{2,1,0:T(8,128)}), f32[8,48,96]{2,1,0:T(8,128)}, u32[]{:S(2)}, u32[]{:S(2)}) async-start(f32[8,48,96]{2,1,0:T(8,128)} %broadcast_in_dim.25), calls=%async_computation.2 | async-start | bytes 393216 | tf_op jit(solution)/shard_map/all_to_all | solution.py:55
  87.8 5.8 %all-to-all-done.2.offsets = f32[8,48,96]{2,1,0:T(8,128)} async-done(((f32[8,48,96]{2,1,0:T(8,128)}), f32[8,48,96]{2,1,0:T(8,128)}, u32[]{:S(2)}, u32[]{:S(2)}) %all-to-all-start.2) | async-done | bytes 147488 | tf_op jit(solution)/shard_map/all_to_all | solution.py:55
  94.5 2.7 %shard_map.125 = (f32[24,96]{1,0:T(8,128)S(1)}, f32[16,48,96]{2,1,0:T(8,128)}) custom-call(s32[7]{0:T(128)S(1)} %copy-done.20, f32[8,56,128]{2,1,0:T(8,128)S(1)} %copy-done.6, f32[8,56,128]{2,1,0:T(8,128)S(1)} %copy-done.15, f32[8,48,96]{2,1,0:T(8,128)} %all-to-all-done.2.offsets), custom_call_target="tpu_custom_call" | custom-call | flops 3538944 | bytes 910336 | tf_op jit(solution)/shard_map/pallas_call | solution.py:65
  97.3 6.5 %all-to-all-start.3 = ((f32[16,48,96]{2,1,0:T(8,128)}), f32[16,48,96]{2,1,0:T(8,128)S(1)}, u32[]{:S(2)}, u32[]{:S(2)}) async-start(f32[16,48,96]{2,1,0:T(8,128)} %get-tuple-element.49), calls=%async_computation.3 | async-start | bytes 786432 | tf_op jit(solution)/shard_map/all_to_all | solution.py:374
  105.6 6.2 %all-to-all-done.3.outs = f32[16,48,96]{2,1,0:T(8,128)S(1)} async-done(((f32[16,48,96]{2,1,0:T(8,128)}), f32[16,48,96]{2,1,0:T(8,128)S(1)}, u32[]{:S(2)}, u32[]{:S(2)}) %all-to-all-start.3) | async-done | bytes 294944 | tf_op jit(solution)/shard_map/all_to_all | solution.py:374
  112.8 3.4 %shard_map.126 = (f32[24,544]{1,0:T(8,128)}, f32[1,128]{1,0:T(1,128)S(1)}) custom-call(s32[7]{0:T(128)S(1)} %copy-done.20, f32[16,56,128]{2,1,0:T(8,128)S(1)} %copy-done.4, f32[16,56,128]{2,1,0:T(8,128)S(1)} %copy-done.8, f32[16,48,96]{2,1,0:T(8,128)S(1)} %all-to-all-done.3.outs, f32[96,128]{1,0:T(8,128)S(1)} %copy-done.18, ...), custom_call_target="tpu_custom_call" | custom-call | flops 9584640 | bytes 1604224 | tf_op jit(solution)/shard_map/pallas_call | solution.py:65
  116.3 3.4 %collective-permute-start.15 = (f32[128]{0:T(128)S(1)}, f32[128]{0:T(128)S(1)}, u32[]{:S(2)}, u32[]{:S(2)}) collective-permute-start(f32[128]{0:T(128)S(1)} %bitcast_add_fusion), channel_id=1, source_target_pairs={{0,1},{1,0},{2,3},{3,2},{4,5},{5,4},{6,7},{7,6},{8,9},{9,8},{10,11... | collective-permute-start | bytes 1544 | tf_op jit(solution)/shard_map/ppermute | solution.py:39
  120.5 16.3 %all_to_all.26 = f32[128,1,128]{2,1,0:T(1,128)S(1)} all-to-all(f32[128,1,128]{2,1,0:T(1,128)S(1)} %broadcast_in_dim.26), channel_id=1, replica_groups=mesh['row_0'=4,'row_1'=4,'row_2'=8,'col'=2] {'row_0','row_1','row_2'}, dimensions={0} | all-to-all | bytes 131072 | tf_op jit(solution)/shard_map/all_to_all | solution.py:55
  (104 shorter events, 29.7 us)
Async XLA Ops:
  0.7 8.3 %collective-permute-start = (f32[96,544]{1,0:T(8,128)}, f32[96,544]{1,0:T(8,128)S(1)}, u32[]{:S(2)}, u32[]{:S(2)}) collective-permute-start(f32[96,544]{1,0:T(8,128)} %bitcast.63), channel_id=1, source_target_pairs={{2,0},{4,2},{6,4},{8,6},{10,8},{12,10},{14,12},{16,14},{18,16},{20... | collective-permute-start | bytes 626696 | tf_op jit(solution)/shard_map/ppermute | solution.py:35
  2.8 29.3 %copy-start.19 = (s32[7]{0:T(128)}, s32[7]{0:T(128)S(1)}, u32[]{:S(2)}) copy-start(s32[7]{0:T(128)S(1)} %pad_add_fusion.where) | copy-start | bytes 88
  8.9 4.7 %collective-permute-start.1 = (f32[96,544]{1,0:T(8,128)S(1)}, f32[96,544]{1,0:T(8,128)S(1)}, u32[]{:S(2)}, u32[]{:S(2)}) collective-permute-start(f32[96,544]{1,0:T(8,128)S(1)} %collective-permute-done.right), channel_id=1, source_target_pairs={{0,1},{1,0},{2,3},{3,2},{4,5},{5,4},{6,7},{7,6},{8,9},{9,8},{10,11... | collective-permute-start | bytes 626696 | tf_op jit(solution)/shard_map/ppermute | solution.py:39
  12.4 1.3 collective-permute-start.2
  16.0 1.2 collective-permute-start.3
  18.0 19.4 %all-to-all-start = ((f32[8,56,128]{2,1,0:T(8,128)}), f32[8,56,128]{2,1,0:T(8,128)S(1)}, u32[]{:S(2)}, u32[]{:S(2)}) async-start(f32[8,56,128]{2,1,0:T(8,128)} %broadcast_in_dim.11), calls=%async_computation | async-start | bytes 458752 | tf_op jit(solution)/shard_map/all_to_all | solution.py:55
  32.1 26.8 %copy-start.2 = (f32[112,544]{1,0:T(8,128)}, f32[112,544]{1,0:T(8,128)S(1)}, u32[]{:S(2)}) copy-start(f32[112,544]{1,0:T(8,128)S(1)} %shard_map.122.both) | copy-start | bytes 731140
  37.3 4.4 %collective-permute-start.4 = (f32[8,56,128]{2,1,0:T(8,128)S(1)}, f32[8,56,128]{2,1,0:T(8,128)S(1)}, u32[]{:S(2)}, u32[]{:S(2)}) collective-permute-start(f32[8,56,128]{2,1,0:T(8,128)S(1)} %all-to-all-done.mine), channel_id=1, source_target_pairs={{0,1},{1,0},{2,3},{3,2},{4,5},{5,4},{6,7},{7,6},{8,9},{9,8},{10,11... | collective-permute-start | bytes 688136 | tf_op jit(solution)/shard_map/ppermute | solution.py:39
  38.8 16.3 %collective-permute-start.6 = (f32[112,544]{1,0:T(8,128)S(1)}, f32[112,544]{1,0:T(8,128)}, u32[]{:S(2)}, u32[]{:S(2)}) collective-permute-start(f32[112,544]{1,0:T(8,128)S(1)} %shard_map.122.both), channel_id=1, source_target_pairs={{0,2},{2,4},{4,6},{6,8},{8,10},{10,12},{12,14},{14,16},{16,18},{18... | collective-permute-start | bytes 731144 | tf_op jit(solution)/shard_map/ppermute | solution.py:35
  45.8 17.9 %all-to-all-start.1 = ((f32[16,56,128]{2,1,0:T(8,128)}), f32[16,56,128]{2,1,0:T(8,128)S(1)}, u32[]{:S(2)}, u32[]{:S(2)}) async-start(f32[16,56,128]{2,1,0:T(8,128)} %get-tuple-element.39), calls=%async_computation.1 | async-start | bytes 917504 | tf_op jit(solution)/shard_map/all_to_all | solution.py:338
  53.8 3.4 %collective-permute-start.8 = (f32[96,544]{1,0:T(8,128)}, f32[96,544]{1,0:T(8,128)S(1)}, u32[]{:S(2)}, u32[]{:S(2)}) collective-permute-start(f32[96,544]{1,0:T(8,128)} %copy-done.17), channel_id=1, source_target_pairs={{0,1},{1,0},{2,3},{3,2},{4,5},{5,4},{6,7},{7,6},{8,9},{9,8},{10,11... | collective-permute-start | bytes 626696 | tf_op jit(solution)/shard_map/ppermute | solution.py:39
  54.5 3.7 %collective-permute-start.5 = (f32[3,112,96]{2,1,0:T(8,128)}, f32[3,112,96]{2,1,0:T(8,128)S(1)}, u32[]{:S(2)}, u32[]{:S(2)}) collective-permute-start(f32[3,112,96]{2,1,0:T(8,128)} %convolution_bitcast_fusion.1), channel_id=1, source_target_pairs={{0,1},{1,0},{2,3},{3,2},{4,5},{5,4},{6,7},{7,6},{8,9},{9,8},{10,11... | collective-permute-start | bytes 387080 | tf_op jit(solution)/shard_map/ppermute | solution.py:39
  54.6 5.0 %collective-permute-start.9 = (f32[96,544]{1,0:T(8,128)S(1)}, f32[96,544]{1,0:T(8,128)}, u32[]{:S(2)}, u32[]{:S(2)}) collective-permute-start(f32[96,544]{1,0:T(8,128)S(1)} %slice.33), channel_id=1, source_target_pairs={{0,1},{1,0},{2,3},{3,2},{4,5},{5,4},{6,7},{7,6},{8,9},{9,8},{10,11... | collective-permute-start | bytes 626696 | tf_op jit(solution)/shard_map/ppermute | solution.py:39
  56.9 2.1 %collective-permute-start.7 = (f32[3,112,96]{2,1,0:T(8,128)S(1)}, f32[3,112,96]{2,1,0:T(8,128)S(1)}, u32[]{:S(2)}, u32[]{:S(2)}) collective-permute-start(f32[3,112,96]{2,1,0:T(8,128)S(1)} %convolution_bitcast_fusion), channel_id=1, source_target_pairs={{0,1},{1,0},{2,3},{3,2},{4,5},{5,4},{6,7},{7,6},{8,9},{9,8},{10,11... | collective-permute-start | bytes 387080 | tf_op jit(solution)/shard_map/ppermute | solution.py:39
  63.7 3.3 %collective-permute-start.10 = (f32[16,56,128]{2,1,0:T(8,128)S(1)}, f32[16,56,128]{2,1,0:T(8,128)S(1)}, u32[]{:S(2)}, u32[]{:S(2)}) collective-permute-start(f32[16,56,128]{2,1,0:T(8,128)S(1)} %all-to-all-done.1.mine), channel_id=1, source_target_pairs={{0,1},{1,0},{2,3},{3,2},{4,5},{5,4},{6,7},{7,6},{8,9},{9,8},{10,11... | collective-permute-start | bytes 1376264 | tf_op jit(solution)/shard_map/ppermute | solution.py:39
  75.6 1.9 %collective-permute-start.11 = (f32[9,8,96]{2,1,0:T(8,128)}, f32[9,8,96]{2,1,0:T(8,128)S(1)}, u32[]{:S(2)}, u32[]{:S(2)}) collective-permute-start(f32[9,8,96]{2,1,0:T(8,128)} %get-tuple-element.48), channel_id=1, source_target_pairs={{0,1},{1,0},{2,3},{3,2},{4,5},{5,4},{6,7},{7,6},{8,9},{9,8},{10,11... | collective-permute-start | bytes 82952 | tf_op jit(solution)/shard_map/ppermute | solution.py:39
  76.1 8.1 %collective-permute-start.12 = (f32[3,9,544]{2,1,0:T(8,128)}, f32[3,9,544]{2,1,0:T(8,128)}, u32[]{:S(2)}, u32[]{:S(2)}) collective-permute-start(f32[3,9,544]{2,1,0:T(8,128)} %get-tuple-element.53), channel_id=1, source_target_pairs={{0,1},{1,0},{2,3},{3,2},{4,5},{5,4},{6,7},{7,6},{8,9},{9,8},{10,11... | collective-permute-start | bytes 176264 | tf_op jit(solution)/shard_map/ppermute | solution.py:39
  76.2 8.0 %collective-permute-start.13 = (f32[3,9,544]{2,1,0:T(8,128)}, f32[3,9,544]{2,1,0:T(8,128)}, u32[]{:S(2)}, u32[]{:S(2)}) collective-permute-start(f32[3,9,544]{2,1,0:T(8,128)} %get-tuple-element.54), channel_id=1, source_target_pairs={{2,0},{4,2},{6,4},{8,6},{10,8},{12,10},{14,12},{16,14},{18,16},{20... | collective-permute-start | bytes 176264 | tf_op jit(solution)/shard_map/ppermute | solution.py:35
  79.0 14.6 %all-to-all-start.2 = ((f32[8,48,96]{2,1,0:T(8,128)}), f32[8,48,96]{2,1,0:T(8,128)}, u32[]{:S(2)}, u32[]{:S(2)}) async-start(f32[8,48,96]{2,1,0:T(8,128)} %broadcast_in_dim.25), calls=%async_computation.2 | async-start | bytes 393216 | tf_op jit(solution)/shard_map/all_to_all | solution.py:55
  84.2 27.6 %copy-start.4 = (f32[16,56,128]{2,1,0:T(8,128)S(1)}, f32[16,56,128]{2,1,0:T(8,128)}, u32[]{:S(2)}) copy-start(f32[16,56,128]{2,1,0:T(8,128)} %copy-done.3) | copy-start | bytes 1376260
  84.2 27.6 %copy-start.18 = (f32[96,128]{1,0:T(8,128)S(1)}, f32[96,128]{1,0:T(8,128)}, u32[]{:S(2)}) copy-start(f32[96,128]{1,0:T(8,128)} %get-tuple-element.50.prefix) | copy-start | bytes 147460
  86.9 17.7 %collective-permute-start.14 = (f32[24,544]{1,0:T(8,128)S(1)}, f32[24,544]{1,0:T(8,128)S(1)}, u32[]{:S(2)}, u32[]{:S(2)}) collective-permute-start(f32[24,544]{1,0:T(8,128)S(1)} %constant_dynamic-slice_fusion), channel_id=1, source_target_pairs={{0,1},{1,0},{2,3},{3,2},{4,5},{5,4},{6,7},{7,6},{8,9},{9,8},{10,11... | collective-permute-start | bytes 156680 | tf_op jit(solution)/shard_map/ppermute | solution.py:39
  97.3 14.5 %all-to-all-start.3 = ((f32[16,48,96]{2,1,0:T(8,128)}), f32[16,48,96]{2,1,0:T(8,128)S(1)}, u32[]{:S(2)}, u32[]{:S(2)}) async-start(f32[16,48,96]{2,1,0:T(8,128)} %get-tuple-element.49), calls=%async_computation.3 | async-start | bytes 786432 | tf_op jit(solution)/shard_map/all_to_all | solution.py:374
  116.3 4.2 %collective-permute-start.15 = (f32[128]{0:T(128)S(1)}, f32[128]{0:T(128)S(1)}, u32[]{:S(2)}, u32[]{:S(2)}) collective-permute-start(f32[128]{0:T(128)S(1)} %bitcast_add_fusion), channel_id=1, source_target_pairs={{0,1},{1,0},{2,3},{3,2},{4,5},{5,4},{6,7},{7,6},{8,9},{9,8},{10,11... | collective-permute-start | bytes 1544 | tf_op jit(solution)/shard_map/ppermute | solution.py:39
  (22 other events, 124.5 us)

commit v5 on v4

--- a/solution.py
+++ b/solution.py
@@ -97,7 +97,7 @@
     for k in range(count - 1):
         run = dot(run[:, :rows], maps[count - 2 - k])
         reach[count - 2 - k] = run
-        early = maps[0][:rmax] if k == 0 else dot(maps[k][:rmax, :rmax], early)
+        early = maps[0][:rmax] if k == 0 else close(maps[k][:rmax, :rmax], early)
         chosen = jnp.where(place == k + 1, early, chosen)
     prefix[...] = chosen
     out = jnp.where(side == 0, run[:half_rows], run[half_rows:])
@@ -354,7 +354,7 @@
     )
     upper = along_rows(upper_send, -1)
     partial = terms[:params] + swapped(terms)[:params]
-    shared = jnp.concatenate([partial + terms[params : 2 * params], terms[2 * params :]], axis=0)
+    shared = terms[params:] + jnp.pad(partial, ((0, params), (0, 0), (0, 0)))
     shared = shared.reshape(2 * params * count, rmax)
     offsets = everywhere(shared, LINE)
     dense = dense + swapped(dense_other)

time: 139 us -> 140 us (level)
  transfers between devices with their start and end apart: 20 -> 20, of which waited for: 9 -> 9; matrix products, arithmetic and copies ran while one was open for 8% -> 9% of each run, Pallas kernels for 9% -> 9%
where the time goes in v5:
time: 140 us; the launch traced here: 139 us
  starting transfers between devices  47.6 us (34%)
  waiting for transfers between devices  25.6 us (18%)
  Pallas kernels  24.8 us (18%)
  blocking collectives  16.3 us (12%)
  local copies, waits for them, and re-layouts  11.6 us (8%)
  other arithmetic  7.31 us (5%)
  matrix products  4.74 us (3%)
    pallas_call x7, Pallas kernels, on_core(): pl.pallas_call(kernel, out_shape=outs, in_specs=[SMEM] + [VMEM] * len(arr...  24.8 us
    all_to_all x1, blocking collectives, everywhere(): lax.all_to_all(jnp.broadcast_to(x[None], (count, *x.shape)), axis, 0, 0,...  16.3 us
    all_to_all x2, starting transfers between devices, everywhere(): lax.all_to_all(jnp.broadcast_to(x[None], (count, *x.shape)), axis, 0, 0,...  13.9 us
    ppermute x13, starting transfers between devices, swapped(): return lax.ppermute(block, 'col', [(0, 1), (1, 0)])  13.5 us
    all_to_all x2, waiting for transfers between devices, everywhere(): lax.all_to_all(jnp.broadcast_to(x[None], (count, *x.shape)), axis, 0, 0,...  9.72 us
    unnamed x52, local copies, waits for them, and re-layouts  9.36 us
    all_to_all x1, starting transfers between devices, body(): totals = lax.all_to_all(send, PLANE, 0, 0, tiled=True)  7.99 us
    all_to_all x1, starting transfers between devices, body(): outs = lax.all_to_all(send, PLANE, 0, 0, tiled=True)  6.53 us
  transfers between devices with their start and end apart: 20, of which 9 were waited for; matrix products, arithmetic and copies ran while one was open for 9% of the time, Pallas kernels for 9%

profile of v5, /device:TPU:1, one launch (start us, length us, event | category | flops | bytes accessed | tf_op | source)
XLA Modules:
  0.0 138.8 jit_solution(4900272549757498453)
XLA Ops:
  2.8 1.7 %copy-done = f32[1,1088,544]{1,2,0:T(8,128)S(1)} copy-done((f32[1,1088,544]{1,2,0:T(8,128)S(1)}, f32[1,1088,544]{1,2,0:T(8,128)}, u32[]{:S(2)}) %copy-start) | copy-done | bytes 2367512
  5.5 2.3 %shard_map.120 = (f32[96,544]{1,0:T(8,128)S(1)}, f32[96,544]{1,0:T(8,128)S(1)}) custom-call(s32[7]{0:T(128)S(1)} %pad_add_fusion.where, f32[544,1088]{1,0:T(8,128)S(1)} %bitcast.55, f32[96,544]{1,0:T(8,128)S(1)} %bitcast.57), custom_call_target="tpu_custom_call" | custom-call | flops 113639424 | bytes 2994176 | tf_op jit(solution)/shard_map/pallas_call | solution.py:65
  8.9 3.4 %collective-permute-start.1 = (f32[96,544]{1,0:T(8,128)S(1)}, f32[96,544]{1,0:T(8,128)S(1)}, u32[]{:S(2)}, u32[]{:S(2)}) collective-permute-start(f32[96,544]{1,0:T(8,128)S(1)} %collective-permute-done.right), channel_id=1, source_target_pairs={{0,1},{1,0},{2,3},{3,2},{4,5},{5,4},{6,7},{7,6},{8,9},{9,8},{10,11... | collective-permute-start | bytes 626696 | tf_op jit(solution)/shard_map/ppermute | solution.py:39
  13.7 1.6 %shard_map.121 = (f32[56,128]{1,0:T(8,128)S(1)}, f32[56,128]{1,0:T(8,128)S(1)}) custom-call(s32[7]{0:T(128)S(1)} %pad_add_fusion.where, f32[96,544]{1,0:T(8,128)S(1)} %collective-permute-done.right, f32[96,544]{1,0:T(8,128)S(1)} %collective-permute-done.1.right_other, f32[9,544]{1,0:T(8,128)S(1)} %pad_maximum_fusion.source, ...), custom_call_target="tpu_custom_call" | custom-call | flops 23396352 | bytes 932096 | tf_op jit(solution)/shard_map/pallas_call | solution.py:65
  17.9 8.7 %all-to-all-start = ((f32[8,56,128]{2,1,0:T(8,128)}), f32[8,56,128]{2,1,0:T(8,128)S(1)}, u32[]{:S(2)}, u32[]{:S(2)}) async-start(f32[8,56,128]{2,1,0:T(8,128)} %broadcast_in_dim.11), calls=%async_computation | async-start | bytes 458752 | tf_op jit(solution)/shard_map/all_to_all | solution.py:55
  28.6 3.5 %shard_map.122.both = f32[112,544]{1,0:T(8,128)S(1)} custom-call(s32[7]{0:T(128)S(1)} %pad_add_fusion.where, f32[544,1088]{1,0:T(8,128)S(1)} %bitcast.56, f32[9,544]{1,0:T(8,128)S(1)} %pad_maximum_fusion.source, f32[9,544]{1,0:T(8,128)S(1)} %collective-permute-done.2.source_other, f32[96,544]{1,0:T(8,128)S(1)} %copy-done.11, f32[96,544]{1,0:T(8,128)S(1)} %copy-done.13), custom_call_target="tpu_custom_call" | custom-call | flops 132579328 | bytes 3068160 | tf_op jit(solution)/shard_map/pallas_call | solution.py:65
  33.4 3.9 %all-to-all-done.mine = f32[8,56,128]{2,1,0:T(8,128)S(1)} async-done(((f32[8,56,128]{2,1,0:T(8,128)}), f32[8,56,128]{2,1,0:T(8,128)S(1)}, u32[]{:S(2)}, u32[]{:S(2)}) %all-to-all-start) | async-done | bytes 229408 | tf_op jit(solution)/shard_map/all_to_all | solution.py:55
  37.3 1.5 %collective-permute-start.4 = (f32[8,56,128]{2,1,0:T(8,128)S(1)}, f32[8,56,128]{2,1,0:T(8,128)S(1)}, u32[]{:S(2)}, u32[]{:S(2)}) collective-permute-start(f32[8,56,128]{2,1,0:T(8,128)S(1)} %all-to-all-done.mine), channel_id=1, source_target_pairs={{0,1},{1,0},{2,3},{3,2},{4,5},{5,4},{6,7},{7,6},{8,9},{9,8},{10,11... | collective-permute-start | bytes 688136 | tf_op jit(solution)/shard_map/ppermute | solution.py:39
  38.8 2.9 %collective-permute-start.6 = (f32[112,544]{1,0:T(8,128)S(1)}, f32[112,544]{1,0:T(8,128)}, u32[]{:S(2)}, u32[]{:S(2)}) collective-permute-start(f32[112,544]{1,0:T(8,128)S(1)} %shard_map.122.both), channel_id=1, source_target_pairs={{0,2},{2,4},{4,6},{6,8},{8,10},{10,12},{12,14},{14,16},{16,18},{18... | collective-permute-start | bytes 731144 | tf_op jit(solution)/shard_map/ppermute | solution.py:35
  42.4 3.4 %shard_map.123 = (f32[8,112,128]{2,1,0:T(8,128)}, f32[96,128]{1,0:T(8,128)}, f32[16,56,128]{2,1,0:T(8,128)}) custom-call(s32[7]{0:T(128)} %copy-done.19, f32[8,56,128]{2,1,0:T(8,128)} %copy-done.5, f32[8,56,128]{2,1,0:T(8,128)} %copy-done.14), custom_call_target="tpu_custom_call" | custom-call | flops 33030144 | bytes 1425408 | tf_op jit(solution)/shard_map/pallas_call | solution.py:65
  45.8 8.0 %all-to-all-start.1 = ((f32[16,56,128]{2,1,0:T(8,128)}), f32[16,56,128]{2,1,0:T(8,128)S(1)}, u32[]{:S(2)}, u32[]{:S(2)}) async-start(f32[16,56,128]{2,1,0:T(8,128)} %get-tuple-element.39), calls=%async_computation.1 | async-start | bytes 917504 | tf_op jit(solution)/shard_map/all_to_all | solution.py:338
  55.1 1.8 %convolution_bitcast_fusion = f32[3,112,96]{2,1,0:T(8,128)S(1)} fusion(f32[112,544]{1,0:T(8,128)} %collective-permute-done.6, f32[3,1,544,96]{2,3,1,0:T(8,128)} %param.14), kind=kOutput, calls=%fused_computation.2 | convolution fusion | flops 105283584 | bytes 999424 | tf_op jit(solution)/shard_map/mh,krh->kmr/dot_general | solution.py:328
  59.7 4.1 %all-to-all-done.1.mine = f32[16,56,128]{2,1,0:T(8,128)S(1)} async-done(((f32[16,56,128]{2,1,0:T(8,128)}), f32[16,56,128]{2,1,0:T(8,128)S(1)}, u32[]{:S(2)}, u32[]{:S(2)}) %all-to-all-start.1) | async-done | bytes 458784 | tf_op jit(solution)/shard_map/all_to_all | solution.py:338
  63.7 1.9 %collective-permute-start.10 = (f32[16,56,128]{2,1,0:T(8,128)S(1)}, f32[16,56,128]{2,1,0:T(8,128)S(1)}, u32[]{:S(2)}, u32[]{:S(2)}) collective-permute-start(f32[16,56,128]{2,1,0:T(8,128)S(1)} %all-to-all-done.1.mine), channel_id=1, source_target_pairs={{0,1},{1,0},{2,3},{3,2},{4,5},{5,4},{6,7},{7,6},{8,9},{9,8},{10,11... | collective-permute-start | bytes 1376264 | tf_op jit(solution)/shard_map/ppermute | solution.py:39
  65.6 1.4 %collective-permute-done.10.other = f32[16,56,128]{2,1,0:T(8,128)S(1)} collective-permute-done((f32[16,56,128]{2,1,0:T(8,128)S(1)}, f32[16,56,128]{2,1,0:T(8,128)S(1)}, u32[]{:S(2)}, u32[]{:S(2)}) %collective-permute-start.10) | collective-permute-done | bytes 458784 | tf_op jit(solution)/shard_map/ppermute | solution.py:39
  67.8 7.8 %shard_map.124 = (f32[9,544]{1,0:T(8,128)}, f32[3,9,544]{2,1,0:T(8,128)}, f32[3,9,544]{2,1,0:T(8,128)}, f32[3,9,544]{2,1,0:T(8,128)}, f32[9,8,96]{2,1,0:T(8,128)}) custom-call(s32[7]{0:T(128)} %copy-done.19, f32[16,56,128]{2,1,0:T(8,128)} %copy-done.3, f32[16,56,128]{2,1,0:T(8,128)} %copy-done.7, f32[8,112,128]{2,1,0:T(8,128)} %get-tuple-element.43.reach, ...), custom_call_target="tpu_custom_call" | custom-call | flops 17989632 | bytes 7115008 | tf_op jit(solution)/shard_map/pallas_call | solution.py:65
  79.7 5.2 %all-to-all-start.2 = ((f32[8,48,96]{2,1,0:T(8,128)}), f32[8,48,96]{2,1,0:T(8,128)}, u32[]{:S(2)}, u32[]{:S(2)}) async-start(f32[8,48,96]{2,1,0:T(8,128)} %broadcast_in_dim.25), calls=%async_computation.2 | async-start | bytes 393216 | tf_op jit(solution)/shard_map/all_to_all | solution.py:55
  88.5 5.8 %all-to-all-done.2.offsets = f32[8,48,96]{2,1,0:T(8,128)} async-done(((f32[8,48,96]{2,1,0:T(8,128)}), f32[8,48,96]{2,1,0:T(8,128)}, u32[]{:S(2)}, u32[]{:S(2)}) %all-to-all-start.2) | async-done | bytes 147488 | tf_op jit(solution)/shard_map/all_to_all | solution.py:55
  95.2 2.7 %shard_map.125 = (f32[24,96]{1,0:T(8,128)S(1)}, f32[16,48,96]{2,1,0:T(8,128)}) custom-call(s32[7]{0:T(128)S(1)} %copy-done.20, f32[8,56,128]{2,1,0:T(8,128)S(1)} %copy-done.6, f32[8,56,128]{2,1,0:T(8,128)S(1)} %copy-done.15, f32[8,48,96]{2,1,0:T(8,128)} %all-to-all-done.2.offsets), custom_call_target="tpu_custom_call" | custom-call | flops 3538944 | bytes 910336 | tf_op jit(solution)/shard_map/pallas_call | solution.py:65
  97.9 6.5 %all-to-all-start.3 = ((f32[16,48,96]{2,1,0:T(8,128)}), f32[16,48,96]{2,1,0:T(8,128)S(1)}, u32[]{:S(2)}, u32[]{:S(2)}) async-start(f32[16,48,96]{2,1,0:T(8,128)} %get-tuple-element.49), calls=%async_computation.3 | async-start | bytes 786432 | tf_op jit(solution)/shard_map/all_to_all | solution.py:374
  106.3 6.2 %all-to-all-done.3.outs = f32[16,48,96]{2,1,0:T(8,128)S(1)} async-done(((f32[16,48,96]{2,1,0:T(8,128)}), f32[16,48,96]{2,1,0:T(8,128)S(1)}, u32[]{:S(2)}, u32[]{:S(2)}) %all-to-all-start.3) | async-done | bytes 294944 | tf_op jit(solution)/shard_map/all_to_all | solution.py:374
  113.5 3.4 %shard_map.126 = (f32[24,544]{1,0:T(8,128)}, f32[1,128]{1,0:T(1,128)S(1)}) custom-call(s32[7]{0:T(128)S(1)} %copy-done.20, f32[16,56,128]{2,1,0:T(8,128)S(1)} %copy-done.4, f32[16,56,128]{2,1,0:T(8,128)S(1)} %copy-done.8, f32[16,48,96]{2,1,0:T(8,128)S(1)} %all-to-all-done.3.outs, f32[96,128]{1,0:T(8,128)S(1)} %copy-done.18, ...), custom_call_target="tpu_custom_call" | custom-call | flops 9584640 | bytes 1604224 | tf_op jit(solution)/shard_map/pallas_call | solution.py:65
  117.0 3.4 %collective-permute-start.15 = (f32[128]{0:T(128)S(1)}, f32[128]{0:T(128)S(1)}, u32[]{:S(2)}, u32[]{:S(2)}) collective-permute-start(f32[128]{0:T(128)S(1)} %bitcast_add_fusion), channel_id=1, source_target_pairs={{0,1},{1,0},{2,3},{3,2},{4,5},{5,4},{6,7},{7,6},{8,9},{9,8},{10,11... | collective-permute-start | bytes 1544 | tf_op jit(solution)/shard_map/ppermute | solution.py:39
  121.2 16.3 %all_to_all.26 = f32[128,1,128]{2,1,0:T(1,128)S(1)} all-to-all(f32[128,1,128]{2,1,0:T(1,128)S(1)} %broadcast_in_dim.26), channel_id=1, replica_groups=mesh['row_0'=4,'row_1'=4,'row_2'=8,'col'=2] {'row_0','row_1','row_2'}, dimensions={0} | all-to-all | bytes 131072 | tf_op jit(solution)/shard_map/all_to_all | solution.py:55
  (104 shorter events, 30.4 us)
Async XLA Ops:
  0.7 8.3 %collective-permute-start = (f32[96,544]{1,0:T(8,128)}, f32[96,544]{1,0:T(8,128)S(1)}, u32[]{:S(2)}, u32[]{:S(2)}) collective-permute-start(f32[96,544]{1,0:T(8,128)} %bitcast.63), channel_id=1, source_target_pairs={{2,0},{4,2},{6,4},{8,6},{10,8},{12,10},{14,12},{16,14},{18,16},{20... | collective-permute-start | bytes 626696 | tf_op jit(solution)/shard_map/ppermute | solution.py:35
  2.8 29.3 %copy-start.19 = (s32[7]{0:T(128)}, s32[7]{0:T(128)S(1)}, u32[]{:S(2)}) copy-start(s32[7]{0:T(128)S(1)} %pad_add_fusion.where) | copy-start | bytes 88
  8.9 4.7 %collective-permute-start.1 = (f32[96,544]{1,0:T(8,128)S(1)}, f32[96,544]{1,0:T(8,128)S(1)}, u32[]{:S(2)}, u32[]{:S(2)}) collective-permute-start(f32[96,544]{1,0:T(8,128)S(1)} %collective-permute-done.right), channel_id=1, source_target_pairs={{0,1},{1,0},{2,3},{3,2},{4,5},{5,4},{6,7},{7,6},{8,9},{9,8},{10,11... | collective-permute-start | bytes 626696 | tf_op jit(solution)/shard_map/ppermute | solution.py:39
  12.4 1.3 collective-permute-start.2
  16.0 1.2 collective-permute-start.3
  17.9 19.4 %all-to-all-start = ((f32[8,56,128]{2,1,0:T(8,128)}), f32[8,56,128]{2,1,0:T(8,128)S(1)}, u32[]{:S(2)}, u32[]{:S(2)}) async-start(f32[8,56,128]{2,1,0:T(8,128)} %broadcast_in_dim.11), calls=%async_computation | async-start | bytes 458752 | tf_op jit(solution)/shard_map/all_to_all | solution.py:55
  32.1 26.8 %copy-start.2 = (f32[112,544]{1,0:T(8,128)}, f32[112,544]{1,0:T(8,128)S(1)}, u32[]{:S(2)}) copy-start(f32[112,544]{1,0:T(8,128)S(1)} %shard_map.122.both) | copy-start | bytes 731140
  37.3 4.4 %collective-permute-start.4 = (f32[8,56,128]{2,1,0:T(8,128)S(1)}, f32[8,56,128]{2,1,0:T(8,128)S(1)}, u32[]{:S(2)}, u32[]{:S(2)}) collective-permute-start(f32[8,56,128]{2,1,0:T(8,128)S(1)} %all-to-all-done.mine), channel_id=1, source_target_pairs={{0,1},{1,0},{2,3},{3,2},{4,5},{5,4},{6,7},{7,6},{8,9},{9,8},{10,11... | collective-permute-start | bytes 688136 | tf_op jit(solution)/shard_map/ppermute | solution.py:39
  38.8 16.3 %collective-permute-start.6 = (f32[112,544]{1,0:T(8,128)S(1)}, f32[112,544]{1,0:T(8,128)}, u32[]{:S(2)}, u32[]{:S(2)}) collective-permute-start(f32[112,544]{1,0:T(8,128)S(1)} %shard_map.122.both), channel_id=1, source_target_pairs={{0,2},{2,4},{4,6},{6,8},{8,10},{10,12},{12,14},{14,16},{16,18},{18... | collective-permute-start | bytes 731144 | tf_op jit(solution)/shard_map/ppermute | solution.py:35
  45.8 17.9 %all-to-all-start.1 = ((f32[16,56,128]{2,1,0:T(8,128)}), f32[16,56,128]{2,1,0:T(8,128)S(1)}, u32[]{:S(2)}, u32[]{:S(2)}) async-start(f32[16,56,128]{2,1,0:T(8,128)} %get-tuple-element.39), calls=%async_computation.1 | async-start | bytes 917504 | tf_op jit(solution)/shard_map/all_to_all | solution.py:338
  53.8 3.4 %collective-permute-start.8 = (f32[96,544]{1,0:T(8,128)}, f32[96,544]{1,0:T(8,128)S(1)}, u32[]{:S(2)}, u32[]{:S(2)}) collective-permute-start(f32[96,544]{1,0:T(8,128)} %copy-done.17), channel_id=1, source_target_pairs={{0,1},{1,0},{2,3},{3,2},{4,5},{5,4},{6,7},{7,6},{8,9},{9,8},{10,11... | collective-permute-start | bytes 626696 | tf_op jit(solution)/shard_map/ppermute | solution.py:39
  54.5 3.7 %collective-permute-start.5 = (f32[3,112,96]{2,1,0:T(8,128)}, f32[3,112,96]{2,1,0:T(8,128)S(1)}, u32[]{:S(2)}, u32[]{:S(2)}) collective-permute-start(f32[3,112,96]{2,1,0:T(8,128)} %convolution_bitcast_fusion.1), channel_id=1, source_target_pairs={{0,1},{1,0},{2,3},{3,2},{4,5},{5,4},{6,7},{7,6},{8,9},{9,8},{10,11... | collective-permute-start | bytes 387080 | tf_op jit(solution)/shard_map/ppermute | solution.py:39
  54.6 5.0 %collective-permute-start.9 = (f32[96,544]{1,0:T(8,128)S(1)}, f32[96,544]{1,0:T(8,128)}, u32[]{:S(2)}, u32[]{:S(2)}) collective-permute-start(f32[96,544]{1,0:T(8,128)S(1)} %slice.30), channel_id=1, source_target_pairs={{0,1},{1,0},{2,3},{3,2},{4,5},{5,4},{6,7},{7,6},{8,9},{9,8},{10,11... | collective-permute-start | bytes 626696 | tf_op jit(solution)/shard_map/ppermute | solution.py:39
  56.9 2.1 %collective-permute-start.7 = (f32[3,112,96]{2,1,0:T(8,128)S(1)}, f32[3,112,96]{2,1,0:T(8,128)S(1)}, u32[]{:S(2)}, u32[]{:S(2)}) collective-permute-start(f32[3,112,96]{2,1,0:T(8,128)S(1)} %convolution_bitcast_fusion), channel_id=1, source_target_pairs={{0,1},{1,0},{2,3},{3,2},{4,5},{5,4},{6,7},{7,6},{8,9},{9,8},{10,11... | collective-permute-start | bytes 387080 | tf_op jit(solution)/shard_map/ppermute | solution.py:39
  63.7 3.3 %collective-permute-start.10 = (f32[16,56,128]{2,1,0:T(8,128)S(1)}, f32[16,56,128]{2,1,0:T(8,128)S(1)}, u32[]{:S(2)}, u32[]{:S(2)}) collective-permute-start(f32[16,56,128]{2,1,0:T(8,128)S(1)} %all-to-all-done.1.mine), channel_id=1, source_target_pairs={{0,1},{1,0},{2,3},{3,2},{4,5},{5,4},{6,7},{7,6},{8,9},{9,8},{10,11... | collective-permute-start | bytes 1376264 | tf_op jit(solution)/shard_map/ppermute | solution.py:39
  75.6 1.9 %collective-permute-start.11 = (f32[9,8,96]{2,1,0:T(8,128)}, f32[9,8,96]{2,1,0:T(8,128)S(1)}, u32[]{:S(2)}, u32[]{:S(2)}) collective-permute-start(f32[9,8,96]{2,1,0:T(8,128)} %get-tuple-element.48), channel_id=1, source_target_pairs={{0,1},{1,0},{2,3},{3,2},{4,5},{5,4},{6,7},{7,6},{8,9},{9,8},{10,11... | collective-permute-start | bytes 82952 | tf_op jit(solution)/shard_map/ppermute | solution.py:39
  76.1 8.8 %collective-permute-start.12 = (f32[3,9,544]{2,1,0:T(8,128)}, f32[3,9,544]{2,1,0:T(8,128)}, u32[]{:S(2)}, u32[]{:S(2)}) collective-permute-start(f32[3,9,544]{2,1,0:T(8,128)} %get-tuple-element.53), channel_id=1, source_target_pairs={{0,1},{1,0},{2,3},{3,2},{4,5},{5,4},{6,7},{7,6},{8,9},{9,8},{10,11... | collective-permute-start | bytes 176264 | tf_op jit(solution)/shard_map/ppermute | solution.py:39
  76.2 8.7 %collective-permute-start.13 = (f32[3,9,544]{2,1,0:T(8,128)}, f32[3,9,544]{2,1,0:T(8,128)}, u32[]{:S(2)}, u32[]{:S(2)}) collective-permute-start(f32[3,9,544]{2,1,0:T(8,128)} %get-tuple-element.54), channel_id=1, source_target_pairs={{2,0},{4,2},{6,4},{8,6},{10,8},{12,10},{14,12},{16,14},{18,16},{20... | collective-permute-start | bytes 176264 | tf_op jit(solution)/shard_map/ppermute | solution.py:35
  79.7 14.6 %all-to-all-start.2 = ((f32[8,48,96]{2,1,0:T(8,128)}), f32[8,48,96]{2,1,0:T(8,128)}, u32[]{:S(2)}, u32[]{:S(2)}) async-start(f32[8,48,96]{2,1,0:T(8,128)} %broadcast_in_dim.25), calls=%async_computation.2 | async-start | bytes 393216 | tf_op jit(solution)/shard_map/all_to_all | solution.py:55
  84.9 27.6 %copy-start.4 = (f32[16,56,128]{2,1,0:T(8,128)S(1)}, f32[16,56,128]{2,1,0:T(8,128)}, u32[]{:S(2)}) copy-start(f32[16,56,128]{2,1,0:T(8,128)} %copy-done.3) | copy-start | bytes 1376260
  84.9 27.6 %copy-start.18 = (f32[96,128]{1,0:T(8,128)S(1)}, f32[96,128]{1,0:T(8,128)}, u32[]{:S(2)}) copy-start(f32[96,128]{1,0:T(8,128)} %get-tuple-element.50.prefix) | copy-start | bytes 147460
  87.6 17.7 %collective-permute-start.14 = (f32[24,544]{1,0:T(8,128)S(1)}, f32[24,544]{1,0:T(8,128)S(1)}, u32[]{:S(2)}, u32[]{:S(2)}) collective-permute-start(f32[24,544]{1,0:T(8,128)S(1)} %constant_dynamic-slice_fusion), channel_id=1, source_target_pairs={{0,1},{1,0},{2,3},{3,2},{4,5},{5,4},{6,7},{7,6},{8,9},{9,8},{10,11... | collective-permute-start | bytes 156680 | tf_op jit(solution)/shard_map/ppermute | solution.py:39
  97.9 14.6 %all-to-all-start.3 = ((f32[16,48,96]{2,1,0:T(8,128)}), f32[16,48,96]{2,1,0:T(8,128)S(1)}, u32[]{:S(2)}, u32[]{:S(2)}) async-start(f32[16,48,96]{2,1,0:T(8,128)} %get-tuple-element.49), calls=%async_computation.3 | async-start | bytes 786432 | tf_op jit(solution)/shard_map/all_to_all | solution.py:374
  117.0 4.2 %collective-permute-start.15 = (f32[128]{0:T(128)S(1)}, f32[128]{0:T(128)S(1)}, u32[]{:S(2)}, u32[]{:S(2)}) collective-permute-start(f32[128]{0:T(128)S(1)} %bitcast_add_fusion), channel_id=1, source_target_pairs={{0,1},{1,0},{2,3},{3,2},{4,5},{5,4},{6,7},{7,6},{8,9},{9,8},{10,11... | collective-permute-start | bytes 1544 | tf_op jit(solution)/shard_map/ppermute | solution.py:39
  (22 other events, 125.8 us)

commit v6 on v4

--- a/solution.py
+++ b/solution.py
@@ -322,11 +322,8 @@
     here_terms = jnp.einsum("mh,krh->kmr", both, d_left, precision=high)
     maps, both, here_terms = lax.optimization_barrier((maps, both, here_terms))
     maps_other = swapped(maps)
-    both_before = along_rows(both, 1)
     both_other = swapped(both[lines:])
     here_terms = here_terms + swapped(here_terms)
-    ahead_terms = jnp.einsum("mh,krh->kmr", both_before, d_right, precision=high)
-    ahead_terms = ahead_terms + swapped(ahead_terms)
     reach, prefix, send = on_core(
         functools.partial(line_back, rmax),
         [floats(in_line, rows, LANES), floats(rmax, LANES), floats(groups, rows // 2, LANES)],
@@ -335,6 +332,10 @@
         4 * in_line * rows * rmax * rmax,
         limit=60,
     )
+    late_both, send = lax.optimization_barrier((both, send))
+    both_before = along_rows(late_both, 1)
+    ahead_terms = jnp.einsum("mh,krh->kmr", both_before, d_right, precision=high)
+    ahead_terms = ahead_terms + swapped(ahead_terms)
     totals = lax.all_to_all(send, PLANE, 0, 0, tiled=True)
     totals, here_terms, ahead_terms, moved, both_other = lax.optimization_barrier(
         (totals, here_terms, ahead_terms, moved, both_other)

time: 139 us -> 140 us (level)
  transfers between devices with their start and end apart: 20 -> 20, of which waited for: 9 -> 10; matrix products, arithmetic and copies ran while one was open for 8% -> 8% of each run, Pallas kernels for 9% -> 6%
where the time goes in v6:
time: 140 us; the launch traced here: 139 us
  starting transfers between devices  48 us (34%)
  waiting for transfers between devices  26.3 us (19%)
  Pallas kernels  24.8 us (18%)
  blocking collectives  16.3 us (12%)
  local copies, waits for them, and re-layouts  11.6 us (8%)
  other arithmetic  6.59 us (5%)
  matrix products  4.74 us (3%)
    pallas_call x7, Pallas kernels, on_core(): pl.pallas_call(kernel, out_shape=outs, in_specs=[SMEM] + [VMEM] * len(arr...  24.8 us
    all_to_all x1, blocking collectives, everywhere(): lax.all_to_all(jnp.broadcast_to(x[None], (count, *x.shape)), axis, 0, 0,...  16.3 us
    ppermute x13, starting transfers between devices, swapped(): return lax.ppermute(block, 'col', [(0, 1), (1, 0)])  14.1 us
    all_to_all x2, starting transfers between devices, everywhere(): lax.all_to_all(jnp.broadcast_to(x[None], (count, *x.shape)), axis, 0, 0,...  13.8 us
    all_to_all x2, waiting for transfers between devices, everywhere(): lax.all_to_all(jnp.broadcast_to(x[None], (count, *x.shape)), axis, 0, 0,...  9.74 us
    unnamed x52, local copies, waits for them, and re-layouts  9.37 us
    all_to_all x1, starting transfers between devices, body(): totals = lax.all_to_all(send, PLANE, 0, 0, tiled=True)  7.98 us
    all_to_all x1, starting transfers between devices, body(): outs = lax.all_to_all(send, PLANE, 0, 0, tiled=True)  6.54 us
  transfers between devices with their start and end apart: 20, of which 10 were waited for; matrix products, arithmetic and copies ran while one was open for 8% of the time, Pallas kernels for 6%

profile of v6, /device:TPU:1, one launch (start us, length us, event | category | flops | bytes accessed | tf_op | source)
XLA Modules:
  0.0 139.2 jit_solution(13109084585615899909)
XLA Ops:
  2.8 1.7 %copy-done = f32[1,1088,544]{1,2,0:T(8,128)S(1)} copy-done((f32[1,1088,544]{1,2,0:T(8,128)S(1)}, f32[1,1088,544]{1,2,0:T(8,128)}, u32[]{:S(2)}) %copy-start) | copy-done | bytes 2367512
  5.5 2.3 %shard_map.120 = (f32[96,544]{1,0:T(8,128)S(1)}, f32[96,544]{1,0:T(8,128)S(1)}) custom-call(s32[7]{0:T(128)S(1)} %pad_add_fusion.where, f32[544,1088]{1,0:T(8,128)S(1)} %bitcast.55, f32[96,544]{1,0:T(8,128)S(1)} %bitcast.57), custom_call_target="tpu_custom_call" | custom-call | flops 113639424 | bytes 2994176 | tf_op jit(solution)/shard_map/pallas_call | solution.py:65
  8.9 3.4 %collective-permute-start.1 = (f32[96,544]{1,0:T(8,128)S(1)}, f32[96,544]{1,0:T(8,128)S(1)}, u32[]{:S(2)}, u32[]{:S(2)}) collective-permute-start(f32[96,544]{1,0:T(8,128)S(1)} %collective-permute-done.right), channel_id=1, source_target_pairs={{0,1},{1,0},{2,3},{3,2},{4,5},{5,4},{6,7},{7,6},{8,9},{9,8},{10,11... | collective-permute-start | bytes 626696 | tf_op jit(solution)/shard_map/ppermute | solution.py:39
  13.7 1.6 %shard_map.121 = (f32[56,128]{1,0:T(8,128)S(1)}, f32[56,128]{1,0:T(8,128)S(1)}) custom-call(s32[7]{0:T(128)S(1)} %pad_add_fusion.where, f32[96,544]{1,0:T(8,128)S(1)} %collective-permute-done.right, f32[96,544]{1,0:T(8,128)S(1)} %collective-permute-done.1.right_other, f32[9,544]{1,0:T(8,128)S(1)} %pad_maximum_fusion.source, ...), custom_call_target="tpu_custom_call" | custom-call | flops 23396352 | bytes 932096 | tf_op jit(solution)/shard_map/pallas_call | solution.py:65
  18.0 8.7 %all-to-all-start = ((f32[8,56,128]{2,1,0:T(8,128)}), f32[8,56,128]{2,1,0:T(8,128)S(1)}, u32[]{:S(2)}, u32[]{:S(2)}) async-start(f32[8,56,128]{2,1,0:T(8,128)} %broadcast_in_dim.11), calls=%async_computation | async-start | bytes 458752 | tf_op jit(solution)/shard_map/all_to_all | solution.py:55
  28.6 3.5 %shard_map.122.both = f32[112,544]{1,0:T(8,128)S(1)} custom-call(s32[7]{0:T(128)S(1)} %pad_add_fusion.where, f32[544,1088]{1,0:T(8,128)S(1)} %bitcast.56, f32[9,544]{1,0:T(8,128)S(1)} %pad_maximum_fusion.source, f32[9,544]{1,0:T(8,128)S(1)} %collective-permute-done.2.source_other, f32[96,544]{1,0:T(8,128)S(1)} %copy-done.11, f32[96,544]{1,0:T(8,128)S(1)} %copy-done.13), custom_call_target="tpu_custom_call" | custom-call | flops 132579328 | bytes 3068160 | tf_op jit(solution)/shard_map/pallas_call | solution.py:65
  33.4 3.9 %all-to-all-done.mine = f32[8,56,128]{2,1,0:T(8,128)S(1)} async-done(((f32[8,56,128]{2,1,0:T(8,128)}), f32[8,56,128]{2,1,0:T(8,128)S(1)}, u32[]{:S(2)}, u32[]{:S(2)}) %all-to-all-start) | async-done | bytes 229408 | tf_op jit(solution)/shard_map/all_to_all | solution.py:55
  37.3 1.5 %collective-permute-start.4 = (f32[8,56,128]{2,1,0:T(8,128)S(1)}, f32[8,56,128]{2,1,0:T(8,128)S(1)}, u32[]{:S(2)}, u32[]{:S(2)}) collective-permute-start(f32[8,56,128]{2,1,0:T(8,128)S(1)} %all-to-all-done.mine), channel_id=1, source_target_pairs={{0,1},{1,0},{2,3},{3,2},{4,5},{5,4},{6,7},{7,6},{8,9},{9,8},{10,11... | collective-permute-start | bytes 688136 | tf_op jit(solution)/shard_map/ppermute | solution.py:39
  40.6 3.4 %shard_map.123 = (f32[8,112,128]{2,1,0:T(8,128)}, f32[96,128]{1,0:T(8,128)}, f32[16,56,128]{2,1,0:T(8,128)}) custom-call(s32[7]{0:T(128)} %copy-done.19, f32[8,56,128]{2,1,0:T(8,128)} %copy-done.5, f32[8,56,128]{2,1,0:T(8,128)} %copy-done.14), custom_call_target="tpu_custom_call" | custom-call | flops 33030144 | bytes 1425408 | tf_op jit(solution)/shard_map/pallas_call | solution.py:65
  44.0 2.9 %collective-permute-start.6 = (f32[112,544]{1,0:T(8,128)S(1)}, f32[112,544]{1,0:T(8,128)}, u32[]{:S(2)}, u32[]{:S(2)}) collective-permute-start(f32[112,544]{1,0:T(8,128)S(1)} %shard_map.122.both), channel_id=1, source_target_pairs={{0,2},{2,4},{4,6},{6,8},{8,10},{10,12},{12,14},{14,16},{16,18},{18... | collective-permute-start | bytes 731144 | tf_op jit(solution)/shard_map/ppermute | solution.py:35
  46.9 8.0 %all-to-all-start.1 = ((f32[16,56,128]{2,1,0:T(8,128)}), f32[16,56,128]{2,1,0:T(8,128)S(1)}, u32[]{:S(2)}, u32[]{:S(2)}) async-start(f32[16,56,128]{2,1,0:T(8,128)} %get-tuple-element.43), calls=%async_computation.1 | async-start | bytes 917504 | tf_op jit(solution)/shard_map/all_to_all | solution.py:339
  56.6 1.8 %convolution_bitcast_fusion = f32[3,112,96]{2,1,0:T(8,128)S(1)} fusion(f32[112,544]{1,0:T(8,128)} %collective-permute-done.6, f32[3,1,544,96]{2,3,1,0:T(8,128)} %param.14), kind=kOutput, calls=%fused_computation.2 | convolution fusion | flops 105283584 | bytes 999424 | tf_op jit(solution)/shard_map/mh,krh->kmr/dot_general | solution.py:337
  61.1 3.6 %all-to-all-done.1.mine = f32[16,56,128]{2,1,0:T(8,128)S(1)} async-done(((f32[16,56,128]{2,1,0:T(8,128)}), f32[16,56,128]{2,1,0:T(8,128)S(1)}, u32[]{:S(2)}, u32[]{:S(2)}) %all-to-all-start.1) | async-done | bytes 458784 | tf_op jit(solution)/shard_map/all_to_all | solution.py:339
  64.7 2.0 %collective-permute-start.10 = (f32[16,56,128]{2,1,0:T(8,128)S(1)}, f32[16,56,128]{2,1,0:T(8,128)S(1)}, u32[]{:S(2)}, u32[]{:S(2)}) collective-permute-start(f32[16,56,128]{2,1,0:T(8,128)S(1)} %all-to-all-done.1.mine), channel_id=1, source_target_pairs={{0,1},{1,0},{2,3},{3,2},{4,5},{5,4},{6,7},{7,6},{8,9},{9,8},{10,11... | collective-permute-start | bytes 1376264 | tf_op jit(solution)/shard_map/ppermute | solution.py:39
  66.8 1.4 %collective-permute-done.10.other = f32[16,56,128]{2,1,0:T(8,128)S(1)} collective-permute-done((f32[16,56,128]{2,1,0:T(8,128)S(1)}, f32[16,56,128]{2,1,0:T(8,128)S(1)}, u32[]{:S(2)}, u32[]{:S(2)}) %collective-permute-start.10) | collective-permute-done | bytes 458784 | tf_op jit(solution)/shard_map/ppermute | solution.py:39
  69.0 7.8 %shard_map.124 = (f32[9,544]{1,0:T(8,128)}, f32[3,9,544]{2,1,0:T(8,128)}, f32[3,9,544]{2,1,0:T(8,128)}, f32[3,9,544]{2,1,0:T(8,128)}, f32[9,8,96]{2,1,0:T(8,128)}) custom-call(s32[7]{0:T(128)} %copy-done.19, f32[16,56,128]{2,1,0:T(8,128)} %copy-done.3, f32[16,56,128]{2,1,0:T(8,128)} %copy-done.7, f32[8,112,128]{2,1,0:T(8,128)} %get-tuple-element.47.reach, ...), custom_call_target="tpu_custom_call" | custom-call | flops 17989632 | bytes 7115008 | tf_op jit(solution)/shard_map/pallas_call | solution.py:65
  80.2 5.1 %all-to-all-start.2 = ((f32[8,48,96]{2,1,0:T(8,128)}), f32[8,48,96]{2,1,0:T(8,128)}, u32[]{:S(2)}, u32[]{:S(2)}) async-start(f32[8,48,96]{2,1,0:T(8,128)} %broadcast_in_dim.25), calls=%async_computation.2 | async-start | bytes 393216 | tf_op jit(solution)/shard_map/all_to_all | solution.py:55
  88.9 5.8 %all-to-all-done.2.offsets = f32[8,48,96]{2,1,0:T(8,128)} async-done(((f32[8,48,96]{2,1,0:T(8,128)}), f32[8,48,96]{2,1,0:T(8,128)}, u32[]{:S(2)}, u32[]{:S(2)}) %all-to-all-start.2) | async-done | bytes 147488 | tf_op jit(solution)/shard_map/all_to_all | solution.py:55
  95.6 2.7 %shard_map.125 = (f32[24,96]{1,0:T(8,128)S(1)}, f32[16,48,96]{2,1,0:T(8,128)}) custom-call(s32[7]{0:T(128)S(1)} %copy-done.20, f32[8,56,128]{2,1,0:T(8,128)S(1)} %copy-done.6, f32[8,56,128]{2,1,0:T(8,128)S(1)} %copy-done.15, f32[8,48,96]{2,1,0:T(8,128)} %all-to-all-done.2.offsets), custom_call_target="tpu_custom_call" | custom-call | flops 3538944 | bytes 910336 | tf_op jit(solution)/shard_map/pallas_call | solution.py:65
  98.3 6.5 %all-to-all-start.3 = ((f32[16,48,96]{2,1,0:T(8,128)}), f32[16,48,96]{2,1,0:T(8,128)S(1)}, u32[]{:S(2)}, u32[]{:S(2)}) async-start(f32[16,48,96]{2,1,0:T(8,128)} %get-tuple-element.53), calls=%async_computation.3 | async-start | bytes 786432 | tf_op jit(solution)/shard_map/all_to_all | solution.py:375
  106.7 6.2 %all-to-all-done.3.outs = f32[16,48,96]{2,1,0:T(8,128)S(1)} async-done(((f32[16,48,96]{2,1,0:T(8,128)}), f32[16,48,96]{2,1,0:T(8,128)S(1)}, u32[]{:S(2)}, u32[]{:S(2)}) %all-to-all-start.3) | async-done | bytes 294944 | tf_op jit(solution)/shard_map/all_to_all | solution.py:375
  113.9 3.4 %shard_map.126 = (f32[24,544]{1,0:T(8,128)}, f32[1,128]{1,0:T(1,128)S(1)}) custom-call(s32[7]{0:T(128)S(1)} %copy-done.20, f32[16,56,128]{2,1,0:T(8,128)S(1)} %copy-done.4, f32[16,56,128]{2,1,0:T(8,128)S(1)} %copy-done.8, f32[16,48,96]{2,1,0:T(8,128)S(1)} %all-to-all-done.3.outs, f32[96,128]{1,0:T(8,128)S(1)} %copy-done.18, ...), custom_call_target="tpu_custom_call" | custom-call | flops 9584640 | bytes 1604224 | tf_op jit(solution)/shard_map/pallas_call | solution.py:65
  117.4 3.4 %collective-permute-start.15 = (f32[128]{0:T(128)S(1)}, f32[128]{0:T(128)S(1)}, u32[]{:S(2)}, u32[]{:S(2)}) collective-permute-start(f32[128]{0:T(128)S(1)} %bitcast_add_fusion), channel_id=1, source_target_pairs={{0,1},{1,0},{2,3},{3,2},{4,5},{5,4},{6,7},{7,6},{8,9},{9,8},{10,11... | collective-permute-start | bytes 1544 | tf_op jit(solution)/shard_map/ppermute | solution.py:39
  121.6 16.3 %all_to_all.26 = f32[128,1,128]{2,1,0:T(1,128)S(1)} all-to-all(f32[128,1,128]{2,1,0:T(1,128)S(1)} %broadcast_in_dim.26), channel_id=1, replica_groups=mesh['row_0'=4,'row_1'=4,'row_2'=8,'col'=2] {'row_0','row_1','row_2'}, dimensions={0} | all-to-all | bytes 131072 | tf_op jit(solution)/shard_map/all_to_all | solution.py:55
  (104 shorter events, 31.1 us)
Async XLA Ops:
  0.7 8.3 %collective-permute-start = (f32[96,544]{1,0:T(8,128)}, f32[96,544]{1,0:T(8,128)S(1)}, u32[]{:S(2)}, u32[]{:S(2)}) collective-permute-start(f32[96,544]{1,0:T(8,128)} %bitcast.63), channel_id=1, source_target_pairs={{2,0},{4,2},{6,4},{8,6},{10,8},{12,10},{14,12},{16,14},{18,16},{20... | collective-permute-start | bytes 626696 | tf_op jit(solution)/shard_map/ppermute | solution.py:35
  2.8 29.3 %copy-start.19 = (s32[7]{0:T(128)}, s32[7]{0:T(128)S(1)}, u32[]{:S(2)}) copy-start(s32[7]{0:T(128)S(1)} %pad_add_fusion.where) | copy-start | bytes 88
  8.9 4.7 %collective-permute-start.1 = (f32[96,544]{1,0:T(8,128)S(1)}, f32[96,544]{1,0:T(8,128)S(1)}, u32[]{:S(2)}, u32[]{:S(2)}) collective-permute-start(f32[96,544]{1,0:T(8,128)S(1)} %collective-permute-done.right), channel_id=1, source_target_pairs={{0,1},{1,0},{2,3},{3,2},{4,5},{5,4},{6,7},{7,6},{8,9},{9,8},{10,11... | collective-permute-start | bytes 626696 | tf_op jit(solution)/shard_map/ppermute | solution.py:39
  12.4 1.3 collective-permute-start.2
  16.0 1.2 collective-permute-start.3
  18.0 19.4 %all-to-all-start = ((f32[8,56,128]{2,1,0:T(8,128)}), f32[8,56,128]{2,1,0:T(8,128)S(1)}, u32[]{:S(2)}, u32[]{:S(2)}) async-start(f32[8,56,128]{2,1,0:T(8,128)} %broadcast_in_dim.11), calls=%async_computation | async-start | bytes 458752 | tf_op jit(solution)/shard_map/all_to_all | solution.py:55
  32.1 28.3 %copy-start.2 = (f32[112,544]{1,0:T(8,128)}, f32[112,544]{1,0:T(8,128)S(1)}, u32[]{:S(2)}) copy-start(f32[112,544]{1,0:T(8,128)S(1)} %shard_map.122.both) | copy-start | bytes 731140
  37.3 2.6 %collective-permute-start.4 = (f32[8,56,128]{2,1,0:T(8,128)S(1)}, f32[8,56,128]{2,1,0:T(8,128)S(1)}, u32[]{:S(2)}, u32[]{:S(2)}) collective-permute-start(f32[8,56,128]{2,1,0:T(8,128)S(1)} %all-to-all-done.mine), channel_id=1, source_target_pairs={{0,1},{1,0},{2,3},{3,2},{4,5},{5,4},{6,7},{7,6},{8,9},{9,8},{10,11... | collective-permute-start | bytes 688136 | tf_op jit(solution)/shard_map/ppermute | solution.py:39
  44.0 12.5 %collective-permute-start.6 = (f32[112,544]{1,0:T(8,128)S(1)}, f32[112,544]{1,0:T(8,128)}, u32[]{:S(2)}, u32[]{:S(2)}) collective-permute-start(f32[112,544]{1,0:T(8,128)S(1)} %shard_map.122.both), channel_id=1, source_target_pairs={{0,2},{2,4},{4,6},{6,8},{8,10},{10,12},{12,14},{14,16},{16,18},{18... | collective-permute-start | bytes 731144 | tf_op jit(solution)/shard_map/ppermute | solution.py:35
  46.9 17.8 %all-to-all-start.1 = ((f32[16,56,128]{2,1,0:T(8,128)}), f32[16,56,128]{2,1,0:T(8,128)S(1)}, u32[]{:S(2)}, u32[]{:S(2)}) async-start(f32[16,56,128]{2,1,0:T(8,128)} %get-tuple-element.43), calls=%async_computation.1 | async-start | bytes 917504 | tf_op jit(solution)/shard_map/all_to_all | solution.py:339
  54.9 3.8 %collective-permute-start.8 = (f32[96,544]{1,0:T(8,128)}, f32[96,544]{1,0:T(8,128)S(1)}, u32[]{:S(2)}, u32[]{:S(2)}) collective-permute-start(f32[96,544]{1,0:T(8,128)} %copy-done.17), channel_id=1, source_target_pairs={{0,1},{1,0},{2,3},{3,2},{4,5},{5,4},{6,7},{7,6},{8,9},{9,8},{10,11... | collective-permute-start | bytes 626696 | tf_op jit(solution)/shard_map/ppermute | solution.py:39
  56.0 3.7 %collective-permute-start.5 = (f32[3,112,96]{2,1,0:T(8,128)}, f32[3,112,96]{2,1,0:T(8,128)S(1)}, u32[]{:S(2)}, u32[]{:S(2)}) collective-permute-start(f32[3,112,96]{2,1,0:T(8,128)} %convolution_bitcast_fusion.1), channel_id=1, source_target_pairs={{0,1},{1,0},{2,3},{3,2},{4,5},{5,4},{6,7},{7,6},{8,9},{9,8},{10,11... | collective-permute-start | bytes 387080 | tf_op jit(solution)/shard_map/ppermute | solution.py:39
  56.1 5.0 %collective-permute-start.9 = (f32[96,544]{1,0:T(8,128)S(1)}, f32[96,544]{1,0:T(8,128)}, u32[]{:S(2)}, u32[]{:S(2)}) collective-permute-start(f32[96,544]{1,0:T(8,128)S(1)} %slice.33), channel_id=1, source_target_pairs={{0,1},{1,0},{2,3},{3,2},{4,5},{5,4},{6,7},{7,6},{8,9},{9,8},{10,11... | collective-permute-start | bytes 626696 | tf_op jit(solution)/shard_map/ppermute | solution.py:39
  58.3 2.1 %collective-permute-start.7 = (f32[3,112,96]{2,1,0:T(8,128)S(1)}, f32[3,112,96]{2,1,0:T(8,128)S(1)}, u32[]{:S(2)}, u32[]{:S(2)}) collective-permute-start(f32[3,112,96]{2,1,0:T(8,128)S(1)} %convolution_bitcast_fusion), channel_id=1, source_target_pairs={{0,1},{1,0},{2,3},{3,2},{4,5},{5,4},{6,7},{7,6},{8,9},{9,8},{10,11... | collective-permute-start | bytes 387080 | tf_op jit(solution)/shard_map/ppermute | solution.py:39
  64.7 3.5 %collective-permute-start.10 = (f32[16,56,128]{2,1,0:T(8,128)S(1)}, f32[16,56,128]{2,1,0:T(8,128)S(1)}, u32[]{:S(2)}, u32[]{:S(2)}) collective-permute-start(f32[16,56,128]{2,1,0:T(8,128)S(1)} %all-to-all-done.1.mine), channel_id=1, source_target_pairs={{0,1},{1,0},{2,3},{3,2},{4,5},{5,4},{6,7},{7,6},{8,9},{9,8},{10,11... | collective-permute-start | bytes 1376264 | tf_op jit(solution)/shard_map/ppermute | solution.py:39
  76.8 1.9 %collective-permute-start.11 = (f32[9,8,96]{2,1,0:T(8,128)}, f32[9,8,96]{2,1,0:T(8,128)S(1)}, u32[]{:S(2)}, u32[]{:S(2)}) collective-permute-start(f32[9,8,96]{2,1,0:T(8,128)} %get-tuple-element.52), channel_id=1, source_target_pairs={{0,1},{1,0},{2,3},{3,2},{4,5},{5,4},{6,7},{7,6},{8,9},{9,8},{10,11... | collective-permute-start | bytes 82952 | tf_op jit(solution)/shard_map/ppermute | solution.py:39
  77.3 8.0 %collective-permute-start.12 = (f32[3,9,544]{2,1,0:T(8,128)}, f32[3,9,544]{2,1,0:T(8,128)}, u32[]{:S(2)}, u32[]{:S(2)}) collective-permute-start(f32[3,9,544]{2,1,0:T(8,128)} %get-tuple-element.57), channel_id=1, source_target_pairs={{0,1},{1,0},{2,3},{3,2},{4,5},{5,4},{6,7},{7,6},{8,9},{9,8},{10,11... | collective-permute-start | bytes 176264 | tf_op jit(solution)/shard_map/ppermute | solution.py:39
  77.4 7.9 %collective-permute-start.13 = (f32[3,9,544]{2,1,0:T(8,128)}, f32[3,9,544]{2,1,0:T(8,128)}, u32[]{:S(2)}, u32[]{:S(2)}) collective-permute-start(f32[3,9,544]{2,1,0:T(8,128)} %get-tuple-element.58), channel_id=1, source_target_pairs={{2,0},{4,2},{6,4},{8,6},{10,8},{12,10},{14,12},{16,14},{18,16},{20... | collective-permute-start | bytes 176264 | tf_op jit(solution)/shard_map/ppermute | solution.py:35
  80.2 14.5 %all-to-all-start.2 = ((f32[8,48,96]{2,1,0:T(8,128)}), f32[8,48,96]{2,1,0:T(8,128)}, u32[]{:S(2)}, u32[]{:S(2)}) async-start(f32[8,48,96]{2,1,0:T(8,128)} %broadcast_in_dim.25), calls=%async_computation.2 | async-start | bytes 393216 | tf_op jit(solution)/shard_map/all_to_all | solution.py:55
  85.3 27.6 %copy-start.4 = (f32[16,56,128]{2,1,0:T(8,128)S(1)}, f32[16,56,128]{2,1,0:T(8,128)}, u32[]{:S(2)}) copy-start(f32[16,56,128]{2,1,0:T(8,128)} %copy-done.3) | copy-start | bytes 1376260
  85.3 27.6 %copy-start.18 = (f32[96,128]{1,0:T(8,128)S(1)}, f32[96,128]{1,0:T(8,128)}, u32[]{:S(2)}) copy-start(f32[96,128]{1,0:T(8,128)} %get-tuple-element.54.prefix) | copy-start | bytes 147460
  88.0 17.8 %collective-permute-start.14 = (f32[24,544]{1,0:T(8,128)S(1)}, f32[24,544]{1,0:T(8,128)S(1)}, u32[]{:S(2)}, u32[]{:S(2)}) collective-permute-start(f32[24,544]{1,0:T(8,128)S(1)} %constant_dynamic-slice_fusion), channel_id=1, source_target_pairs={{0,1},{1,0},{2,3},{3,2},{4,5},{5,4},{6,7},{7,6},{8,9},{9,8},{10,11... | collective-permute-start | bytes 156680 | tf_op jit(solution)/shard_map/ppermute | solution.py:39
  98.3 14.6 %all-to-all-start.3 = ((f32[16,48,96]{2,1,0:T(8,128)}), f32[16,48,96]{2,1,0:T(8,128)S(1)}, u32[]{:S(2)}, u32[]{:S(2)}) async-start(f32[16,48,96]{2,1,0:T(8,128)} %get-tuple-element.53), calls=%async_computation.3 | async-start | bytes 786432 | tf_op jit(solution)/shard_map/all_to_all | solution.py:375
  117.4 4.2 %collective-permute-start.15 = (f32[128]{0:T(128)S(1)}, f32[128]{0:T(128)S(1)}, u32[]{:S(2)}, u32[]{:S(2)}) collective-permute-start(f32[128]{0:T(128)S(1)} %bitcast_add_fusion), channel_id=1, source_target_pairs={{0,1},{1,0},{2,3},{3,2},{4,5},{5,4},{6,7},{7,6},{8,9},{9,8},{10,11... | collective-permute-start | bytes 1544 | tf_op jit(solution)/shard_map/ppermute | solution.py:39
  (22 other events, 122.9 us)
